TPU v7x, 32 devices: a whole 2x2x4 slice. The times are simulated.
32 devices in a mesh: fsdp: 16 (over z, y, core), tp: 2 (over x).
Axes of the slice: x: 2, y: 2, z: 4, core: 2. Of those that a mesh axis runs over, the one named last changes fastest.
Arguments:
- latents_in: bfloat16 [1024, 16, 1024], P('tp', 'fsdp'), may hold values from -6 to 6
- condition: bfloat16 [16, 1024], P('fsdp'), may hold values from -6 to 6
- grad_out: bfloat16 [1024, 16, 1024], P('tp', 'fsdp'), may hold values from -6 to 6
- qkv_weight: bfloat16 [1024, 3, 1024], P('fsdp', None, 'tp'), may hold values from -0.1875 to 0.1875
- proj_weight: bfloat16 [1024, 1024], P('tp', 'fsdp'), may hold values from -3 to 3
- up_weight: bfloat16 [1024, 4096], P('fsdp', 'tp'), may hold values from -0.1875 to 0.1875
- down_weight: bfloat16 [4096, 1024], P('tp', 'fsdp'), may hold values from -0.09375 to 0.09375
- ada_weight: bfloat16 [1024, 6, 1024], P('fsdp', None, 'tp'), may hold values from -0.1875 to 0.1875
- query_bias: bfloat16 [1024], P(('fsdp', 'tp')), may hold values from -1.75 to 1.75
- value_bias: bfloat16 [1024], P(('fsdp', 'tp')), may hold values from -1.75 to 1.75
- proj_bias: bfloat16 [1024], P(('fsdp', 'tp')), may hold values from -1.75 to 1.75
- up_bias: bfloat16 [4096], P(('fsdp', 'tp')), may hold values from -1.75 to 1.75
- down_bias: bfloat16 [1024], P(('fsdp', 'tp')), may hold values from -1.75 to 1.75
- ada_bias: bfloat16 [6, 1024], P(None, ('fsdp', 'tp')), may hold values from -1.75 to 1.75
Outputs:
- block_out: bfloat16 [1024, 16, 1024], P('tp', 'fsdp')
- input_grad: float32 [1024, 16, 1024], P('tp', 'fsdp')
- cond_grad: float32 [16, 1024], P('fsdp', 'tp')
- qkv_weight_grad: float32 [1024, 3, 1024], P('fsdp', None, 'tp')
- proj_weight_grad: float32 [1024, 1024], P('tp', 'fsdp')
- up_weight_grad: float32 [1024, 4096], P('fsdp', 'tp')
- down_weight_grad: float32 [4096, 1024], P('tp', 'fsdp')
- ada_weight_grad: float32 [1024, 6, 1024], P('fsdp', None, 'tp')
- query_bias_grad: float32 [1024], P(('fsdp', 'tp'))
- value_bias_grad: float32 [1024], P(('fsdp', 'tp'))
- proj_bias_grad: float32 [1024], P(('fsdp', 'tp'))
- up_bias_grad: float32 [4096], P(('fsdp', 'tp'))
- down_bias_grad: float32 [1024], P(('fsdp', 'tp'))
- ada_bias_grad: float32 [6, 1024], P(None, ('fsdp', 'tp'))
All inputs are finite; a program needn't handle non-finite values.
Results may differ from a plain program's by a relative error of at most 0.019.
Values may be sent and summed in bfloat16 or wider, within the bound.
A program may use at most 192 MiB of HBM per device.

v0:
```python
import math

import jax
import jax.numpy as jnp
from jax import lax
from jax.sharding import PartitionSpec as P

HD = 64


epsilon = 1e-06


def layer_norm(values):
    centred = values - jnp.mean(values, axis=-1, keepdims=True)
    return centred * lax.rsqrt(jnp.mean(centred * centred, axis=-1, keepdims=True) + epsilon)


def modulate(values, shift_part, scale_part):
    return layer_norm(values) * (1.0 + scale_part) + shift_part


def gelu_tanh(values):
    return jax.nn.gelu(values, approximate=True)


def gather_rows(piece):
    return lax.all_gather(piece, "tp", axis=0, tiled=True)


def gather_grads(piece):
    return lax.all_gather(piece, "tp", axis=0, tiled=True)


def scatter_rows(product, row_count):
    return lax.psum_scatter(
        product(jnp.int32(0), row_count * lax.axis_size("tp")).astype(jnp.bfloat16),
        "tp",
        scatter_dimension=0,
        tiled=True,
    ).astype(jnp.float32)


def scatter_grads(product, row_count):
    return lax.psum_scatter(
        product(jnp.int32(0), row_count * lax.axis_size("tp")).astype(jnp.bfloat16),
        "tp",
        scatter_dimension=0,
        tiled=True,
    ).astype(jnp.float32)


def split_heads(packed):
    head_count = packed.shape[3] // HD
    shaped = packed.reshape(packed.shape[0], packed.shape[1], 3, head_count, HD)
    return (shaped[:, :, 0], shaped[:, :, 1], shaped[:, :, 2])


def attend_forward(packed):
    length, latents, local_width = (packed.shape[0], packed.shape[1], packed.shape[3])
    queries, key_rows, value_rows = split_heads(packed)
    block_rows = min(512, length)
    score_scale = 1.0 / math.sqrt(HD)
    blocks = queries.reshape(length // block_rows, block_rows, latents, local_width // HD, HD)

    def one_block(q_rows):
        scores = (
            jnp.einsum("qbhd,kbhd->bhqk", q_rows, key_rows, preferred_element_type=jnp.float32)
            * score_scale
        )
        largest = jnp.max(scores, axis=-1, keepdims=True)
        exponent = jnp.exp(scores - largest)
        summed = jnp.sum(exponent, axis=-1, keepdims=True)
        weights_soft = (exponent / summed).astype(jnp.bfloat16)
        mixture = jnp.einsum(
            "bhqk,kbhd->qbhd", weights_soft, value_rows, preferred_element_type=jnp.float32
        )
        return (mixture.astype(jnp.bfloat16), largest[..., 0] + jnp.log(summed[..., 0]))

    mixture_all, log_sums = lax.map(one_block, blocks)
    return (mixture_all.reshape(length, latents, local_width), log_sums)


def attend_backward(packed, log_sums, heads_grad):
    length, latents, local_width = (packed.shape[0], packed.shape[1], packed.shape[3])
    head_count = local_width // HD
    queries, key_rows, value_rows = split_heads(packed)
    block_rows = min(512, length)
    count_blocks = length // block_rows
    score_scale = 1.0 / math.sqrt(HD)
    q_blocks = queries.reshape(count_blocks, block_rows, latents, head_count, HD)
    g_blocks = heads_grad.reshape(count_blocks, block_rows, latents, head_count, HD)

    def one_block(carried, inputs):
        key_grad, value_grad = carried
        q_rows, g_rows, log_rows = inputs
        scores = (
            jnp.einsum("qbhd,kbhd->bhqk", q_rows, key_rows, preferred_element_type=jnp.float32)
            * score_scale
        )
        weights_soft = jnp.exp(scores - log_rows[..., None])
        soft_grad = jnp.einsum(
            "qbhd,kbhd->bhqk", g_rows, value_rows, preferred_element_type=jnp.float32
        )
        inner_sum = jnp.sum(weights_soft * soft_grad, axis=-1, keepdims=True)
        score_grad = (weights_soft * (soft_grad - inner_sum)).astype(jnp.bfloat16)
        query_grad = (
            jnp.einsum("bhqk,kbhd->qbhd", score_grad, key_rows, preferred_element_type=jnp.float32)
            * score_scale
        )
        key_grad = (
            key_grad
            + jnp.einsum("bhqk,qbhd->kbhd", score_grad, q_rows, preferred_element_type=jnp.float32)
            * score_scale
        )
        value_grad = value_grad + jnp.einsum(
            "bhqk,qbhd->kbhd",
            weights_soft.astype(jnp.bfloat16),
            g_rows,
            preferred_element_type=jnp.float32,
        )
        return ((key_grad, value_grad), query_grad)

    zero_rows = jnp.zeros((length, latents, head_count, HD), jnp.float32)
    (key_grad, value_grad), query_grad = lax.scan(
        one_block, (zero_rows, zero_rows), (q_blocks, g_blocks, log_sums)
    )
    stacked = jnp.stack(
        [
            query_grad.reshape(length, latents, local_width),
            key_grad.reshape(length, latents, local_width),
            value_grad.reshape(length, latents, local_width),
        ],
        axis=2,
    )
    return stacked.astype(jnp.bfloat16)


def on_device(
    latents_in,
    condition,
    grad_out,
    qkv_weight,
    proj_weight,
    up_weight,
    down_weight,
    ada_weight,
    query_bias,
    value_bias,
    proj_bias,
    up_bias,
    down_bias,
    ada_bias,
):
    tp_index = lax.axis_index("tp")
    local_rows = latents_in.shape[0]
    local_width = qkv_weight.shape[2]
    local_hidden = up_weight.shape[1]
    model_width = latents_in.shape[2]
    width_start = tp_index * local_width
    hidden_start = tp_index * local_hidden
    full_qkv, full_proj, full_up, full_down, full_ada = (
        lax.all_gather(qkv_weight, "fsdp", axis=0, tiled=True),
        lax.all_gather(proj_weight, "fsdp", axis=1, tiled=True),
        lax.all_gather(up_weight, "fsdp", axis=0, tiled=True),
        lax.all_gather(down_weight, "fsdp", axis=1, tiled=True),
        lax.all_gather(ada_weight, "fsdp", axis=0, tiled=True),
    )
    bias_list = (
        lax.all_gather(query_bias, ("fsdp", "tp"), axis=0, tiled=True),
        lax.all_gather(value_bias, ("fsdp", "tp"), axis=0, tiled=True),
        lax.all_gather(proj_bias, ("fsdp", "tp"), axis=0, tiled=True),
        lax.all_gather(up_bias, ("fsdp", "tp"), axis=0, tiled=True),
        lax.all_gather(down_bias, ("fsdp", "tp"), axis=0, tiled=True),
        lax.all_gather(ada_bias, ("fsdp", "tp"), axis=1, tiled=True),
    )
    all_query, all_value, all_proj, all_up, all_down, all_ada = [
        item_bias.astype(jnp.float32) for item_bias in bias_list
    ]
    hidden_total = all_up.shape[0]
    cond_float = condition.astype(jnp.float32)
    silu_cond = jax.nn.silu(cond_float).astype(jnp.bfloat16)
    ada_cols = lax.dynamic_slice_in_dim(all_ada, width_start, local_width, 1)
    mod_part = (
        jnp.einsum("bc,ctf->btf", silu_cond, full_ada, preferred_element_type=jnp.float32)
        + ada_cols
    )
    modulation = lax.all_gather(mod_part, "tp", axis=2, tiled=True)
    shift_one, scale_one, gate_one = (modulation[:, 0], modulation[:, 1], modulation[:, 2])
    shift_two, scale_two, gate_two = (modulation[:, 3], modulation[:, 4], modulation[:, 5])
    input_float = latents_in.astype(jnp.float32)
    attn_in = modulate(input_float, shift_one, scale_one).astype(jnp.bfloat16)
    attn_full = gather_rows(attn_in)
    query_cols = lax.dynamic_slice_in_dim(all_query, width_start, local_width, 0)
    value_cols = lax.dynamic_slice_in_dim(all_value, width_start, local_width, 0)
    bias_three = jnp.stack([query_cols, jnp.zeros_like(query_cols), value_cols])
    packed = (
        jnp.einsum("sbd,dtf->sbtf", attn_full, full_qkv, preferred_element_type=jnp.float32)
        + bias_three
    ).astype(jnp.bfloat16)
    heads_out, log_sums = attend_forward(packed)

    def project_heads(first_row, row_count):
        return jnp.einsum("sbf,fd->sbd", heads_out, full_proj, preferred_element_type=jnp.float32)

    branch_one = scatter_rows(project_heads, local_rows) + all_proj
    middle = input_float + gate_one * branch_one
    mlp_in = modulate(middle, shift_two, scale_two).astype(jnp.bfloat16)
    mlp_full = gather_rows(mlp_in)
    up_cols = lax.dynamic_slice_in_dim(all_up, hidden_start, local_hidden, 0)
    hidden = (
        jnp.einsum("sbd,df->sbf", mlp_full, full_up, preferred_element_type=jnp.float32) + up_cols
    )
    active = gelu_tanh(hidden).astype(jnp.bfloat16)

    def project_hidden(first_row, row_count):
        return jnp.einsum("sbf,fd->sbd", active, full_down, preferred_element_type=jnp.float32)

    branch_two = scatter_rows(project_hidden, local_rows) + all_down
    block_out = (middle + gate_two * branch_two).astype(jnp.bfloat16)
    grad_float = grad_out.astype(jnp.float32)
    gate_two_grad = jnp.sum(grad_float * branch_two, axis=0)
    branch_two_grad = (grad_float * gate_two).astype(jnp.bfloat16)
    down_bias_part = jnp.sum(branch_two_grad.astype(jnp.float32), axis=(0, 1))
    _, gelu_pull = jax.vjp(gelu_tanh, hidden)
    branch_two_full = gather_grads(branch_two_grad)
    active_grad = jnp.einsum(
        "sbd,fd->sbf", branch_two_full, full_down, preferred_element_type=jnp.float32
    )
    down_grad = jnp.einsum(
        "sbf,sbd->fd", active, branch_two_full, preferred_element_type=jnp.float32
    )
    hidden_grad = gelu_pull(active_grad)[0].astype(jnp.bfloat16)
    up_grad = jnp.einsum("sbd,sbf->df", mlp_full, hidden_grad, preferred_element_type=jnp.float32)
    up_bias_part = lax.dynamic_update_slice(
        jnp.zeros((hidden_total,), jnp.float32),
        jnp.sum(hidden_grad.astype(jnp.float32), axis=(0, 1)),
        (hidden_start,),
    )

    def back_hidden(first_row, row_count):
        return jnp.einsum("sbf,df->sbd", hidden_grad, full_up, preferred_element_type=jnp.float32)

    mlp_in_grad = scatter_grads(back_hidden, local_rows)
    _, second_pull = jax.vjp(modulate, middle, shift_two, scale_two)
    middle_part, shift_two_grad, scale_two_grad = second_pull(mlp_in_grad)
    middle_grad = grad_float + middle_part
    gate_one_grad = jnp.sum(middle_grad * branch_one, axis=0)
    branch_one_grad = (middle_grad * gate_one).astype(jnp.bfloat16)
    proj_bias_part = jnp.sum(branch_one_grad.astype(jnp.float32), axis=(0, 1))
    branch_one_full = gather_grads(branch_one_grad)
    heads_grad = jnp.einsum(
        "sbd,fd->sbf", branch_one_full, full_proj, preferred_element_type=jnp.float32
    ).astype(jnp.bfloat16)
    proj_grad = jnp.einsum(
        "sbf,sbd->fd", heads_out, branch_one_full, preferred_element_type=jnp.float32
    )
    packed_grad = attend_backward(packed, log_sums, heads_grad)
    qkv_grad = jnp.einsum(
        "sbd,sbtf->dtf", attn_full, packed_grad, preferred_element_type=jnp.float32
    )
    packed_sums = jnp.sum(packed_grad.astype(jnp.float32), axis=(0, 1))
    zero_width = jnp.zeros((model_width,), jnp.float32)
    query_bias_part = lax.dynamic_update_slice(zero_width, packed_sums[0], (width_start,))
    value_bias_part = lax.dynamic_update_slice(zero_width, packed_sums[2], (width_start,))

    def back_packed(first_row, row_count):
        return jnp.einsum(
            "sbtf,dtf->sbd", packed_grad, full_qkv, preferred_element_type=jnp.float32
        )

    attn_in_grad = scatter_grads(back_packed, local_rows)
    _, first_pull = jax.vjp(modulate, input_float, shift_one, scale_one)
    input_part, shift_one_grad, scale_one_grad = first_pull(attn_in_grad)
    input_grad = middle_grad + input_part
    mod_grad = jnp.stack(
        [
            shift_one_grad,
            scale_one_grad,
            gate_one_grad,
            shift_two_grad,
            scale_two_grad,
            gate_two_grad,
        ],
        axis=1,
    )
    mod_cols_grad = lax.psum_scatter(
        mod_grad.astype(jnp.bfloat16), "tp", scatter_dimension=2, tiled=True
    ).astype(jnp.float32)
    ada_grad = jnp.einsum(
        "bc,btf->ctf", silu_cond.astype(jnp.float32), mod_cols_grad, precision=lax.Precision.HIGHEST
    )
    ada_bias_part = lax.dynamic_update_slice(
        jnp.zeros((6, model_width), jnp.float32), jnp.sum(mod_cols_grad, axis=0), (0, width_start)
    )
    silu_grad = jnp.einsum(
        "btf,ctf->bc", mod_cols_grad, full_ada.astype(jnp.float32), precision=lax.Precision.HIGHEST
    )
    silu_cols = lax.psum_scatter(silu_grad, "tp", scatter_dimension=1, tiled=True)
    cond_width = silu_cols.shape[1]
    cond_cols = lax.dynamic_slice_in_dim(cond_float, tp_index * cond_width, cond_width, 1)
    _, silu_pull = jax.vjp(jax.nn.silu, cond_cols)
    cond_grad = silu_pull(silu_cols)[0]
    qkv_sum, proj_sum, up_sum, down_sum, ada_sum = (
        lax.psum_scatter(
            qkv_grad.astype(jnp.bfloat16), "fsdp", scatter_dimension=0, tiled=True
        ).astype(jnp.float32),
        lax.psum_scatter(
            proj_grad.astype(jnp.bfloat16), "fsdp", scatter_dimension=1, tiled=True
        ).astype(jnp.float32),
        lax.psum_scatter(
            up_grad.astype(jnp.bfloat16), "fsdp", scatter_dimension=0, tiled=True
        ).astype(jnp.float32),
        lax.psum_scatter(
            down_grad.astype(jnp.bfloat16), "fsdp", scatter_dimension=1, tiled=True
        ).astype(jnp.float32),
        lax.psum_scatter(
            ada_grad.astype(jnp.bfloat16), "fsdp", scatter_dimension=0, tiled=True
        ).astype(jnp.float32),
    )
    query_sum, value_sum, proj_bias_sum, up_bias_sum, down_bias_sum, ada_bias_sum = (
        lax.psum_scatter(query_bias_part, ("fsdp", "tp"), scatter_dimension=0, tiled=True),
        lax.psum_scatter(value_bias_part, ("fsdp", "tp"), scatter_dimension=0, tiled=True),
        lax.psum_scatter(proj_bias_part, ("fsdp", "tp"), scatter_dimension=0, tiled=True),
        lax.psum_scatter(up_bias_part, ("fsdp", "tp"), scatter_dimension=0, tiled=True),
        lax.psum_scatter(down_bias_part, ("fsdp", "tp"), scatter_dimension=0, tiled=True),
        lax.psum_scatter(ada_bias_part, ("fsdp", "tp"), scatter_dimension=1, tiled=True),
    )
    return (
        block_out,
        input_grad,
        cond_grad,
        qkv_sum,
        proj_sum,
        up_sum,
        down_sum,
        ada_sum,
        query_sum,
        value_sum,
        proj_bias_sum,
        up_bias_sum,
        down_bias_sum,
        ada_bias_sum,
    )


def solution(mesh):
    return jax.shard_map(
        on_device,
        mesh=mesh,
        in_specs=(
            P("tp", "fsdp", None),
            P("fsdp", None),
            P("tp", "fsdp", None),
            P("fsdp", None, "tp"),
            P("tp", "fsdp"),
            P("fsdp", "tp"),
            P("tp", "fsdp"),
            P("fsdp", None, "tp"),
            P(("fsdp", "tp")),
            P(("fsdp", "tp")),
            P(("fsdp", "tp")),
            P(("fsdp", "tp")),
            P(("fsdp", "tp")),
            P(None, ("fsdp", "tp")),
        ),
        out_specs=(
            P("tp", "fsdp", None),
            P("tp", "fsdp", None),
            P("fsdp", "tp"),
            P("fsdp", None, "tp"),
            P("tp", "fsdp"),
            P("fsdp", "tp"),
            P("tp", "fsdp"),
            P("fsdp", None, "tp"),
            P(("fsdp", "tp")),
            P(("fsdp", "tp")),
            P(("fsdp", "tp")),
            P(("fsdp", "tp")),
            P(("fsdp", "tp")),
            P(None, ("fsdp", "tp")),
        ),
        check_vma=False,
    )
```

profile of v0, /device:TPU:0, one launch (start us, length us, event | category | flops | bytes accessed | tf_op | source)
XLA Modules:
  0.0 1221.3 jit_solution(16518706140946443054)
XLA Ops:
  8.7 71.3 %all-gather.1 = bf16[32,32,6]{1,2,0:T(8,128)(2,1)S(1)} all-gather(bf16[1,32,6]{1,2,0:T(8,128)(2,1)} %bitcast.263), channel_id=1, replica_groups=mesh['fsdp'=16,'tp'=2] {'fsdp','tp'}, dimensions={0}, use_global_device_ids=true | all-gather | bytes 12672 | tf_op jit(solution)/shard_map/all_gather | solution.py:175
  87.8 4.5 all-gather
  96.6 38.1 %all-reduce.10 = (bf16[1024]{0:T(1024)(128)(2,1)S(1)}, bf16[1024]{0:T(1024)(128)(2,1)S(1)}, bf16[1024]{0:T(1024)(128)(2,1)}, bf16[1024]{0:T(1024)(128)(2,1)}) all-reduce(bf16[1024]{0:T(1024)(128)(2,1)S(1)} %dynamic-update-slice, bf16[1024]{0:T(1024)(128)(2,1)S(1)} %dynamic-update-slice.1, ...), channel_id=1, replica_groups=mesh['fsdp'=16,'tp'=2] {'fsdp','tp'}, use_global_device_ids=true, to_apply=%add | all-reduce | flops 4096 | bytes 16384
  135.1 21.1 %all-gather.15.cloned.1.call-done = bf16[1024,1,1024]{2,0,1:T(8,128)(2,1)} async-done(((bf16[512,1,1024]{2,0,1:T(8,128)(2,1)}), bf16[1024,1,1024]{2,0,1:T(8,128)(2,1)}) %all-gather.15.cloned.1.call-update) | async-done | bytes 2097168 | tf_op jit(solution)/shard_map/all_gather | solution.py:28
  156.1 6.0 add_convert_fusion
  166.4 22.7 %while.27 = (s32[]{:T(128)}, bf16[2,512,1,8,64]{1,4,3,2,0:T(8,128)(2,1)}, f32[2,1,8,512]{3,2,1,0:T(8,128)S(1)}, bf16[2,512,1,8,64]{1,4,3,2,0:T(8,128)(2,1)S(1)},...) while((s32[]{:T(128)}, bf16[2,512,1,8,64]{1,4,3,2,0:T(8,128)(2,1)}, ...), condition=%wide.region_5.6_spmd, body=%wide.region_2.5_spmd.sunk | while | flops 1111748608 | bytes 66191540 | solution.py:80
  172.4 4.3 fusion.132
  183.7 4.3 fusion.132
  196.1 4.3 convert_bitcast_fusion.2
  201.0 30.3 %reduce-scatter.17.cloned.1.call-done = bf16[512,1,1024]{2,0,1:T(8,128)(2,1)} async-done(((bf16[1024,1,1024]{2,0,1:T(8,128)(2,1)}), bf16[512,1,1024]{2,0,1:T(8,128)(2,1)}) %reduce-scatter.17.cloned.1.call-update) | async-done | bytes 1048592 | tf_op jit(solution)/shard_map/reduce_scatter | solution.py:36
  240.7 66.7 %all-gather.2 = bf16[32,1,128]{2,1,0:T(2,128)(2,1)S(1)} all-gather(bf16[1,1,128]{2,1,0:T(2,128)(2,1)S(1)} %bitcast.264), channel_id=1, replica_groups=mesh['fsdp'=16,'tp'=2] {'fsdp','tp'}, dimensions={0}, use_global_device_ids=true | all-gather | bytes 8448 | tf_op jit(solution)/shard_map/all_gather | solution.py:173
  307.5 10.7 all-gather.21.cloned.1.call-done
  318.2 10.6 fusion.73
  328.8 42.5 %all-gather.25.cloned.1.call-done = bf16[2048,1024]{0,1:T(8,128)(2,1)} async-done(((bf16[2048,64]{0,1:T(8,128)(2,1)}), bf16[2048,1024]{0,1:T(8,128)(2,1)}) %all-gather.25.cloned.1.call-update) | async-done | bytes 4194320 | tf_op jit(solution)/shard_map/all_gather | solution.py:166
  371.4 33.8 %all-gather.27.cloned.1.call-done = bf16[1024,1,1024]{2,0,1:T(8,128)(2,1)} async-done(((bf16[512,1,1024]{2,0,1:T(8,128)(2,1)}), bf16[1024,1,1024]{2,0,1:T(8,128)(2,1)}) %all-gather.27.cloned.1.call-update) | async-done | bytes 2097168 | tf_op jit(solution)/shard_map/all_gather | solution.py:32
  405.2 13.9 %convert_reduce_fusion = (f32[2048]{0:T(1024)}, bf16[1024,2048]{1,0:T(8,128)(2,1)S(1)}) fusion(f32[1024,2048]{1,0:T(8,128)} %fusion.73, f32[2048]{0:T(1024)S(1)} %dynamic_slice.32, bf16[2048,1024]{0,1:T(8,128)(2,1)} %all-gather.25.cloned.1.call-done, bf16[1024,1,1024]{2,0,1:T(8,128)(2,1)} %all-gather.27.cloned.1.call-done), kind=kOutput, calls=%fused_computation.57 | convolution fusion | flops 4343199744 | bytes 18890752 | tf_op jit(solution)/shard_map/sbd,fd->sbf/dot_general | solution.py:227
  421.1 5.7 convert_bitcast_fusion
  426.9 31.9 %reduce-scatter.21.cloned.1.call-done = bf16[512,1,1024]{2,0,1:T(8,128)(2,1)} async-done(((bf16[1024,1,1024]{2,0,1:T(8,128)(2,1)}), bf16[512,1,1024]{2,0,1:T(8,128)(2,1)}) %reduce-scatter.21.cloned.1.call-update) | async-done | bytes 1048592 | tf_op jit(solution)/shard_map/reduce_scatter | solution.py:45
  468.1 33.2 %all-gather.29.cloned.1.call-done = bf16[1024,1,1024]{2,0,1:T(8,128)(2,1)} async-done(((bf16[512,1,1024]{2,0,1:T(8,128)(2,1)}), bf16[1024,1,1024]{2,0,1:T(8,128)(2,1)}) %all-gather.29.cloned.1.call-update) | async-done | bytes 2097168 | tf_op jit(solution)/shard_map/all_gather | solution.py:32
  505.2 4.3 reshape.605
  512.8 76.6 %while.28 = (s32[]{:T(128)}, f32[1024,1,8,64]{0,3,2,1:T(8,128)}, f32[1024,1,8,64]{0,3,2,1:T(8,128)}, bf16[2,512,1,8,64]{1,4,3,2,0:T(8,128)(2,1)}, bf16[2,512,1,8...) while((s32[]{:T(128)}, f32[1024,1,8,64]{0,3,2,1:T(8,128)}, ...), condition=%wide.region_15.16_spmd.clone, body=%wide.region_13.15_spmd.clone.sunk | while | flops 2737565696 | bytes 178372816 | solution.py:125
  515.2 4.5 bitcast_add_fusion.6
  519.7 9.6 multiply_reduce_fusion.7
  529.3 10.4 multiply_convert_fusion.8
  539.7 7.0 fusion.142
  552.1 5.7 bitcast_add_fusion.6
  557.8 9.6 multiply_reduce_fusion.7
  567.4 10.4 multiply_convert_fusion.8
  577.8 7.0 fusion.142
  584.9 4.5 bitcast_add_fusion.5
  601.6 7.7 fusion.77
  609.5 11.4 convert_bitcast_fusion.1
  621.6 19.8 %reduce-scatter.23.cloned.1.call-done = bf16[512,1,1024]{2,0,1:T(8,128)(2,1)} async-done(((bf16[1024,1,1024]{2,0,1:T(8,128)(2,1)}), bf16[512,1,1024]{2,0,1:T(8,128)(2,1)}) %reduce-scatter.23.cloned.1.call-update) | async-done | bytes 1048592 | tf_op jit(solution)/shard_map/reduce_scatter | solution.py:45
  646.0 30.2 %reduce-scatter.19.cloned.1.call-done = bf16[512,1,1024]{2,0,1:T(8,128)(2,1)} async-done(((bf16[1024,1,1024]{2,0,1:T(8,128)(2,1)}), bf16[512,1,1024]{2,0,1:T(8,128)(2,1)}) %reduce-scatter.19.cloned.1.call-update) | async-done | bytes 1048592 | tf_op jit(solution)/shard_map/reduce_scatter | solution.py:36
  676.2 5.0 fusion.62
  682.0 10.9 convolution_convert_fusion
  694.4 8.3 convolution_convert_fusion.1
  707.2 5.8 convolution_bitcast_fusion
  714.3 6.9 convolution_convert_fusion.2
  722.0 4.6 multiply_convert_fusion.1
  732.7 40.0 %all-reduce.9 = (f32[1024]{0:T(1024)S(1)}, f32[1024]{0:T(1024)S(1)}, f32[1024]{0:T(1024)S(1)}, f32[4096]{0:T(1024)S(1)}, f32[1024]{0:T(1024)S(1)}) all-reduce(f32[1024]{0:T(1024)S(1)} %dynamic_update_slice.24, f32[1024]{0:T(1024)S(1)} %dynamic_update_slice.25, ...), channel_id=14, replica_groups=mesh['fsdp'=16,'tp'=2] {'fsdp','tp'}, use_global_device_ids=true, to_apply=%region_33.34.clone | all-reduce | flops 8192 | bytes 65536
  777.5 66.8 %reduce-scatter.31.cloned.1.call-done = bf16[64,2048]{1,0:T(8,128)(2,1)} async-done(((bf16[1024,2048]{1,0:T(8,128)(2,1)}), bf16[64,2048]{1,0:T(8,128)(2,1)}) %reduce-scatter.31.cloned.1.call-update) | async-done | bytes 262160 | tf_op jit(solution)/shard_map/reduce_scatter | solution.py:311
  846.0 58.7 %reduce-scatter.29.cloned.1.call-done = bf16[512,64]{0,1:T(8,128)(2,1)} async-done(((bf16[512,1024]{0,1:T(8,128)(2,1)}), bf16[512,64]{0,1:T(8,128)(2,1)}) %reduce-scatter.29.cloned.1.call-update) | async-done | bytes 65552 | tf_op jit(solution)/shard_map/reduce_scatter | solution.py:308
  906.2 5.1 copy.72
  911.3 9.9 reduce-scatter.37.cloned.1.call-done
  922.8 134.6 %reduce-scatter.39.cloned.1.call-done = f32[32,6]{1,0:T(8,128)} async-done(((f32[1024,6]{1,0:T(8,128)}), f32[32,6]{1,0:T(8,128)}) %reduce-scatter.39.cloned.1.call-update) | async-done | bytes 784
  1058.8 64.9 %reduce-scatter.27.cloned.1.call-done = bf16[64,3,512]{2,0,1:T(8,128)(2,1)} async-done(((bf16[1024,3,512]{2,0,1:T(8,128)(2,1)}), bf16[64,3,512]{2,0,1:T(8,128)(2,1)}) %reduce-scatter.27.cloned.1.call-update) | async-done | bytes 196624 | tf_op jit(solution)/shard_map/reduce_scatter | solution.py:305
  1125.4 86.8 %reduce-scatter.35.cloned.1.call-done = bf16[64,6,512]{2,0,1:T(8,128)(2,1)} async-done(((bf16[1024,6,512]{2,0,1:T(8,128)(2,1)}), bf16[64,6,512]{2,0,1:T(8,128)(2,1)}) %reduce-scatter.35.cloned.1.call-update) | async-done | bytes 393232 | tf_op jit(solution)/shard_map/reduce_scatter | solution.py:317
  (299 shorter events, 121.4 us)
Async XLA Ops:
  7.2 76.7 %all-gather.13.cloned.1.call-start = ((), (), s32[]{:S(2)}) async-start(), calls=%async_computation.12 | async-start | bytes 6684672 | tf_op jit(solution)/shard_map/all_gather | solution.py:167
  7.9 127.1 %all-gather.17.cloned.1.call-start = ((), (), s32[]{:S(2)}) async-start(), calls=%async_computation.14 | async-start | bytes 3342336 | tf_op jit(solution)/shard_map/all_gather | solution.py:163
  8.7 147.4 %all-gather.15.cloned.1.call-start = ((), (), s32[]{:S(2)}) async-start(), calls=%async_computation.13 | async-start | bytes 3145728 | tf_op jit(solution)/shard_map/all_gather | solution.py:28
  81.6 11.3 copy-start.34
  83.9 9.1 copy-start.40
  83.9 9.7 copy-start.1
  87.7 8.2 copy-start.62
  87.7 8.4 copy-start.63
  87.7 8.6 copy-start.64
  95.0 101.1 %all-gather.19.cloned.1.call-start = ((), (), s32[]{:S(2)}) async-start(), calls=%async_computation.15 | async-start | bytes 1114112 | tf_op jit(solution)/shard_map/all_gather | solution.py:164
  95.6 135.8 %reduce-scatter.17.cloned.1.call-start = ((), (), s32[]{:S(2)}) async-start(), calls=%async_computation.16 | async-start | bytes 3145728 | tf_op jit(solution)/shard_map/reduce_scatter | solution.py:36
  196.1 35.3 %copy-start.2 = (bf16[512,1,1024]{2,0,1:T(8,128)(2,1)S(1)}, bf16[512,1,1024]{2,0,1:T(8,128)(2,1)}, u32[]{:S(2)}) copy-start(bf16[512,1,1024]{2,0,1:T(8,128)(2,1)} %param.18) | copy-start | bytes 3145732
  196.1 35.3 %copy-start.28 = (f32[1,1,1024]{2,1,0:T(1,128)S(1)}, f32[1,1,1024]{2,1,0:T(1,128)}, u32[]{:S(2)}) copy-start(f32[1,1,1024]{2,1,0:T(1,128)} %get-tuple-element.306) | copy-start | bytes 12292
  200.3 34.7 %copy-start.36 = (f32[1,1,1024]{2,1,0:T(1,128)S(1)}, f32[1,1,1024]{2,1,0:T(1,128)}, u32[]{:S(2)}) copy-start(f32[1,1,1024]{2,1,0:T(1,128)} %get-tuple-element.303) | copy-start | bytes 12292
  200.3 34.7 %copy-start.46 = (f32[1,1,1024]{2,1,0:T(1,128)S(1)}, f32[1,1,1024]{2,1,0:T(1,128)}, u32[]{:S(2)}) copy-start(f32[1,1,1024]{2,1,0:T(1,128)} %get-tuple-element.302) | copy-start | bytes 12292
  200.3 107.1 %all-gather.23.cloned.1.call-start = ((), (), s32[]{:S(2)}) async-start(), calls=%async_computation.18 | async-start | bytes 4456448 | tf_op jit(solution)/shard_map/all_gather | solution.py:165
  200.9 117.3 %all-gather.21.cloned.1.call-start = ((), (), s32[]{:S(2)}) async-start(), calls=%async_computation.17 | async-start | bytes 3145728 | tf_op jit(solution)/shard_map/all_gather | solution.py:28
  201.0 261.4 %copy-start.30 = (f32[1024]{0:T(1024)}, f32[1024]{0:T(1024)S(1)}, u32[]{:S(2)}) copy-start(f32[1024]{0:T(1024)S(1)} %convert_element_type.207) | copy-start | bytes 12292
  236.8 134.6 %all-gather.25.cloned.1.call-start = ((), (), s32[]{:S(2)}) async-start(), calls=%async_computation.19 | async-start | bytes 4456448 | tf_op jit(solution)/shard_map/all_gather | solution.py:166
  237.5 167.7 %all-gather.27.cloned.1.call-start = ((), (), s32[]{:S(2)}) async-start(), calls=%async_computation.21 | async-start | bytes 3145728 | tf_op jit(solution)/shard_map/all_gather | solution.py:32
  240.7 218.2 %reduce-scatter.21.cloned.1.call-start = ((), (), s32[]{:S(2)}) async-start(), calls=%async_computation.22 | async-start | bytes 3145728 | tf_op jit(solution)/shard_map/reduce_scatter | solution.py:45
  307.5 97.7 %copy-start.52 = (f32[2048]{0:T(1024)}, f32[2048]{0:T(1024)S(1)}, u32[]{:S(2)}) copy-start(f32[2048]{0:T(1024)S(1)} %dynamic_slice.32) | copy-start | bytes 24580
  405.2 15.9 %copy-start.57 = (bf16[1024,2048]{1,0:T(8,128)(2,1)S(1)}, bf16[1024,2048]{1,0:T(8,128)(2,1)}, u32[]{:S(2)}) copy-start(bf16[1024,2048]{1,0:T(8,128)(2,1)} %all-gather.23.cloned.1.call-done) | copy-start | bytes 12582916
  426.9 74.5 %all-gather.29.cloned.1.call-start = ((), (), s32[]{:S(2)}) async-start(), calls=%async_computation.23 | async-start | bytes 3145728 | tf_op jit(solution)/shard_map/all_gather | solution.py:32
  464.8 36.6 %copy-start.60 = (bf16[512,1024]{0,1:T(8,128)(2,1)S(1)}, bf16[512,1024]{0,1:T(8,128)(2,1)}, u32[]{:S(2)}) copy-start(bf16[512,1024]{0,1:T(8,128)(2,1)} %all-gather.19.cloned.1.call-done) | copy-start | bytes 3145732
  464.8 40.4 %copy-start.44 = (f32[512]{0:T(512)}, f32[512]{0:T(512)S(1)}, u32[]{:S(2)}) copy-start(f32[512]{0:T(512)S(1)} %negate_multiply_fusion.1) | copy-start | bytes 6148
  468.1 173.3 %reduce-scatter.23.cloned.1.call-start = ((), (), s32[]{:S(2)}) async-start(), calls=%async_computation.24 | async-start | bytes 3145728 | tf_op jit(solution)/shard_map/reduce_scatter | solution.py:45
  609.4 11.6 copy-start.54
  609.4 11.6 copy-start.18
  609.4 66.7 %reduce-scatter.19.cloned.1.call-start = ((), (), s32[]{:S(2)}) async-start(), calls=%async_computation.20 | async-start | bytes 3145728 | tf_op jit(solution)/shard_map/reduce_scatter | solution.py:36
  620.9 22.0 %copy-start.3 = (bf16[512,1,1024]{2,0,1:T(8,128)(2,1)S(1)}, bf16[512,1,1024]{2,0,1:T(8,128)(2,1)}, u32[]{:S(2)}) copy-start(bf16[512,1,1024]{2,0,1:T(8,128)(2,1)} %param.18) | copy-start | bytes 3145732
  620.9 22.0 %copy-start.33 = (f32[1,1,1024]{2,1,0:T(1,128)S(1)}, f32[1,1,1024]{2,1,0:T(1,128)}, u32[]{:S(2)}) copy-start(f32[1,1,1024]{2,1,0:T(1,128)} %copy-done.32) | copy-start | bytes 12292
  620.9 22.0 %copy-start.35 = (f32[512]{0:T(512)S(1)}, f32[512]{0:T(512)}, u32[]{:S(2)}) copy-start(f32[512]{0:T(512)} %copy-done.34) | copy-start | bytes 6148
  620.9 23.8 %copy-start.43 = (f32[512]{0:T(512)S(1)}, f32[512]{0:T(512)}, u32[]{:S(2)}) copy-start(f32[512]{0:T(512)} %copy-done.42) | copy-start | bytes 6148
  620.9 23.8 %copy-start.41 = (f32[512]{0:T(512)S(1)}, f32[512]{0:T(512)}, u32[]{:S(2)}) copy-start(f32[512]{0:T(512)} %copy-done.40) | copy-start | bytes 6148
  620.9 86.2 %reduce-scatter.25.cloned.1.call-start = ((), (), s32[]{:S(2)}) async-start(), calls=%async_computation.25 | async-start | bytes 24576 | tf_op jit(solution)/shard_map/reduce_scatter | solution.py:287
  621.0 55.2 %copy-start.9 = (bf16[512,1,1024]{2,0,1:T(8,128)(2,1)S(1)}, bf16[512,1,1024]{2,0,1:T(8,128)(2,1)}, u32[]{:S(2)}) copy-start(bf16[512,1,1024]{2,0,1:T(8,128)(2,1)} %reduce-scatter.17.cloned.1.call-done) | copy-start | bytes 3145732
  621.0 55.2 %copy-start.29 = (f32[1,1,1024]{2,1,0:T(1,128)S(1)}, f32[1,1,1024]{2,1,0:T(1,128)}, u32[]{:S(2)}) copy-start(f32[1,1,1024]{2,1,0:T(1,128)} %get-tuple-element.306) | copy-start | bytes 12292
  621.0 55.2 %copy-start.31 = (f32[1024]{0:T(1024)S(1)}, f32[1024]{0:T(1024)}, u32[]{:S(2)}) copy-start(f32[1024]{0:T(1024)} %copy-done.30) | copy-start | bytes 12292
  621.0 55.1 %copy-start.38 = (f32[1,1,1024]{2,1,0:T(1,128)S(1)}, f32[1,1,1024]{2,1,0:T(1,128)}, u32[]{:S(2)}) copy-start(f32[1,1,1024]{2,1,0:T(1,128)} %get-tuple-element.301) | copy-start | bytes 12292
  621.0 55.1 %copy-start.45 = (f32[512]{0:T(512)S(1)}, f32[512]{0:T(512)}, u32[]{:S(2)}) copy-start(f32[512]{0:T(512)} %copy-done.44) | copy-start | bytes 6148
  681.9 93.8 %reduce-scatter.33.cloned.1.call-start = ((), (), s32[]{:S(2)}) async-start(), calls=%async_computation.29 | async-start | bytes 4456448 | tf_op jit(solution)/shard_map/reduce_scatter | solution.py:314
  692.8 151.4 %reduce-scatter.31.cloned.1.call-start = ((), (), s32[]{:S(2)}) async-start(), calls=%async_computation.28 | async-start | bytes 4456448 | tf_op jit(solution)/shard_map/reduce_scatter | solution.py:311
  702.7 202.0 %reduce-scatter.29.cloned.1.call-start = ((), (), s32[]{:S(2)}) async-start(), calls=%async_computation.27 | async-start | bytes 1114112 | tf_op jit(solution)/shard_map/reduce_scatter | solution.py:308
  707.1 214.1 %reduce-scatter.37.cloned.1.call-start = ((), (), s32[]{:S(2)}) async-start(), calls=%async_computation.31 | async-start | bytes 786432
  713.1 344.3 %reduce-scatter.39.cloned.1.call-start = ((), (), s32[]{:S(2)}) async-start(), calls=%async_computation.32 | async-start | bytes 540672
  714.2 409.5 %reduce-scatter.27.cloned.1.call-start = ((), (), s32[]{:S(2)}) async-start(), calls=%async_computation.26 | async-start | bytes 3342336 | tf_op jit(solution)/shard_map/reduce_scatter | solution.py:305
  721.3 491.0 %reduce-scatter.35.cloned.1.call-start = ((), (), s32[]{:S(2)}) async-start(), calls=%async_computation.30 | async-start | bytes 6684672 | tf_op jit(solution)/shard_map/reduce_scatter | solution.py:317
  (44 other events, 173.0 us)
Sparse Core Ops, SparseCore 0:
  10.2 64.8 all-gather.12
  77.2 44.3 all-gather.16
  123.7 32.3 all-gather.14
  158.1 37.8 all-gather.18
  200.5 30.8 reduce-scatter.16
  233.6 50.7 all-gather.22
  286.6 31.6 all-gather.20
  320.6 50.6 all-gather.24
  373.6 31.5 all-gather.26
  427.0 31.8 reduce-scatter.20
  468.2 33.1 all-gather.28
  609.5 31.8 reduce-scatter.22
  644.3 31.8 reduce-scatter.18
  682.0 9.7 reduce-scatter.24
  695.5 72.9 reduce-scatter.32
  772.8 71.4 reduce-scatter.30
  848.3 56.4 reduce-scatter.28
  907.5 13.6 reduce-scatter.36
  923.4 133.9 reduce-scatter.38
  1061.5 62.1 reduce-scatter.26
  1128.1 84.0 reduce-scatter.34
where the time goes:
time: 1230 us; the launch traced here: 1220 us
  waiting for transfers between devices  682 us (55%)
  blocking collectives  221 us (18%)
  matrix products  171 us (14%)
  other arithmetic  77.1 us (6%)
  local copies, waits for them, and re-layouts  54.4 us (4%)
  between operations  15.4 us (1%)
    unnamed x23, waiting for transfers between devices  148 us
    reduce_scatter x1, waiting for transfers between devices, on_device(): lax.psum_scatter(ada_grad.astype(jnp.bfloat16), 'fsdp', scatter_dimension...  86.8 us
    unnamed x2, blocking collectives  78.2 us
    all_gather x1, blocking collectives, on_device(): lax.all_gather(ada_bias, ('fsdp', 'tp'), axis=1, tiled=True)  71.3 us
    all_gather x2, waiting for transfers between devices, gather_grads(): return lax.all_gather(piece, 'tp', axis=0, tiled=True)  67 us
    reduce_scatter x1, waiting for transfers between devices, on_device(): lax.psum_scatter(up_grad.astype(jnp.bfloat16), 'fsdp', scatter_dimension=...  66.8 us
    all_gather x1, blocking collectives, on_device(): lax.all_gather(up_bias, ('fsdp', 'tp'), axis=0, tiled=True)  66.7 us
    reduce_scatter x1, waiting for transfers between devices, on_device(): lax.psum_scatter(qkv_grad.astype(jnp.bfloat16), 'fsdp', scatter_dimension...  64.9 us
  transfers between devices with their start and end apart: 21, of which 16 were waited for; matrix products, arithmetic and copies ran while one was open for 12% of the time, Pallas kernels for 0%

commit v1 on v0

--- a/solution.py
+++ b/solution.py
@@ -1,9 +1,13 @@
+import functools
 import math
 
 import jax
 import jax.numpy as jnp
 from jax import lax
+from jax.experimental import pallas as pl
+from jax.experimental.pallas import tpu as pltpu
 from jax.sharding import PartitionSpec as P
+
 
 HD = 64
 
@@ -136,7 +140,7 @@
     return stacked.astype(jnp.bfloat16)
 
 
-def on_device(
+def on_device_general(
     latents_in,
     condition,
     grad_out,
@@ -344,9 +348,571 @@
     )
 
 
+MESH = pl.DeviceIdType.MESH
+ANY = pl.ANY
+BF = jnp.bfloat16
+F32 = jnp.float32
+
+
+def place():
+    f, x = lax.axis_index("fsdp"), lax.axis_index("tp")
+    z, y, c = f // 4, lax.rem(f // 2, 2), lax.rem(f, 2)
+    return z, y, c, x
+
+
+def at(z, y, c, x):
+    return ((z * 2 + y) * 2 + c, x)
+
+
+def remote(src, dst, send, recv, device):
+    return pltpu.make_async_remote_copy(
+        src_ref=src, dst_ref=dst, send_sem=send, recv_sem=recv, device_id=device, device_id_type=MESH
+    )
+
+
+def greet(devices):
+    barrier = pltpu.get_barrier_semaphore()
+    for device in devices:
+        pl.semaphore_signal(barrier, inc=1, device_id=device, device_id_type=MESH)
+    pl.semaphore_wait(barrier, len(devices))
+
+
+def partners(z, y, c, x, diagonal=False):
+    out = [at(z, y, 1 - c, x), at(z, 1 - y, c, x), at(z, y, c, 1 - x)]
+    out += [at(lax.rem(z + d, 4), y, c, x) for d in (1, 2, 3)]
+    if diagonal:
+        out.append(at(z, y, 1 - c, 1 - x))
+    return out
+
+
+class Gather:
+    sems = 8
+
+    def __init__(self, own, full, send, recv, local):
+        self.own, self.full, self.send, self.recv, self.local = own, full, send, recv, local
+
+    def _core(self):
+        z, y, c, x = place()
+        rows = pl.ds(pl.multiple_of(c * 64, 64), 64)
+        spot = self.full.at[x, z, y, rows]
+        return (
+            pltpu.make_async_copy(self.own.at[c], spot, self.local),
+            remote(self.own.at[1 - c], spot, self.send.at[0], self.recv.at[0], at(z, y, 1 - c, x)),
+        )
+
+    def _z(self, d):
+        z, y, c, x = place()
+        spot = self.full.at[x, z, y]
+        return remote(spot, spot, self.send.at[d], self.recv.at[d], at(lax.rem(z + d, 4), y, c, x))
+
+    def _xy(self, k):
+        z, y, c, x = place()
+        if k == 0:
+            spot, to = self.full.at[x, pl.ds(0, 2), y], at(z, y, c, 1 - x)
+        elif k == 1:
+            spot, to = self.full.at[x, pl.ds(2, 2), y], at(z, 1 - y, c, x)
+        elif k == 2:
+            spot, to = self.full.at[:, pl.ds(0, 2), y], at(z, 1 - y, c, x)
+        else:
+            spot, to = self.full.at[x, pl.ds(2, 2)], at(z, y, c, 1 - x)
+        return remote(spot, spot, self.send.at[4 + k], self.recv.at[4 + k], to)
+
+    def start_core(self):
+        for copy in self._core():
+            copy.start()
+
+    def core_to_z(self):
+        local, far = self._core()
+        local.wait()
+        far.wait()
+        for d in (1, 2, 3):
+            self._z(d).start()
+
+    def z_to_xy(self):
+        for d in (1, 2, 3):
+            self._z(d).wait()
+        self._xy(0).start()
+        self._xy(1).start()
+
+    def xy_to_last(self):
+        self._xy(0).wait()
+        self._xy(2).start()
+        self._xy(1).wait()
+        self._xy(3).start()
+
+    def finish(self):
+        self._xy(2).wait()
+        self._xy(3).wait()
+
+
+class Scatter:
+    sems = 8
+
+    def __init__(self, part, first_a, first_b, second, third, total, out, send, recv, local):
+        self.part, self.first_a, self.first_b = part, first_a, first_b
+        self.second, self.third, self.total, self.out = second, third, total, out
+        self.send, self.recv, self.local = send, recv, local
+
+    def _copy(self, k):
+        z, y, c, x = place()
+        send, recv = self.send.at[k], self.recv.at[k]
+        if k == 0:
+            return remote(self.part.at[:, pl.ds(0, 2), 1 - y], self.first_a, send, recv, at(z, 1 - y, c, x))
+        if k == 1:
+            return remote(self.part.at[1 - x, pl.ds(2, 2)], self.first_b, send, recv, at(z, y, c, 1 - x))
+        if k == 2:
+            return remote(self.first_a.at[1 - x], self.second.at[pl.ds(0, 2)], send, recv, at(z, y, c, 1 - x))
+        if k == 3:
+            return remote(self.first_b.at[:, 1 - y], self.second.at[pl.ds(2, 2)], send, recv, at(z, 1 - y, c, x))
+        if k <= 6:
+            d = k - 3
+            to = lax.rem(z + d, 4)
+            return remote(self.second.at[to], self.third.at[d - 1], send, recv, at(to, y, c, x))
+        rows = pl.ds(pl.multiple_of((1 - c) * 64, 64), 64)
+        return remote(self.total.at[rows], self.out.at[c], send, recv, at(z, y, 1 - c, x))
+
+    def _own(self):
+        z, y, c, x = place()
+        rows = pl.ds(pl.multiple_of(c * 64, 64), 64)
+        return pltpu.make_async_copy(self.total.at[rows], self.out.at[c], self.local)
+
+    def start(self):
+        self._copy(0).start()
+        self._copy(1).start()
+
+    def first(self):
+        z, y, c, x = place()
+        self._copy(0).wait()
+
+        def add_a(i, carry):
+            self.first_a[i // 2, i % 2] = (
+                self.first_a[i // 2, i % 2].astype(F32) + self.part[i // 2, i % 2, y].astype(F32)
+            ).astype(BF)
+            return carry
+
+        lax.fori_loop(0, 4, add_a, 0)
+        self._copy(2).start()
+        self._copy(1).wait()
+
+        def add_b(i, carry):
+            self.first_b[i // 2, i % 2] = (
+                self.first_b[i // 2, i % 2].astype(F32) + self.part[x, 2 + i // 2, i % 2].astype(F32)
+            ).astype(BF)
+            return carry
+
+        lax.fori_loop(0, 4, add_b, 0)
+        self._copy(3).start()
+
+    def next(self):
+        z, y, c, x = place()
+        self._copy(2).wait()
+
+        def add_a(i, carry):
+            self.second[i] = (self.second[i].astype(F32) + self.first_a[x, i].astype(F32)).astype(BF)
+            return carry
+
+        lax.fori_loop(0, 2, add_a, 0)
+        self._copy(3).wait()
+
+        def add_b(i, carry):
+            self.second[2 + i] = (self.second[2 + i].astype(F32) + self.first_b[i, y].astype(F32)).astype(BF)
+            return carry
+
+        lax.fori_loop(0, 2, add_b, 0)
+        for k in (4, 5, 6):
+            self._copy(k).start()
+
+    def last(self):
+        z, y, c, x = place()
+        for k in (4, 5, 6):
+            self._copy(k).wait()
+
+        def add(i, carry):
+            rows = pl.ds(pl.multiple_of(i * 64, 64), 64)
+            total = self.second[z, rows].astype(F32)
+            for d in range(3):
+                total = total + self.third[d, rows].astype(F32)
+            self.total[rows] = total
+            return carry
+
+        lax.fori_loop(0, 2, add, 0)
+        self._copy(7).start()
+        self._own().start()
+
+    def finish(self):
+        self._copy(7).wait()
+        self._own().wait()
+
+
+class Swap:
+    sems = 2
+
+    def __init__(self, own, full, send, recv, local):
+        self.own, self.full, self.send, self.recv, self.local = own, full, send, recv, local
+
+    def _far(self):
+        z, y, c, x = place()
+        return remote(self.own, self.full.at[1 - c], self.send.at[0], self.recv.at[0], at(z, y, 1 - c, 1 - x))
+
+    def _near(self):
+        z, y, c, x = place()
+        return pltpu.make_async_copy(self.own, self.full.at[c], self.local)
+
+    def _core(self):
+        z, y, c, x = place()
+        spot = self.full.at[c]
+        return remote(spot, spot, self.send.at[1], self.recv.at[1], at(z, y, 1 - c, x))
+
+    def start(self):
+        z, y, c, x = place()
+
+        @pl.when(c != x)
+        def _():
+            self._far().start()
+
+        @pl.when(c == x)
+        def _():
+            self._near().start()
+
+    def share(self):
+        z, y, c, x = place()
+
+        @pl.when(c != x)
+        def _():
+            self._far().wait()
+
+        @pl.when(c == x)
+        def _():
+            self._near().wait()
+
+        self._core().start()
+
+    def finish(self):
+        self._core().wait()
+
+
+COLS = (768, 256, 1024, 1024)
+
+
+def gather_kernel(lat, grad, wq, wp, wu, wd, lat_full, grad_full, gq, gp, gu, gd, send, recv, local):
+    z, y, c, x = place()
+    greet(partners(z, y, c, x, True))
+    swaps = [
+        Swap(own, full, send.at[4 + i], recv.at[4 + i], local.at[4 + i])
+        for i, (own, full) in enumerate(((lat, lat_full), (grad, grad_full)))
+    ]
+    groups = [
+        Gather(own, full, send.at[i], recv.at[i], local.at[i])
+        for i, (own, full) in enumerate(((wq, gq), (wp, gp), (wu, gu), (wd, gd)))
+    ]
+    for group in groups:
+        group.start_core()
+    swaps[0].start()
+    for group in groups:
+        group.core_to_z()
+    for group in groups:
+        group.z_to_xy()
+    swaps[0].share()
+    swaps[1].start()
+    for group in groups:
+        group.xy_to_last()
+    for group in groups:
+        group.finish()
+    swaps[1].share()
+    for swap in swaps:
+        swap.finish()
+
+
+def gather_all(lat, grad, wq, wp, wu, wd):
+    outs = [jax.ShapeDtypeStruct((2, 512, 1024), BF)] * 2
+    outs += [jax.ShapeDtypeStruct((2, 4, 2, 128, n), BF) for n in COLS]
+    return pl.pallas_call(
+        gather_kernel,
+        out_shape=outs,
+        in_specs=[pl.BlockSpec(memory_space=ANY)] * 6,
+        out_specs=[pl.BlockSpec(memory_space=ANY)] * 6,
+        scratch_shapes=[
+            pltpu.SemaphoreType.DMA((6, 8)),
+            pltpu.SemaphoreType.DMA((6, 8)),
+            pltpu.SemaphoreType.DMA((6,)),
+        ],
+        compiler_params=pltpu.CompilerParams(collective_id=0, has_side_effects=True),
+        name="gather_all",
+    )(lat, grad, wq, wp, wu, wd)
+
+
+def scatter_buffers(n):
+    return [
+        pltpu.VMEM((2, 2, 128, n), BF),
+        pltpu.VMEM((2, 2, 128, n), BF),
+        pltpu.VMEM((4, 128, n), BF),
+        pltpu.VMEM((3, 128, n), BF),
+        pltpu.VMEM((128, n), F32),
+    ]
+
+
+def scatter_kernel(dq, dp, du, dd, oq, op, ou, od, *rest):
+    buffers, (send, recv, local) = rest[:-3], rest[-3:]
+    z, y, c, x = place()
+    greet(partners(z, y, c, x))
+    groups = []
+    for i, (part, out) in enumerate(((dq, oq), (dp, op), (du, ou), (dd, od))):
+        groups.append(Scatter(part, *buffers[5 * i : 5 * i + 5], out, send.at[i], recv.at[i], local.at[i]))
+    groups = [groups[i] for i in (3, 2, 1, 0)]
+    for group in groups:
+        group.start()
+    for group in groups:
+        group.first()
+    for group in groups:
+        group.next()
+    for group in groups:
+        group.last()
+    for group in groups:
+        group.finish()
+
+
+def scatter_all(*parts):
+    scratch = []
+    for n in COLS:
+        scratch += scatter_buffers(n)
+    return pl.pallas_call(
+        scatter_kernel,
+        out_shape=[jax.ShapeDtypeStruct((2, 64, n), F32) for n in COLS],
+        in_specs=[pl.BlockSpec(memory_space=pltpu.VMEM)] * 4,
+        out_specs=[pl.BlockSpec(memory_space=ANY)] * 4,
+        scratch_shapes=scratch
+        + [
+            pltpu.SemaphoreType.DMA((4, 8)),
+            pltpu.SemaphoreType.DMA((4, 8)),
+            pltpu.SemaphoreType.DMA((4,)),
+        ],
+        compiler_params=pltpu.CompilerParams(
+            collective_id=1, has_side_effects=True, vmem_limit_bytes=56 * 2**20
+        ),
+        name="scatter_all",
+    )(*parts)
+
+
+def swap_back_kernel(block, grad, block_out, grad_out, send, recv, local):
+    z, y, c, x = place()
+    greet([at(z, y, 1 - c, 1 - x)])
+
+    @pl.when(c != x)
+    def _():
+        copies = [
+            remote(a, b, send.at[i], recv.at[i], at(z, y, 1 - c, 1 - x))
+            for i, (a, b) in enumerate(((block, block_out), (grad, grad_out)))
+        ]
+        for copy in copies:
+            copy.start()
+        for copy in copies:
+            copy.wait()
+
+    @pl.when(c == x)
+    def _():
+        copies = [
+            pltpu.make_async_copy(a, b, local.at[i]) for i, (a, b) in enumerate(((block, block_out), (grad, grad_out)))
+        ]
+        for copy in copies:
+            copy.start()
+        for copy in copies:
+            copy.wait()
+
+
+def swap_back(block, grad):
+    return pl.pallas_call(
+        swap_back_kernel,
+        out_shape=[jax.ShapeDtypeStruct(a.shape, a.dtype) for a in (block, grad)],
+        in_specs=[pl.BlockSpec(memory_space=ANY)] * 2,
+        out_specs=[pl.BlockSpec(memory_space=ANY)] * 2,
+        scratch_shapes=[
+            pltpu.SemaphoreType.DMA((2,)),
+            pltpu.SemaphoreType.DMA((2,)),
+            pltpu.SemaphoreType.DMA((2,)),
+        ],
+        compiler_params=pltpu.CompilerParams(collective_id=2, has_side_effects=True),
+        name="swap_back",
+    )(block, grad)
+
+
+def pair_sum(partial):
+    pairs = [(i, i ^ 1) for i in range(16)]
+    rounded = partial.astype(BF)
+    return partial + lax.ppermute(rounded, "fsdp", pairs).astype(F32)
+
+
+def spread(vectors, sizes):
+    everyone = lax.all_gather(vectors, ("fsdp", "tp"), axis=0, tiled=False)
+    parts, first = [], 0
+    for size in sizes:
+        parts.append(everyone[:, first : first + size])
+        first += size
+    return parts
+
+
+def on_device_pairs(
+    latents_in,
+    condition,
+    grad_out,
+    qkv_weight,
+    proj_weight,
+    up_weight,
+    down_weight,
+    ada_weight,
+    query_bias,
+    value_bias,
+    proj_bias,
+    up_bias,
+    down_bias,
+    ada_bias,
+):
+    z, y, c, x = place()
+    wq = qkv_weight.reshape(64, 3, 2, 256).transpose(2, 0, 1, 3).reshape(2, 64, 768)
+    wp = proj_weight.T.reshape(64, 2, 256).transpose(1, 0, 2)
+    wu = up_weight.reshape(64, 2, 1024).transpose(1, 0, 2)
+    wd = down_weight.T.reshape(64, 2, 1024).transpose(1, 0, 2)
+    lat_full, grad_full, gq, gp, gu, gd = gather_all(
+        latents_in.reshape(512, 1024), grad_out.reshape(512, 1024), wq, wp, wu, wd
+    )
+    gq, gp, gu, gd = [g.reshape(2, 1024, -1) for g in (gq, gp, gu, gd)]
+    biases = jnp.concatenate([query_bias, value_bias, proj_bias, down_bias, up_bias, ada_bias.reshape(-1)])
+    all_q, all_v, all_p, all_d, all_u, all_a = [
+        b.astype(F32) for b in spread(biases, (32, 32, 32, 32, 128, 192))
+    ]
+    all_q, all_v, all_p, all_d, all_u = [b.reshape(-1) for b in (all_q, all_v, all_p, all_d, all_u)]
+    all_a = all_a.reshape(32, 6, 32).transpose(1, 0, 2).reshape(6, 1024)
+    conditions = lax.all_gather(condition, "fsdp", axis=0, tiled=True)
+    silu_all = jax.nn.silu(conditions.astype(F32)).astype(BF)
+    my_rows = (z * 4 + y * 2 + c) * 64
+    silu_mine = lax.dynamic_slice_in_dim(silu_all, my_rows, 64, 1)
+    mod_part = jnp.einsum("bc,ctf->btf", silu_mine, ada_weight, preferred_element_type=F32)
+    mod_half = lax.psum_scatter(mod_part, "fsdp", scatter_dimension=0, tiled=True)
+    mods = lax.all_gather(mod_half, ("fsdp", "tp"), axis=0, tiled=True)
+    latent = (z * 2 + y) * 2 + x
+    modulation = (
+        lax.dynamic_slice_in_dim(mods, latent * 2, 2, 0).transpose(1, 0, 2).reshape(6, 1024) + all_a
+    )
+    m = [modulation[i : i + 1] for i in range(6)]
+    half = lambda v, width: jnp.stack(
+        [lax.dynamic_slice_in_dim(v, b * 2 * width + c * width, width, 0) for b in range(2)]
+    )
+    q_cols, v_cols, u_cols = half(all_q, 256), half(all_v, 256), half(all_u, 1024)
+
+    xin = lat_full.reshape(1024, 1024).astype(F32)
+    attn_in = modulate(xin, m[0], m[1]).astype(BF)
+    bias_three = jnp.stack([q_cols, jnp.zeros_like(q_cols), v_cols], 1).reshape(2, 1, 768)
+    packed = (jnp.einsum("sd,xdn->xsn", attn_in, gq, preferred_element_type=F32) + bias_three).astype(BF)
+    packed4 = packed.reshape(2, 1024, 3, 256).transpose(1, 2, 0, 3).reshape(1024, 1, 3, 512)
+    heads_out, log_sums = attend_forward(packed4)
+    heads_out = heads_out.reshape(1024, 512)
+    wproj = gp.transpose(1, 0, 2).reshape(1024, 512)
+    branch_one = pair_sum(jnp.einsum("sf,df->sd", heads_out, wproj, preferred_element_type=F32)) + all_p
+    middle = xin + m[2] * branch_one
+    mlp_in = modulate(middle, m[3], m[4]).astype(BF)
+    hidden = jnp.einsum("sd,xdn->xsn", mlp_in, gu, preferred_element_type=F32) + u_cols[:, None]
+    active = gelu_tanh(hidden).astype(BF)
+    branch_two = pair_sum(jnp.einsum("xsn,xdn->sd", active, gd, preferred_element_type=F32)) + all_d
+    block_out = (middle + m[5] * branch_two).astype(BF)
+    g = grad_full.reshape(1024, 1024).astype(F32)
+    gate_two_grad = jnp.sum(g * branch_two, 0)
+    g2 = (g * m[5]).astype(BF)
+    own_rows = lambda a: lax.dynamic_slice_in_dim(a, c * 512, 512, 0)
+    down_bias_part = jnp.sum(own_rows(g2).astype(F32), 0)
+    _, gelu_pull = jax.vjp(gelu_tanh, hidden)
+    active_grad = jnp.einsum("sd,xdn->xsn", g2, gd, preferred_element_type=F32)
+    down_grad = jnp.einsum("sd,xsn->xdn", g2, active, preferred_element_type=F32).astype(BF)
+    hidden_grad = gelu_pull(active_grad)[0].astype(BF)
+    up_grad = jnp.einsum("sd,xsn->xdn", mlp_in, hidden_grad, preferred_element_type=F32).astype(BF)
+    up_bias_part = jnp.sum(hidden_grad.astype(F32), 1)
+    mlp_in_grad = pair_sum(jnp.einsum("xsn,xdn->sd", hidden_grad, gu, preferred_element_type=F32))
+    _, second_pull = jax.vjp(modulate, middle, m[3], m[4])
+    middle_part, shift_two_grad, scale_two_grad = second_pull(mlp_in_grad)
+    middle_grad = g + middle_part
+    gate_one_grad = jnp.sum(middle_grad * branch_one, 0)
+    g1 = (middle_grad * m[2]).astype(BF)
+    proj_bias_part = jnp.sum(own_rows(g1).astype(F32), 0)
+    heads_grad = jnp.einsum("sd,df->sf", g1, wproj, preferred_element_type=F32).astype(BF)
+    proj_grad = jnp.einsum("sd,sf->df", g1, heads_out, preferred_element_type=F32).astype(BF)
+    proj_grad = proj_grad.reshape(1024, 2, 256).transpose(1, 0, 2)
+    packed_grad = attend_backward(packed4, log_sums, heads_grad.reshape(1024, 1, 512)).reshape(1024, 3, 2, 256)
+    packed_grad = packed_grad.transpose(2, 0, 1, 3).reshape(2, 1024, 768)
+    qkv_grad = jnp.einsum("sd,xsn->xdn", attn_in, packed_grad, preferred_element_type=F32).astype(BF)
+    packed_sums = jnp.sum(packed_grad.astype(F32), 1)
+    attn_in_grad = pair_sum(jnp.einsum("xsn,xdn->sd", packed_grad, gq, preferred_element_type=F32))
+    _, first_pull = jax.vjp(modulate, xin, m[0], m[1])
+    input_part, shift_one_grad, scale_one_grad = first_pull(attn_in_grad)
+    input_grad = middle_grad + input_part
+
+    block_mine, grad_mine = swap_back(own_rows(block_out), own_rows(input_grad.astype(BF)))
+    parts = scatter_all(
+        *[p.reshape(2, 4, 2, 128, -1) for p in (qkv_grad, proj_grad, up_grad, down_grad)]
+    )
+    oq, op, ou, od = parts
+    qkv_sum = oq.reshape(2, 64, 3, 256).transpose(1, 2, 0, 3).reshape(64, 3, 512)
+    proj_sum = op.transpose(1, 0, 2).reshape(64, 512).T
+    up_sum = ou.transpose(1, 0, 2).reshape(64, 2048)
+    down_sum = od.transpose(1, 0, 2).reshape(64, 2048).T
+    mod_grad = jnp.stack(
+        [shift_one_grad[0], scale_one_grad[0], gate_one_grad, shift_two_grad[0], scale_two_grad[0], gate_two_grad]
+    )
+    mine = lax.dynamic_slice_in_dim(mod_grad, c * 512, 512, 1)
+    every = lax.all_gather(mine, ("fsdp", "tp"), axis=0, tiled=False).reshape(4, 2, 2, 2, 6, 512)
+    mod_cols = lax.dynamic_index_in_dim(every, x, 2, False).reshape(16, 6, 512)
+    ada_sum = jnp.einsum(
+        "bc,btf->ctf", silu_mine.astype(F32), mod_cols, precision=lax.Precision.HIGHEST
+    )
+    ada_bias_cols = jnp.sum(mod_cols, 0)
+    ada_bias_sum = lax.dynamic_slice_in_dim(ada_bias_cols, (z * 4 + y * 2 + c) % 8 * 64 + x * 32, 32, 1)
+    every_bias = jnp.sum(every, axis=(0, 1, 3))
+    own_col = ((z * 4 + y * 2 + c) * 2 + x) * 32
+    ada_bias_sum = lax.dynamic_slice_in_dim(
+        every_bias.transpose(1, 0, 2).reshape(6, 1024), own_col, 32, 1
+    )
+    silu_part = jnp.einsum(
+        "btf,ctf->bc", mod_cols, ada_weight.astype(F32), precision=lax.Precision.HIGHEST
+    )
+    silu_every = lax.all_gather(silu_part, ("fsdp", "tp"), axis=0, tiled=False).reshape(16, 2, 16, 64).sum(1)
+    f = z * 4 + y * 2 + c
+    silu_row = lax.dynamic_index_in_dim(silu_every, f, 1, False).reshape(1, 1024)
+    silu_cols = lax.dynamic_slice_in_dim(silu_row, x * 512, 512, 1)
+    cond_cols = lax.dynamic_slice_in_dim(condition.astype(F32), x * 512, 512, 1)
+    _, silu_pull = jax.vjp(jax.nn.silu, cond_cols)
+    cond_grad = silu_pull(silu_cols)[0]
+    put = lambda v, width: sum(
+        lax.dynamic_update_slice(
+            jnp.zeros((4 * width,), F32), v[b], (b * 2 * width + c * width,)
+        )
+        for b in range(2)
+    )
+    q_part, v_part = put(packed_sums[:, :256], 256), put(packed_sums[:, 512:], 256)
+    u_part = put(up_bias_part, 1024)
+    bias_parts = jnp.concatenate(
+        [b.reshape(32, -1) for b in (q_part, v_part, proj_bias_part, down_bias_part, u_part)], 1
+    )
+    bias_sums = lax.psum_scatter(bias_parts, ("fsdp", "tp"), scatter_dimension=0, tiled=True)[0]
+    return (
+        block_mine.reshape(512, 1, 1024),
+        grad_mine.astype(F32).reshape(512, 1, 1024),
+        cond_grad,
+        qkv_sum,
+        proj_sum,
+        up_sum,
+        down_sum,
+        ada_sum,
+        bias_sums[0:32],
+        bias_sums[32:64],
+        bias_sums[64:96],
+        bias_sums[128:256],
+        bias_sums[96:128],
+        ada_bias_sum,
+    )
+
+
 def solution(mesh):
+    shape = dict(mesh.shape)
+    pairs = shape["fsdp"] == 16 and shape["tp"] == 2
     return jax.shard_map(
-        on_device,
+        on_device_pairs if pairs else on_device_general,
         mesh=mesh,
         in_specs=(
             P("tp", "fsdp", None),

time: 1230 us -> 1030 us (0.84)
  waiting for transfers between devices: 682 us -> 0.06 us
  Pallas kernels: 0 us -> 386 us
  blocking collectives: 221 us -> 311 us
  local copies, waits for them, and re-layouts: 54.4 us -> 79.3 us
  matrix products: 171 us -> 151 us
    reduce_scatter x10 -> x0, waiting for transfers between devices: 390 us -> none  [the longest x1 86.8 us: on_device(): lax.psum_scatter(ada_grad.astype(jnp.bfloat16), 'fsdp', scatter_dimension...]
    pallas_call x0 -> x3, Pallas kernels: none -> 386 us  [the longest x1 168 us: gather_all(): pl.pallas_call(gather_kernel, out_shape=outs, in_specs=[pl.BlockSpec(memo...]
    unnamed x23 -> x2, waiting for transfers between devices: 148 us -> 0.02 us
    all_gather x9 -> x0, waiting for transfers between devices: 144 us -> none  [the longest x2 67 us: gather_grads(): return lax.all_gather(piece, 'tp', axis=0, tiled=True)]
    all_gather x3 -> x4, blocking collectives: 143 us -> 237 us  [the longest x1 75.9 us: on_device_pairs(): mods = lax.all_gather(mod_half, ('fsdp', 'tp'), axis=0, tiled=True)]
    reshape x1 -> x24, local copies, waits for them, and re-layouts: 4.3 us -> 26.7 us  [the longest x3 4.66 us: on_device_pairs(): all_a = all_a.reshape(32, 6, 32).transpose(1, 0, 2).reshape(6, 1024)]
    dot_general x14 -> x15, matrix products: 101 us -> 81.5 us  [the longest x1 13.2 us: on_device_pairs(): active_grad = jnp.einsum('sd,xdn->xsn', g2, gd, preferred_element_type=F32)]
    unnamed x141 -> x128, local copies, waits for them, and re-layouts: 27 us -> 21.5 us
  transfers between devices with their start and end apart: 21 -> 5, of which waited for: 16 -> 0; matrix products, arithmetic and copies ran while one was open for 12% -> 8% of each run, Pallas kernels for 0% -> 31%
where the time goes in v1:
time: 1030 us; the launch traced here: 1020 us
  Pallas kernels  386 us (37%)
  blocking collectives  311 us (30%)
  matrix products  151 us (15%)
  local copies, waits for them, and re-layouts  79.3 us (8%)
  other arithmetic  78 us (8%)
  between operations  15.2 us (1%)
    pallas_call x1, Pallas kernels, gather_all(): pl.pallas_call(gather_kernel, out_shape=outs, in_specs=[pl.BlockSpec(memo...  168 us
    pallas_call x1, Pallas kernels, scatter_all(): pl.pallas_call(scatter_kernel, out_shape=[jax.ShapeDtypeStruct((2, 64, n)...  153 us
    all_gather x1, blocking collectives, on_device_pairs(): mods = lax.all_gather(mod_half, ('fsdp', 'tp'), axis=0, tiled=True)  75.9 us
    unnamed x2, blocking collectives  74.3 us
    all_gather x1, blocking collectives, on_device_pairs(): lax.all_gather(mine, ('fsdp', 'tp'), axis=0, tiled=False)  69.7 us
    all_gather x1, blocking collectives, on_device_pairs(): lax.all_gather(silu_part, ('fsdp', 'tp'), axis=0, tiled=False)  67.5 us
    pallas_call x1, Pallas kernels, swap_back(): pl.pallas_call(swap_back_kernel, out_shape=[jax.ShapeDtypeStruct(a.shape,...  64.7 us
    all_gather x1, blocking collectives, on_device_pairs(): conditions = lax.all_gather(condition, 'fsdp', axis=0, tiled=True)  23.6 us
  transfers between devices with their start and end apart: 5, of which 0 were waited for; matrix products, arithmetic and copies ran while one was open for 8% of the time, Pallas kernels for 31%

profile of v1, /device:TPU:0, one launch (start us, length us, event | category | flops | bytes accessed | tf_op | source)
XLA Modules:
  0.0 1021.8 jit_solution(17808545914622649968)
XLA Ops:
  7.3 23.6 %all-gather.3 = bf16[16,1,1024]{2,1,0:T(2,128)(2,1)S(1)} all-gather(bf16[1,1,1024]{2,1,0:T(2,128)(2,1)} %bitcast.477), channel_id=1, replica_groups=mesh['fsdp'=16,'tp'=2] {'fsdp'}, dimensions={0}, use_global_device_ids=true | all-gather | bytes 34816 | tf_op jit(solution)/shard_map/all_gather | solution.py:784
  32.7 3.4 concatenate.10
  36.4 37.2 %all-reduce = bf16[14336]{0:T(1024)(128)(2,1)S(1)} all-reduce(bf16[14336]{0:T(1024)(128)(2,1)S(1)} %dynamic-update-slice.3), channel_id=2, replica_groups=mesh['fsdp'=16,'tp'=2] {'fsdp','tp'}, use_global_device_ids=true, to_apply=%add | all-reduce | flops 14336 | bytes 57344
  82.8 168.0 %gather_all.1 = (bf16[2,512,1024]{2,1,0:T(8,128)(2,1)}, bf16[2,512,1024]{2,1,0:T(8,128)(2,1)}, bf16[2,4,2,128,768]{4,3,2,1,0:T(8,128)(2,1)}, bf16[2,4,2,128,256]...) custom-call(bf16[512,1024]{1,0:T(8,128)(2,1)} %bitcast.430, ...), custom_call_target="tpu_custom_call" | custom-call | tf_op jit(solution)/shard_map/gather_all/pallas_call | solution.py:629
  266.9 75.9 %all_gather.25 = f32[32,6,512]{2,1,0:T(8,128)S(1)} all-gather(f32[1,6,512]{2,1,0:T(8,128)S(1)} %copy.100), channel_id=1, replica_groups=mesh['fsdp'=16,'tp'=2] {'fsdp','tp'}, dimensions={0}, use_global_device_ids=true | all-gather | bytes 405504 | tf_op jit(solution)/shard_map/all_gather | solution.py:790
  345.1 4.0 add_convert_fusion
  354.0 23.0 %while.27 = (s32[]{:T(128)}, bf16[2,512,1,8,64]{1,4,3,2,0:T(8,128)(2,1)}, f32[2,1,8,512]{3,2,1,0:T(8,128)S(1)}, bf16[2,512,1,8,64]{1,4,3,2,0:T(8,128)(2,1)S(1)},...) while((s32[]{:T(128)}, bf16[2,512,1,8,64]{1,4,3,2,0:T(8,128)(2,1)}, ...), condition=%wide.region_6.7_spmd, body=%wide.region_3.6_spmd.sunk | while | flops 1111748608 | bytes 66191540 | solution.py:84
  354.0 2.5 multiply_reduce_fusion.8
  356.5 3.4 fusion.140
  360.0 4.3 fusion.141
  367.8 3.4 fusion.140
  371.3 4.3 fusion.141
  379.8 4.0 fusion.102
  388.3 4.0 fusion.95
  393.0 3.0 copy-done.58
  396.0 7.0 fusion.87
  403.0 13.2 %convert_reduce_fusion = (f32[2,1024]{1,0:T(2,128)S(1)}, bf16[2,1024,1024]{2,1,0:T(8,128)(2,1)}) fusion(f32[2,1024,1024]{1,2,0:T(8,128)} %fusion.87, f32[2,1024]{1,0:T(2,128)S(1)} %pad_maximum_fusion, bf16[1024,1024,1]{1,0,2:T(8,128)(2,1)S(1)} %bitcast.419, bf16[2,1024,1024]{2,1,0:T(8,128)(2,1)S(1)} %bitcast.489), kind=kOutput, calls=%fused_computation.63 | convolution fusion | flops 4343199744 | bytes 18890752 | tf_op jit(solution)/shard_map/sd,xdn->xsn/dot_general | solution.py:822
  416.2 6.5 bitcast_convert_fusion.1
  423.3 11.8 %bitcast_convert_fusion.2 = (bf16[1024,1024]{1,0:T(8,128)(2,1)}, f32[1024,1024,1]{1,0,2:T(8,128)}) fusion(bf16[2,1024,1024]{2,1,0:T(8,128)(2,1)S(1)} %bitcast.490, f32[2,1024,1024]{1,2,0:T(8,128)} %fusion.87, f32[2,1024]{1,0:T(2,128)S(1)} %pad_maximum_fusion), kind=kOutput, calls=%fused_computation.80 | convolution fusion | flops 4316987392 | bytes 18882560 | tf_op jit(solution)/shard_map/xsn,xdn->sd/dot_general | solution.py:814
  435.0 6.6 convolution_convert_fusion.1
  442.0 2.7 multiply_reduce_fusion.2
  447.5 6.8 multiply_reduce_fusion.3
  463.2 4.0 fusion.68
  467.9 3.9 reshape.541
  471.8 3.3 copy.111
  475.1 76.7 %while.28 = (s32[]{:T(128)}, f32[1024,1,8,64]{0,3,2,1:T(8,128)}, f32[1024,1,8,64]{0,3,2,1:T(8,128)}, bf16[2,512,1,8,64]{1,4,3,2,0:T(8,128)(2,1)}, bf16[2,512,1,8...) while((s32[]{:T(128)}, f32[1024,1,8,64]{0,3,2,1:T(8,128)}, ...), condition=%wide.region_13.14_spmd.clone, body=%wide.region_11.13_spmd.clone.sunk | while | flops 2737565696 | bytes 178372816 | solution.py:129
  477.9 4.5 bitcast_add_fusion.12
  482.3 9.6 multiply_reduce_fusion.9
  491.9 10.4 %multiply_convert_fusion.6 = bf16[8,512,1024]{2,1,0:T(8,128)(2,1)} fusion(f32[8,512,1024]{2,1,0:T(8,128)} %get-tuple-element.468, f32[8,512,1024]{2,1,0:T(8,128)S(1)} %fusion.150, f32[8,512]{1,0:T(8,128)S(1)} %get-tuple-element.469, f32[8,512]{1,0:T(8,128)S(1)} %dynamic-slice_bitcast_fusion.8), kind=kLoop, calls=%fused_computation.16.clone.1 | loop fusion | flops 20971520 | bytes 41975808 | tf_op jit(solution)/shard_map/while/body/eval_jaxpr/convert_element_type | solution.py:110
  502.3 7.0 fusion.151
  509.3 2.9 bitcast_add_fusion.11
  514.6 5.6 bitcast_add_fusion.12
  520.3 9.6 multiply_reduce_fusion.9
  529.9 10.4 %multiply_convert_fusion.6 = bf16[8,512,1024]{2,1,0:T(8,128)(2,1)} fusion(f32[8,512,1024]{2,1,0:T(8,128)} %get-tuple-element.468, f32[8,512,1024]{2,1,0:T(8,128)S(1)} %fusion.150, f32[8,512]{1,0:T(8,128)S(1)} %get-tuple-element.469, f32[8,512]{1,0:T(8,128)S(1)} %dynamic-slice_bitcast_fusion.8), kind=kLoop, calls=%fused_computation.16.clone.1 | loop fusion | flops 20971520 | bytes 41975808 | tf_op jit(solution)/shard_map/while/body/eval_jaxpr/convert_element_type | solution.py:110
  540.3 7.0 fusion.151
  547.3 4.5 bitcast_add_fusion.11
  567.1 5.4 bitcast_convert_fusion
  573.0 4.8 convert_bitcast_fusion
  577.7 4.8 copy.116
  582.5 10.2 convolution_convert_fusion
  592.7 152.9 %scatter_all.1 = (f32[2,64,768]{2,1,0:T(8,128)}, f32[2,64,256]{2,1,0:T(8,128)}, f32[2,64,1024]{2,1,0:T(8,128)}, f32[2,64,1024]{2,1,0:T(8,128)}) custom-call(bf16[2,4,2,128,768]{4,3,2,1,0:T(8,128)(2,1)} %bitcast.403, bf16[2,4,2,128,256]{4,3,2,1,0:T(8,128)(2,1)} %bitcast.412, bf16[2,4,2,128,1024]{4,3,2,1,0:T(8,128)(2,1)} %bitcast.406, ...), custom_call_target="tpu_custom_call" | custom-call | tf_op jit(solution)/shard_map/scatter_all/pallas_call | solution.py:678
  753.8 4.3 fusion.65
  758.2 69.7 %all-gather.4 = f32[32,6,512]{2,1,0:T(8,128)S(1)} all-gather(f32[1,6,512]{2,1,0:T(8,128)S(1)} %dynamic-slice_bitcast_fusion.1), channel_id=3, replica_groups=mesh['fsdp'=16,'tp'=2] {'fsdp','tp'}, dimensions={0}, use_global_device_ids=true | all-gather | bytes 405504 | tf_op jit(solution)/shard_map/all_gather | solution.py:859
  830.6 4.1 fusion.93
  836.6 64.7 %swap_back.1 = (bf16[512,1024]{1,0:T(8,128)(2,1)}, bf16[512,1024]{1,0:T(8,128)(2,1)}) custom-call(bf16[512,1024]{1,0:T(8,128)(2,1)} %get-tuple-element.368.block, bf16[512,1024]{1,0:T(8,128)(2,1)} %get-tuple-element.366.grad), custom_call_target="tpu_custom_call" | custom-call | tf_op jit(solution)/shard_map/swap_back/pallas_call | solution.py:723
  901.4 37.1 %all-reduce.2 = f32[32,256]{1,0:T(8,128)S(1)} all-reduce(f32[32,256]{1,0:T(8,128)S(1)} %concatenate.11), channel_id=6, replica_groups=mesh['fsdp'=16,'tp'=2] {'fsdp','tp'}, use_global_device_ids=true, to_apply=%region_27.28.clone | all-reduce | flops 8192 | bytes 65536
  938.7 67.5 %all-gather.2 = f32[512,64]{1,0:T(8,128)S(1)} all-gather(f32[16,64]{1,0:T(8,128)S(1)} %convolution_bitcast_fusion), channel_id=4, replica_groups=mesh['fsdp'=16,'tp'=2] {'fsdp','tp'}, dimensions={0}, use_global_device_ids=true | all-gather | bytes 135168 | tf_op jit(solution)/shard_map/all_gather | solution.py:874
  1007.8 3.5 copy.124
  (269 shorter events, 98.3 us)
Async XLA Ops:
  7.2 23.8 %copy-start = (bf16[64,6,512]{2,0,1:T(8,128)(2,1)S(1)}, bf16[64,6,512]{2,0,1:T(8,128)(2,1)}, u32[]{:S(2)}) copy-start(bf16[64,6,512]{2,0,1:T(8,128)(2,1)} %param.25) | copy-start | bytes 1179652
  7.2 257.9 %all-reduce.5.cloned.1.call-start = ((), (), s32[]{:S(2)}) async-start(), calls=%async_computation | async-start | bytes 393216
  73.7 3.7 copy-start.26
  250.8 11.7 %copy-start.24 = (bf16[2,4,2,128,256]{4,3,2,1,0:T(8,128)(2,1)S(1)}, bf16[2,4,2,128,256]{4,3,2,1,0:T(8,128)(2,1)}, u32[]{:S(2)}) copy-start(bf16[2,4,2,128,256]{4,3,2,1,0:T(8,128)(2,1)} %get-tuple-element.111) | copy-start | bytes 3145732
  250.8 93.5 %copy-start.3 = (bf16[2,512,1024]{2,1,0:T(8,128)(2,1)S(1)}, bf16[2,512,1024]{2,1,0:T(8,128)(2,1)}, u32[]{:S(2)}) copy-start(bf16[2,512,1024]{2,1,0:T(8,128)(2,1)} %get-tuple-element.108) | copy-start | bytes 6291460
  263.8 81.3 %copy-start.55 = (f32[1,2,3,256]{3,1,2,0:T(2,128)S(1)}, f32[1,2,3,256]{3,1,2,0:T(2,128)}, u32[]{:S(2)}) copy-start(f32[1,2,3,256]{3,1,2,0:T(2,128)} %copy.146) | copy-start | bytes 18436
  265.1 80.0 %copy-start.59 = (bf16[2,4,2,128,768]{4,3,2,1,0:T(8,128)(2,1)S(1)}, bf16[2,4,2,128,768]{4,3,2,1,0:T(8,128)(2,1)}, u32[]{:S(2)}) copy-start(bf16[2,4,2,128,768]{4,3,2,1,0:T(8,128)(2,1)} %get-tuple-element.109) | copy-start | bytes 9437188
  345.1 4.0 copy-start.20
  349.7 4.3 copy-start.27
  379.7 4.1 copy-start.12
  379.7 4.1 copy-start.36
  379.7 4.2 copy-start.35
  379.7 4.3 copy-start.48
  379.8 4.9 copy-start.49
  379.8 6.3 copy-start.37
  383.8 4.5 copy-start.40
  383.8 4.5 collective-permute-start
  386.1 37.2 %copy-start.53 = (f32[2,1024]{1,0:T(2,128)}, f32[2,1024]{1,0:T(2,128)S(1)}, u32[]{:S(2)}) copy-start(f32[2,1024]{1,0:T(2,128)S(1)} %pad_maximum_fusion) | copy-start | bytes 24580
  392.3 52.4 %copy-start.2 = (f32[1024,1024]{1,0:T(8,128)}, f32[1024,1024]{1,0:T(8,128)S(1)}, u32[]{:S(2)}) copy-start(f32[1024,1024]{1,0:T(8,128)S(1)} %get-tuple-element.312) | copy-start | bytes 12582916
  392.3 3.7 copy-start.58
  396.0 7.0 copy-start.57
  422.7 12.3 %copy-start.61 = (bf16[2,1024,1024]{2,1,0:T(8,128)(2,1)S(1)}, bf16[2,1024,1024]{2,1,0:T(8,128)(2,1)}, u32[]{:S(2)}) copy-start(bf16[2,1024,1024]{2,1,0:T(8,128)(2,1)} %get-tuple-element.363) | copy-start | bytes 12582916
  422.8 19.2 %collective-permute-start.2 = (bf16[1024,1024]{1,0:T(8,128)(2,1)S(1)}, bf16[1024,1024]{1,0:T(8,128)(2,1)S(1)}, u32[]{:S(2)}, u32[]{:S(2)}) collective-permute-start(bf16[1024,1024]{1,0:T(8,128)(2,1)S(1)} %get-tuple-element.356), channel_id=1, source_target_pairs={{0,2},{2,0},{4,6},{6,4},{8,10},{10,8},{12,14},{14,12},{16,18},{18,... | collective-permute-start | bytes 6291464 | tf_op jit(solution)/shard_map/ppermute | solution.py:741
  435.0 11.6 %collective-permute-start.1 = (bf16[1024,1024]{1,0:T(8,128)(2,1)}, bf16[1024,1024]{1,0:T(8,128)(2,1)S(1)}, u32[]{:S(2)}, u32[]{:S(2)}) collective-permute-start(bf16[1024,1024]{1,0:T(8,128)(2,1)} %get-tuple-element.358), channel_id=1, source_target_pairs={{0,2},{2,0},{4,6},{6,4},{8,10},{10,8},{12,14},{14,12},{16,18},{18,... | collective-permute-start | bytes 6291464 | tf_op jit(solution)/shard_map/ppermute | solution.py:741
  454.4 4.2 copy-start.9
  456.4 4.5 copy-start.14
  502.3 7.0 copy-start.1
  540.3 7.0 copy-start.1
  567.1 5.9 copy-start.21
  572.5 181.2 %collective-permute-start.3 = (bf16[1024,1024]{1,0:T(8,128)(2,1)}, bf16[1024,1024]{1,0:T(8,128)(2,1)}, u32[]{:S(2)}, u32[]{:S(2)}) collective-permute-start(bf16[1024,1024]{1,0:T(8,128)(2,1)} %get-tuple-element.360), channel_id=1, source_target_pairs={{0,2},{2,0},{4,6},{6,4},{8,10},{10,8},{12,14},{14,12},{16,18},{18,... | collective-permute-start | bytes 6291464 | tf_op jit(solution)/shard_map/ppermute | solution.py:741
  577.7 4.8 copy-start.15
  577.7 4.8 copy-start.54
  745.6 8.1 copy-start.5
  745.6 8.1 copy-start.32
  745.6 8.1 copy-start.38
  745.6 8.1 copy-start.39
  753.7 4.4 copy-start.46
  753.7 4.3 copy-start.47
  753.8 4.3 copy-start.50
  753.8 4.3 copy-start.51
  753.8 76.8 %copy-start.43 = (f32[1,4,2,128]{3,1,2,0:T(4,128)S(1)}, f32[1,4,2,128]{3,1,2,0:T(4,128)}, u32[]{:S(2)}) copy-start(f32[1,4,2,128]{3,1,2,0:T(4,128)} %copy-done.42) | copy-start | bytes 12292
  830.6 4.2 copy-start.10
  830.6 4.7 copy-start.16
  835.3 66.0 %copy-start.30 = (f32[4096]{0:T(1024)S(1)}, f32[4096]{0:T(1024)}, u32[]{:S(2)}) copy-start(f32[4096]{0:T(1024)} %copy-done.29) | copy-start | bytes 49156
  835.3 66.0 %copy-start.33 = (f32[32,32]{1,0:T(8,128)S(1)}, f32[32,32]{1,0:T(8,128)}, u32[]{:S(2)}) copy-start(f32[32,32]{1,0:T(8,128)} %reshape.493) | copy-start | bytes 12292
  835.3 66.0 %copy-start.34 = (f32[32,32]{1,0:T(8,128)S(1)}, f32[32,32]{1,0:T(8,128)}, u32[]{:S(2)}) copy-start(f32[32,32]{1,0:T(8,128)} %reshape.491) | copy-start | bytes 12292
  938.6 73.9 %copy-start.52 = (bf16[1,1024]{1,0:T(2,128)(2,1)S(1)}, bf16[1,1024]{1,0:T(2,128)(2,1)}, u32[]{:S(2)}) copy-start(bf16[1,1024]{1,0:T(2,128)(2,1)} %param.19) | copy-start | bytes 6148
  938.7 75.1 %copy-start.25 = (bf16[512,1024]{1,0:T(8,128)(2,1)S(1)}, bf16[512,1024]{1,0:T(8,128)(2,1)}, u32[]{:S(2)}) copy-start(bf16[512,1024]{1,0:T(8,128)(2,1)} %get-tuple-element.119) | copy-start | bytes 3145732
  (24 other events, 49.7 us)
Sparse Core Ops, SparseCore 0:
  32.0 109.1 all-reduce.4

commit v2 on v0

--- a/solution.py
+++ b/solution.py
@@ -1,9 +1,13 @@
+import functools
 import math
 
 import jax
 import jax.numpy as jnp
 from jax import lax
+from jax.experimental import pallas as pl
+from jax.experimental.pallas import tpu as pltpu
 from jax.sharding import PartitionSpec as P
+
 
 HD = 64
 
@@ -136,7 +140,7 @@
     return stacked.astype(jnp.bfloat16)
 
 
-def on_device(
+def on_device_general(
     latents_in,
     condition,
     grad_out,
@@ -344,9 +348,1302 @@
     )
 
 
+MESH = pl.DeviceIdType.MESH
+ANY = pl.ANY
+BF = jnp.bfloat16
+F32 = jnp.float32
+MIB = 2**20
+IN_VMEM = pl.BlockSpec(memory_space=pltpu.VMEM)
+IN_ANY = pl.BlockSpec(memory_space=ANY)
+
+
+def place():
+    f, x = lax.axis_index("fsdp"), lax.axis_index("tp")
+    z, y, c = f // 4, lax.rem(f // 2, 2), lax.rem(f, 2)
+    return z, y, c, x
+
+
+def at(z, y, c, x):
+    return ((z * 2 + y) * 2 + c, x)
+
+
+def block(index, size):
+    return pl.ds(pl.multiple_of(index * size, size), size)
+
+
+def remote(src, dst, send, recv, device):
+    return pltpu.make_async_remote_copy(
+        src_ref=src, dst_ref=dst, send_sem=send, recv_sem=recv, device_id=device, device_id_type=MESH
+    )
+
+
+def greet(devices):
+    barrier = pltpu.get_barrier_semaphore()
+    for device in devices:
+        pl.semaphore_signal(barrier, inc=1, device_id=device, device_id_type=MESH)
+    pl.semaphore_wait(barrier, len(devices))
+
+
+def partners(diagonal=False):
+    z, y, c, x = place()
+    out = [at(z, y, 1 - c, x), at(z, 1 - y, c, x), at(z, y, c, 1 - x)]
+    out += [at(lax.rem(z + d, 4), y, c, x) for d in (1, 2, 3)]
+    if diagonal:
+        out.append(at(z, y, 1 - c, 1 - x))
+    return out
+
+
+class Gather:
+    def __init__(self, own, full, send, recv, local):
+        self.own, self.full, self.send, self.recv, self.local = own, full, send, recv, local
+
+    def _core(self):
+        z, y, c, x = place()
+        spot = self.full.at[x, z, y, block(c, 64)]
+        return (
+            pltpu.make_async_copy(self.own.at[c], spot, self.local),
+            remote(self.own.at[1 - c], spot, self.send.at[0], self.recv.at[0], at(z, y, 1 - c, x)),
+        )
+
+    def _z(self, d):
+        z, y, c, x = place()
+        spot = self.full.at[x, z, y]
+        return remote(spot, spot, self.send.at[d], self.recv.at[d], at(lax.rem(z + d, 4), y, c, x))
+
+    def _xy(self, k):
+        z, y, c, x = place()
+        if k == 0:
+            spot, to = self.full.at[x, pl.ds(0, 2), y], at(z, y, c, 1 - x)
+        elif k == 1:
+            spot, to = self.full.at[x, pl.ds(2, 2), y], at(z, 1 - y, c, x)
+        elif k == 2:
+            spot, to = self.full.at[:, pl.ds(0, 2), y], at(z, 1 - y, c, x)
+        else:
+            spot, to = self.full.at[x, pl.ds(2, 2)], at(z, y, c, 1 - x)
+        return remote(spot, spot, self.send.at[4 + k], self.recv.at[4 + k], to)
+
+    def start_core(self):
+        for copy in self._core():
+            copy.start()
+
+    def wait_core(self):
+        for copy in self._core():
+            copy.wait()
+
+    def start_z(self):
+        for d in (1, 2, 3):
+            self._z(d).start()
+
+    def wait_z(self):
+        for d in (1, 2, 3):
+            self._z(d).wait()
+
+    def start_xy(self):
+        self._xy(0).start()
+        self._xy(1).start()
+
+    def xy_to_last(self):
+        self._xy(0).wait()
+        self._xy(2).start()
+        self._xy(1).wait()
+        self._xy(3).start()
+
+    def finish(self):
+        self._xy(2).wait()
+        self._xy(3).wait()
+
+
+class Swap:
+    def __init__(self, own, full, send, recv, local):
+        self.own, self.full, self.send, self.recv, self.local = own, full, send, recv, local
+
+    def _far(self):
+        z, y, c, x = place()
+        return remote(self.own, self.full.at[1 - c], self.send.at[0], self.recv.at[0], at(z, y, 1 - c, 1 - x))
+
+    def _near(self):
+        z, y, c, x = place()
+        return pltpu.make_async_copy(self.own, self.full.at[c], self.local)
+
+    def _core(self):
+        z, y, c, x = place()
+        spot = self.full.at[c]
+        return remote(spot, spot, self.send.at[1], self.recv.at[1], at(z, y, 1 - c, x))
+
+    def start(self):
+        z, y, c, x = place()
+
+        @pl.when(c != x)
+        def _():
+            self._far().start()
+
+        @pl.when(c == x)
+        def _():
+            self._near().start()
+
+    def share(self):
+        z, y, c, x = place()
+
+        @pl.when(c != x)
+        def _():
+            self._far().wait()
+
+        @pl.when(c == x)
+        def _():
+            self._near().wait()
+
+        self._core().start()
+
+    def finish(self):
+        self._core().wait()
+
+
+COLS = (768, 256, 1024, 1024)
+
+
+class SmallGather:
+    def __init__(self, own, full, send, recv):
+        self.own, self.full, self.send, self.recv = own, full, send, recv
+
+    def _copy(self, k):
+        z, y, c, x = place()
+        send, recv = self.send.at[k], self.recv.at[k]
+        if k == 0:
+            return remote(self.own, self.full.at[x, z, y, c], send, recv, at(z, y, 1 - c, x))
+        if k <= 3:
+            spot = self.full.at[x, z, y]
+            return remote(spot, spot, send, recv, at(lax.rem(z + k, 4), y, c, x))
+        if k == 4:
+            spot = self.full.at[x, :, y]
+            return remote(spot, spot, send, recv, at(z, 1 - y, c, x))
+        spot = self.full.at[x]
+        return remote(spot, spot, send, recv, at(z, y, c, 1 - x))
+
+    def start(self):
+        z, y, c, x = place()
+        self.full[x, z, y, c] = self.own[...]
+        self._copy(0).start()
+
+    def step(self, done, begin):
+        for k in done:
+            self._copy(k).wait()
+        for k in begin:
+            self._copy(k).start()
+
+
+def ada_products(small_full, ada, wide, part, silu_out):
+    z, y, c, x = place()
+    wide[...] = jnp.zeros_like(wide)
+    wide[block(c, 64), :] = ada[...]
+    row = z * 2 + y
+    lhs = jnp.concatenate(
+        [small_full[x, zz, yy, cc, pl.ds(row, 1), :] for zz in range(4) for yy in range(2) for cc in range(2)], 0
+    )
+    silu_out[...] = lhs
+    lhs = lhs.astype(BF)
+    part[...] = jnp.zeros_like(part)
+    for j in range(6):
+        product = jnp.dot(lhs, wide[:, j * 512 : (j + 1) * 512], preferred_element_type=F32)
+        for b in range(16):
+            part[b // 4, b // 2 % 2, b % 2, j : j + 1, :] = product[b : b + 1, :]
+
+
+def widen(small_full, row, k, width=1024):
+    pieces = jnp.concatenate(
+        [
+            small_full[xx, zz, yy, cc, row : row + 1, :]
+            for zz in range(4)
+            for yy in range(2)
+            for cc in range(2)
+            for xx in range(2)
+        ],
+        0,
+    ).astype(BF)
+    lane = lax.broadcasted_iota(jnp.int32, (128, width), 1)
+    source = lax.broadcasted_iota(jnp.int32, (128, width), 0)
+    pick = jnp.where(source == k * 32 + lax.rem(lane, 32), 1.0, 0.0).astype(BF)
+    spread_out = jnp.dot(pieces, pick, preferred_element_type=F32)
+    device = lax.broadcasted_iota(jnp.int32, (32, width), 0)
+    lane = lax.broadcasted_iota(jnp.int32, (32, width), 1)
+    return jnp.sum(jnp.where(lane // 32 == device, spread_out, 0.0), 0, keepdims=True)
+
+
+def start_kernel(
+    lat, wq, wp, wu, wd, small, ada,
+    lat_full, gq, gp, gu, gd, vectors, up_bias, silu_out,
+    small_full, wide, part, near_c, near_y, near_z, mods, send, recv, local,
+):
+    z, y, c, x = place()
+    greet(partners(True))
+    swap = Swap(lat, lat_full, send.at[4], recv.at[4], local.at[4])
+    q, p, u, d = [
+        Gather(own, full, send.at[i], recv.at[i], local.at[i])
+        for i, (own, full) in enumerate(((wq, gq), (wp, gp), (wu, gu), (wd, gd)))
+    ]
+    little = SmallGather(small, small_full, send.at[5], recv.at[5])
+    little.start()
+    q.start_core()
+    swap.start()
+    for group in (p, u, d):
+        group.start_core()
+    q.wait_core()
+    q.start_z()
+    little.step((0,), (1, 2, 3))
+    little.step((1, 2, 3), (4,))
+    little.step((4,), (5,))
+    ada_products(small_full, ada, wide, part, silu_out)
+    first = remote(part.at[:, :, 1 - c], near_c, send.at[6, 0], recv.at[6, 0], at(z, y, 1 - c, x))
+    first.start()
+    first.wait()
+    for zz in range(4):
+        for yy in range(2):
+            near_c[zz, yy] = near_c[zz, yy] + part[zz, yy, c]
+    second = remote(near_c.at[:, 1 - y], near_y, send.at[6, 1], recv.at[6, 1], at(z, 1 - y, c, x))
+    second.start()
+    second.wait()
+    for zz in range(4):
+        near_y[zz] = near_y[zz] + near_c[zz, y]
+    thirds = []
+    for s in (1, 2, 3):
+        to = lax.rem(z + s, 4)
+        copy = remote(near_y.at[to], near_z.at[s - 1], send.at[6, 1 + s], recv.at[6, 1 + s], at(to, y, c, x))
+        copy.start()
+        thirds.append(copy)
+    for copy in thirds:
+        copy.wait()
+    near_z[3] = near_y[z] + near_z[0] + near_z[1] + near_z[2]
+    fourth = remote(near_z.at[3], mods.at[1 - c], send.at[6, 5], recv.at[6, 5], at(z, y, 1 - c, 1 - x))
+
+    @pl.when(c != x)
+    def _():
+        fourth.start()
+
+    q.wait_z()
+    q.start_xy()
+    for group in (p, u):
+        group.wait_core()
+        group.start_z()
+
+    @pl.when(c != x)
+    def _():
+        fourth.wait()
+
+    @pl.when(c == x)
+    def _():
+        mods[c] = near_z[3]
+
+    fifth = remote(mods.at[c], mods.at[c], send.at[6, 6], recv.at[6, 6], at(z, y, 1 - c, x))
+    fifth.start()
+    swap.share()
+    little.step((5,), ())
+    bias = [widen(small_full, 8, k) for k in range(4)]
+    ada_bias = [widen(small_full, 10 + j // 4, j % 4) for j in range(6)]
+    for zz in range(4):
+        for yy in range(2):
+            for cc in range(2):
+                for xx in range(2):
+                    device = ((zz * 2 + yy) * 2 + cc) * 2 + xx
+                    up_bias[:, device * 128 : (device + 1) * 128] = small_full[xx, zz, yy, cc, 9:10, :]
+    fifth.wait()
+    for j in range(6):
+        for h in range(2):
+            lanes = slice(h * 512, (h + 1) * 512)
+            vectors[j : j + 1, lanes] = mods[h, j : j + 1, :] + ada_bias[j][:, lanes]
+    for k in range(4):
+        vectors[6 + k : 7 + k, :] = bias[k]
+    q.xy_to_last()
+    swap.finish()
+    d.wait_core()
+    p.wait_z()
+    u.wait_z()
+    q.finish()
+
+
+def start(lat, wq, wp, wu, wd, small, ada):
+    outs = [jax.ShapeDtypeStruct((2, 512, 1024), BF)]
+    outs += [jax.ShapeDtypeStruct((2, 4, 2, 128, n), BF) for n in COLS]
+    outs += [jax.ShapeDtypeStruct((16, 1024), F32), jax.ShapeDtypeStruct((1, 4096), F32)]
+    outs += [jax.ShapeDtypeStruct((16, 128), F32)]
+    return pl.pallas_call(
+        start_kernel,
+        out_shape=outs,
+        in_specs=[IN_ANY] * 5 + [IN_VMEM] * 2,
+        out_specs=[IN_ANY] * 5 + [IN_VMEM] * 3,
+        scratch_shapes=[
+            pltpu.VMEM((2, 4, 2, 2, 16, 128), F32),
+            pltpu.VMEM((128, 3072), BF),
+            pltpu.VMEM((4, 2, 2, 8, 512), F32),
+            pltpu.VMEM((4, 2, 8, 512), F32),
+            pltpu.VMEM((4, 8, 512), F32),
+            pltpu.VMEM((4, 8, 512), F32),
+            pltpu.VMEM((2, 8, 512), F32),
+            pltpu.SemaphoreType.DMA((7, 8)),
+            pltpu.SemaphoreType.DMA((7, 8)),
+            pltpu.SemaphoreType.DMA((5,)),
+        ],
+        compiler_params=pltpu.CompilerParams(
+            collective_id=0, has_side_effects=True, vmem_limit_bytes=60 * MIB
+        ),
+        name="start",
+    )(lat, wq, wp, wu, wd, small, ada)
+
+
+def normalise(values):
+    centred = values - jnp.mean(values, axis=-1, keepdims=True)
+    scale = lax.rsqrt(jnp.mean(centred * centred, axis=-1, keepdims=True) + epsilon)
+    return centred * scale, scale
+
+
+def nn(a, b):
+    return jnp.dot(a, b, preferred_element_type=F32)
+
+
+def nt(a, b):
+    return lax.dot_general(a, b, (((1,), (1,)), ((), ())), preferred_element_type=F32)
+
+
+def tn(a, b):
+    return lax.dot_general(a, b, (((0,), (0,)), ((), ())), preferred_element_type=F32)
+
+
+def in_half(h):
+    return lax.broadcasted_iota(jnp.int32, (1, 128), 1) // 64 == h
+
+
+class Pair:
+    def __init__(self, mine, theirs, send, recv):
+        self.mine, self.theirs, self.send, self.recv = mine, theirs, send, recv
+
+    def _copy(self, i):
+        z, y, c, x = place()
+        rows = block(i, 256)
+        return remote(
+            self.mine.at[rows], self.theirs.at[rows], self.send.at[i], self.recv.at[i], at(z, y, 1 - c, x)
+        )
+
+    def give(self, i, partial):
+        self.mine[block(i, 256), :] = partial.astype(BF)
+        self._copy(i).start()
+
+    def take(self, i):
+        self._copy(i).wait()
+        rows = block(i, 256)
+        return self.mine[rows, :].astype(F32) + self.theirs[rows, :].astype(F32)
+
+
+def loop(count, body):
+    def step(i, carry):
+        body(i)
+        return carry
+
+    lax.fori_loop(0, count, step, 0)
+
+
+def attend_kernel(
+    lat, vectors, gq, gp_in, gu_in, gd_in, grad,
+    attn_in, packed, heads_out, lse, branch_one, middle, grad_full, gp, gu, gd,
+    wp, mine, theirs, send, recv, local,
+):
+    z, y, c, x = place()
+    greet(partners(True))
+    swap = Swap(grad, grad_full, send.at[3], recv.at[3], local.at[3])
+    p, u, d = [Gather(None, full, send.at[i], recv.at[i], local.at[i]) for i, full in enumerate((gp, gu, gd))]
+    p.start_xy()
+    u.start_xy()
+    d.start_z()
+    swap.start()
+
+    def modulated(i):
+        rows = lat[i // 2, block(lax.rem(i, 2), 256), :].astype(F32)
+        normal, _ = normalise(rows)
+        attn_in[block(i, 256), :] = (normal * (1.0 + vectors[1:2, :]) + vectors[0:1, :]).astype(BF)
+
+    loop(4, modulated)
+
+    def project(i):
+        b, rows = i // 2, block(lax.rem(i, 2), 512)
+        columns = pl.ds(pl.multiple_of(b * 512 + c * 256, 256), 256)
+        values = nn(attn_in[rows, :], gq[b])
+        packed[b, rows, 0:256] = (values[:, 0:256] + vectors[6:7, columns]).astype(BF)
+        packed[b, rows, 256:512] = values[:, 256:512].astype(BF)
+        packed[b, rows, 512:768] = (values[:, 512:768] + vectors[7:8, columns]).astype(BF)
+
+    loop(4, project)
+    p.xy_to_last()
+    lane = lax.broadcasted_iota(jnp.int32, (1, 128), 1)
+
+    def attend(i):
+        pair, rows = i // 2, block(lax.rem(i, 2), 512)
+        b, q_at = pair // 2, pl.multiple_of(lax.rem(pair, 2) * 128, 128)
+        queries = packed[b, rows, pl.ds(q_at, 128)] * BF(0.125)
+        keys = packed[b, :, pl.ds(q_at + 256, 128)]
+        values = packed[b, :, pl.ds(q_at + 512, 128)]
+        result = None
+        logs = lse[rows, :]
+        for h in range(2):
+            scores = nt(jnp.where(in_half(h), queries, jnp.zeros_like(queries)), keys)
+            largest = jnp.max(scores, -1, keepdims=True)
+            exponent = jnp.exp(scores - largest)
+            summed = jnp.sum(exponent, -1, keepdims=True)
+            mixture = nn(exponent.astype(BF), values) * (1.0 / summed)
+            result = mixture if h == 0 else jnp.where(in_half(0), result, mixture)
+            logs = jnp.where(lane == pair * 2 + h, largest + jnp.log(summed), logs)
+        heads_out[b, rows, pl.ds(q_at, 128)] = result.astype(BF)
+        lse[rows, :] = logs
+
+        @pl.when(i == 3)
+        def _():
+            u.xy_to_last()
+
+    lse[...] = jnp.zeros_like(lse)
+    loop(8, attend)
+    p.finish()
+    load = pltpu.make_async_copy(gp, wp, local.at[0])
+    load.start()
+    load.wait()
+    pair = Pair(mine, theirs, send.at[4], recv.at[4])
+
+    def out(i):
+        rows = block(i, 256)
+        partial = nt(heads_out[0, rows, :], wp[0].reshape(1024, 256))
+        pair.give(i, partial + nt(heads_out[1, rows, :], wp[1].reshape(1024, 256)))
+
+    loop(4, out)
+
+    def residual(i):
+        rows = block(i, 256)
+        branch = pair.take(i) + vectors[8:9, :]
+        branch_one[rows, :] = branch.astype(BF)
+        middle[rows, :] = lat[i // 2, block(lax.rem(i, 2), 256), :].astype(F32) + vectors[2:3, :] * branch
+
+    loop(4, residual)
+    swap.share()
+    d.wait_z()
+    u.finish()
+    swap.finish()
+
+
+def attend_pairs(lat, vectors, gq, gp, gu, gd, grad):
+    full = lambda n: jax.ShapeDtypeStruct((2, 4, 2, 128, n), BF)
+    tokens = lambda dtype: jax.ShapeDtypeStruct((1024, 1024), dtype)
+    return pl.pallas_call(
+        attend_kernel,
+        out_shape=[
+            tokens(BF),
+            jax.ShapeDtypeStruct((2, 1024, 768), BF),
+            jax.ShapeDtypeStruct((2, 1024, 256), BF),
+            jax.ShapeDtypeStruct((1024, 128), F32),
+            tokens(BF),
+            tokens(F32),
+            jax.ShapeDtypeStruct((2, 512, 1024), BF),
+            full(256),
+            full(1024),
+            full(1024),
+        ],
+        in_specs=[IN_VMEM] * 3 + [IN_ANY] * 4,
+        out_specs=[IN_VMEM] * 6 + [IN_ANY] * 4,
+        scratch_shapes=[
+            pltpu.VMEM((2, 4, 2, 128, 256), BF),
+            pltpu.VMEM((1024, 1024), BF),
+            pltpu.VMEM((1024, 1024), BF),
+            pltpu.SemaphoreType.DMA((5, 8)),
+            pltpu.SemaphoreType.DMA((5, 8)),
+            pltpu.SemaphoreType.DMA((4,)),
+        ],
+        input_output_aliases={3: 7, 4: 8, 5: 9},
+        compiler_params=pltpu.CompilerParams(
+            collective_id=1, has_side_effects=True, vmem_limit_bytes=60 * MIB
+        ),
+        name="attend",
+    )(lat, vectors, gq, gp, gu, gd, grad)
+
+
+class Scatter:
+    def __init__(self, send, recv, part=None, first_a=None, first_b=None, second=None, third=None, total=None, out=None):
+        self.part, self.first_a, self.first_b = part, first_a, first_b
+        self.second, self.third, self.total, self.out = second, third, total, out
+        self.send, self.recv = send, recv
+
+    def _copy(self, k):
+        z, y, c, x = place()
+        send, recv = self.send.at[k], self.recv.at[k]
+        if k == 0:
+            return remote(self.part.at[:, pl.ds(0, 2), 1 - y], self.first_a, send, recv, at(z, 1 - y, c, x))
+        if k == 1:
+            return remote(self.part.at[1 - x, pl.ds(2, 2)], self.first_b, send, recv, at(z, y, c, 1 - x))
+        if k == 2:
+            return remote(self.first_a.at[1 - x], self.second.at[pl.ds(0, 2)], send, recv, at(z, y, c, 1 - x))
+        if k == 3:
+            return remote(self.first_b.at[:, 1 - y], self.second.at[pl.ds(2, 2)], send, recv, at(z, 1 - y, c, x))
+        if k <= 6:
+            d = k - 3
+            to = lax.rem(z + d, 4)
+            return remote(self.second.at[to], self.third.at[d - 1], send, recv, at(to, y, c, x))
+        return remote(self.total.at[block(1 - c, 64)], self.out.at[c], send, recv, at(z, y, 1 - c, x))
+
+    def start(self):
+        self._copy(0).start()
+        self._copy(1).start()
+
+    def turn(self):
+        z, y, c, x = place()
+        self._copy(0).wait()
+
+        def add_a(i):
+            b, zz = i // 2, lax.rem(i, 2)
+            total = self.first_a[b, zz].astype(F32) + self.part[b, zz, y].astype(F32)
+            self.first_a[b, zz] = total.astype(BF)
+
+        loop(4, add_a)
+        self._copy(2).start()
+        self._copy(1).wait()
+
+        def add_b(i):
+            zz, yy = i // 2, lax.rem(i, 2)
+            total = self.first_b[zz, yy].astype(F32) + self.part[x, 2 + zz, yy].astype(F32)
+            self.first_b[zz, yy] = total.astype(BF)
+
+        loop(4, add_b)
+        self._copy(3).start()
+
+    def finish_xy(self):
+        z, y, c, x = place()
+        self._copy(2).wait()
+
+        def add_a(i):
+            self.second[i] = (self.second[i].astype(F32) + self.first_a[x, i].astype(F32)).astype(BF)
+
+        loop(2, add_a)
+        self._copy(3).wait()
+
+        def add_b(i):
+            self.second[2 + i] = (self.second[2 + i].astype(F32) + self.first_b[i, y].astype(F32)).astype(BF)
+
+        loop(2, add_b)
+
+    def start_z(self):
+        for k in (4, 5, 6):
+            self._copy(k).start()
+
+    def finish_z(self):
+        z, y, c, x = place()
+        for k in (4, 5, 6):
+            self._copy(k).wait()
+
+        def add(i):
+            rows = block(i, 64)
+            total = self.second[z, rows].astype(F32)
+            for d in range(3):
+                total = total + self.third[d, rows].astype(F32)
+            self.total[rows] = total
+
+        loop(2, add)
+        self._copy(7).start()
+        self.out[c] = self.total[block(c, 64)]
+
+    def finish(self):
+        self._copy(7).wait()
+
+
+def scatter_xy_buffers(n):
+    return [
+        pltpu.VMEM((2, 2, 128, n), BF),
+        pltpu.VMEM((2, 2, 128, n), BF),
+    ]
+
+
+def gelu_parts(v):
+    k = math.sqrt(2.0 / math.pi)
+    square = v * v
+    t = jnp.tanh(k * v * (1.0 + 0.044715 * square))
+    half = 0.5 * (1.0 + t)
+    return v * half, half + 0.5 * k * v * (1.0 - t * t) * (1.0 + 3.0 * 0.044715 * square)
+
+
+def mlp_kernel(
+    middle_in, grad, branch_one, vectors, up_bias, gu, gd_in,
+    block_out, middle_grad, g_one, up_grad, second, stats, up_sums, gd,
+    mlp_in, g_two, slope, part, first_a, first_b, wd, mine, theirs, theirs_two, send, recv, local,
+):
+    z, y, c, x = place()
+    active, hidden_grad = up_grad, slope
+    load = pltpu.make_async_copy(middle_in, middle_grad, local.at[1])
+    load.start()
+    greet(partners())
+    d = Gather(None, gd, send.at[0], recv.at[0], local.at[0])
+    down = Scatter(send.at[1], recv.at[1], part=part, first_a=first_a, first_b=first_b, second=second)
+    d.start_xy()
+    stats[...] = jnp.zeros_like(stats)
+    up_sums[...] = jnp.zeros_like(up_sums)
+    load.wait()
+
+    def enter(i):
+        rows = block(i, 128)
+        normal, _ = normalise(middle_grad[rows, :])
+        mlp_in[rows, :] = (normal * (1.0 + vectors[4:5, :]) + vectors[3:4, :]).astype(BF)
+        g = (grad[i // 4, block(lax.rem(i, 4), 128), :].astype(F32) * vectors[5:6, :]).astype(BF)
+        g_two[rows, :] = g
+        mine_too = jnp.where(i // 4 == c, 1.0, 0.0)
+        stats[1:2, :] += jnp.sum(g.astype(F32), 0, keepdims=True) * mine_too
+
+    loop(8, enter)
+
+    def ascend(i):
+        b, quarter = i // 4, lax.rem(i, 4)
+        rows = block(quarter, 256)
+        columns = pl.ds(pl.multiple_of(b * 2048 + c * 1024, 1024), 1024)
+        value, gradient = gelu_parts(nn(mlp_in[rows, :], gu[b]) + up_bias[:, columns])
+        active[b, quarter] = value.astype(BF).reshape(2, 128, 1024)
+        slope[b, rows, :] = gradient.astype(BF)
+
+    loop(8, ascend)
+    d.xy_to_last()
+
+    def down_gradient(i):
+        b, zz = i // 2, lax.rem(i, 2)
+        value = tn(g_two[:, block(zz, 512)], active[b].reshape(1024, 1024))
+        part[b, pl.ds(zz * 2, 2)] = value.astype(BF).reshape(2, 2, 128, 1024)
+
+    loop(4, down_gradient)
+    down.start()
+    d.finish()
+    load = pltpu.make_async_copy(gd, wd, local.at[0])
+    load.start()
+    load.wait()
+    pair = Pair(mine, theirs, send.at[2], recv.at[2])
+
+    def descend(i):
+        partial = nt(active[0, i].reshape(256, 1024), wd[0].reshape(1024, 1024))
+        pair.give(i, partial + nt(active[1, i].reshape(256, 1024), wd[1].reshape(1024, 1024)))
+
+    loop(4, descend)
+
+    def hidden_gradient(i):
+        b, rows = i // 4, block(lax.rem(i, 4), 256)
+        value = nn(g_two[rows, :], wd[b].reshape(1024, 1024)) * slope[b, rows, :].astype(F32)
+        value = value.astype(BF)
+        hidden_grad[b, rows, :] = value
+        up_sums[b] += jnp.sum(value.astype(F32), 0, keepdims=True)
+
+    loop(8, hidden_gradient)
+
+    def leave(i):
+        rows = block(i, 256)
+        g = grad[i // 2, block(lax.rem(i, 2), 256), :].astype(F32)
+        branch_two = pair.take(i) + vectors[9:10, :]
+        block_out[rows, :] = (middle_grad[rows, :] + vectors[5:6, :] * branch_two).astype(BF)
+        stats[0:1, :] += jnp.sum(g * branch_two, 0, keepdims=True)
+
+    loop(4, leave)
+    back = Pair(mine, theirs_two, send.at[3], recv.at[3])
+
+    def descend_back(i):
+        rows = block(i, 256)
+        back.give(i, nt(hidden_grad[0, rows, :], gu[0]) + nt(hidden_grad[1, rows, :], gu[1]))
+
+    loop(4, descend_back)
+    down.turn()
+
+    def up_gradient(i):
+        b, zz = i // 2, lax.rem(i, 2)
+        value = tn(mlp_in[:, block(zz, 512)], hidden_grad[b])
+        up_grad[b, pl.ds(zz * 2, 2)] = value.astype(BF).reshape(2, 2, 128, 1024)
+
+    loop(4, up_gradient)
+
+    def residual(i):
+        rows = block(i, 256)
+        dy = back.take(i)
+        normal, scale = normalise(middle_grad[rows, :])
+        stats[2:3, :] += jnp.sum(dy, 0, keepdims=True)
+        stats[3:4, :] += jnp.sum(dy * normal, 0, keepdims=True)
+        dn = dy * (1.0 + vectors[4:5, :])
+        dn = dn - jnp.mean(dn, -1, keepdims=True) - normal * jnp.mean(dn * normal, -1, keepdims=True)
+        total = grad[i // 2, block(lax.rem(i, 2), 256), :].astype(F32) + scale * dn
+        middle_grad[rows, :] = total
+        stats[4:5, :] += jnp.sum(total * branch_one[rows, :].astype(F32), 0, keepdims=True)
+        g = (total * vectors[2:3, :]).astype(BF)
+        g_one[rows, :] = g
+        mine_too = jnp.where(i // 2 == c, 1.0, 0.0)
+        stats[5:6, :] += jnp.sum(g.astype(F32), 0, keepdims=True) * mine_too
+
+    loop(4, residual)
+    down.finish_xy()
+
+
+def mlp(middle, grad, branch_one, vectors, up_bias, gu, gd):
+    full = jax.ShapeDtypeStruct((2, 4, 2, 128, 1024), BF)
+    tokens = lambda dtype: jax.ShapeDtypeStruct((1024, 1024), dtype)
+    wide = pltpu.VMEM((1024, 1024), BF)
+    return pl.pallas_call(
+        mlp_kernel,
+        out_shape=[
+            tokens(BF),
+            tokens(F32),
+            tokens(BF),
+            full,
+            jax.ShapeDtypeStruct((4, 128, 1024), BF),
+            jax.ShapeDtypeStruct((8, 1024), F32),
+            jax.ShapeDtypeStruct((2, 1, 1024), F32),
+            full,
+        ],
+        in_specs=[IN_ANY] + [IN_VMEM] * 5 + [IN_ANY],
+        out_specs=[IN_VMEM] * 7 + [IN_ANY],
+        scratch_shapes=[
+            wide,
+            wide,
+            pltpu.VMEM((2, 1024, 1024), BF),
+            pltpu.VMEM((2, 4, 2, 128, 1024), BF),
+            *scatter_xy_buffers(1024),
+            pltpu.VMEM((2, 4, 2, 128, 1024), BF),
+            wide,
+            wide,
+            wide,
+            pltpu.SemaphoreType.DMA((4, 8)),
+            pltpu.SemaphoreType.DMA((4, 8)),
+            pltpu.SemaphoreType.DMA((2,)),
+        ],
+        input_output_aliases={6: 7},
+        compiler_params=pltpu.CompilerParams(
+            collective_id=2, has_side_effects=True, vmem_limit_bytes=62 * MIB
+        ),
+        name="mlp",
+    )(middle, grad, branch_one, vectors, up_bias, gu, gd)
+
+
+def back_kernel(
+    lat, vectors, g_one, gp, gq, attn_in, packed_in, heads_out, lse, middle_grad_in, up_in, down_second, block_in,
+    input_grad, qkv_grad, proj_grad, up_second, down_out, stats, sums, block_out,
+    heads_grad, packed, packed_grad, delta, key_total, value_total, part, first_a, first_b, third, total_rows,
+    mine, theirs, middle_grad, send, recv, local,
+):
+    z, y, c, x = place()
+    loads = [
+        pltpu.make_async_copy(source, target, local.at[i])
+        for i, (source, target) in enumerate(((up_in, part), (packed_in, packed), (middle_grad_in, middle_grad)))
+    ]
+    for load in loads:
+        load.start()
+    greet(partners(True))
+    up = Scatter(send.at[0], recv.at[0], part=part, first_a=first_a, first_b=first_b, second=up_second)
+    down = Scatter(send.at[1], recv.at[1], second=down_second, third=third, total=total_rows, out=down_out)
+    loads[0].wait()
+    up.start()
+    down.start_z()
+    swap = SwapBack(block_in, block_out, send.at[3, 0], recv.at[3, 0], local.at[3])
+    swap.start()
+    loads[1].wait()
+    sums[...] = jnp.zeros_like(sums)
+    stats[...] = jnp.zeros_like(stats)
+    lane = lax.broadcasted_iota(jnp.int32, (1, 128), 1)
+
+    def enter(i):
+        b, rows = i // 2, block(lax.rem(i, 2), 512)
+        value = nn(g_one[rows, :], gp[b]).astype(BF)
+        heads_grad[b, rows, :] = value
+        products = value.astype(F32) * heads_out[b, rows, :].astype(F32)
+        found = delta[rows, :]
+        for h in range(4):
+            wide = products[:, h // 2 * 128 : h // 2 * 128 + 128]
+            total = jnp.sum(jnp.where(in_half(h % 2), wide, 0.0), -1, keepdims=True)
+            found = jnp.where(lane == b * 4 + h, total, found)
+        delta[rows, :] = found
+
+    delta[...] = jnp.zeros_like(delta)
+    loop(4, enter)
+
+    def proj_gradient(i):
+        b, half = i // 2, lax.rem(i, 2)
+        value = tn(g_one[:, block(half, 512)], heads_out[b])
+        proj_grad[b, pl.ds(half * 2, 2)] = value.astype(BF).reshape(2, 2, 128, 256)
+
+    loop(4, proj_gradient)
+
+    def attend(i):
+        pair, quarter = i // 4, lax.rem(i, 4)
+        rows = block(quarter, 256)
+        b, at_lane = pair // 2, pl.multiple_of(lax.rem(pair, 2) * 128, 128)
+        queries = packed[b, rows, pl.ds(at_lane, 128)] * BF(0.125)
+        keys = packed[b, :, pl.ds(at_lane + 256, 128)]
+        values = packed[b, :, pl.ds(at_lane + 512, 128)]
+        grads = heads_grad[b, rows, pl.ds(at_lane, 128)]
+
+        @pl.when(quarter == 0)
+        def _():
+            key_total[...] = jnp.zeros_like(key_total)
+            value_total[...] = jnp.zeros_like(value_total)
+
+        result = None
+        logs, deltas = lse[rows, :], delta[rows, :]
+        for h in range(2):
+            column = lane == pair * 2 + h
+            log = jnp.sum(jnp.where(column, logs, 0.0), -1, keepdims=True)
+            inner = jnp.sum(jnp.where(column, deltas, 0.0), -1, keepdims=True)
+            query = jnp.where(in_half(h), queries, jnp.zeros_like(queries))
+            grad = jnp.where(in_half(h), grads, jnp.zeros_like(grads))
+            probs = jnp.exp(nt(query, keys) - log)
+            score_grad = (probs * (nt(grad, values) - inner)).astype(BF)
+            query_grad = nn(score_grad, keys)
+            result = query_grad if h == 0 else jnp.where(in_half(0), result, query_grad)
+            key_total[...] += tn(score_grad, query)
+            value_total[...] += tn(probs.astype(BF), grad)
+        result = (result * 0.125).astype(BF)
+        packed_grad[b, rows, pl.ds(at_lane, 128)] = result
+        sums[b, :, pl.ds(at_lane, 128)] += jnp.sum(result.astype(F32), 0, keepdims=True)
+
+        @pl.when(quarter == 3)
+        def _():
+            packed_grad[b, :, pl.ds(at_lane + 256, 128)] = key_total[...].astype(BF)
+            total = value_total[...].astype(BF)
+            packed_grad[b, :, pl.ds(at_lane + 512, 128)] = total
+            sums[b, :, pl.ds(at_lane + 512, 128)] = jnp.sum(total.astype(F32), 0, keepdims=True)
+
+        @pl.when(i == 9)
+        def _():
+            up.turn()
+
+    loop(16, attend)
+    down.finish_z()
+    pair = Pair(mine, theirs, send.at[2], recv.at[2])
+
+    def descend(i):
+        rows = block(i, 256)
+        pair.give(i, nt(packed_grad[0, rows, :], gq[0]) + nt(packed_grad[1, rows, :], gq[1]))
+
+    loop(4, descend)
+
+    def qkv_gradient(i):
+        b, half = i // 2, lax.rem(i, 2)
+        value = tn(attn_in[:, block(half, 512)], packed_grad[b])
+        qkv_grad[b, pl.ds(half * 2, 2)] = value.astype(BF).reshape(2, 2, 128, 768)
+
+    loop(4, qkv_gradient)
+    loads[2].wait()
+
+    def leave(i):
+        rows = block(i, 256)
+        dy = pair.take(i)
+        normal, scale = normalise(lat[i // 2, block(lax.rem(i, 2), 256), :].astype(F32))
+        stats[0:1, :] += jnp.sum(dy, 0, keepdims=True)
+        stats[1:2, :] += jnp.sum(dy * normal, 0, keepdims=True)
+        dn = dy * (1.0 + vectors[1:2, :])
+        dn = dn - jnp.mean(dn, -1, keepdims=True) - normal * jnp.mean(dn * normal, -1, keepdims=True)
+        input_grad[i // 2, block(lax.rem(i, 2), 256), :] = (middle_grad[rows, :] + scale * dn).astype(BF)
+
+    loop(4, leave)
+    down.finish()
+    swap.finish()
+    up.finish_xy()
+
+
+class SwapBack:
+    def __init__(self, full, out, send, recv, local):
+        self.full, self.out, self.send, self.recv, self.local = full, out, send, recv, local
+
+    def _far(self):
+        z, y, c, x = place()
+        return remote(self.full.at[c], self.out, self.send, self.recv, at(z, y, 1 - c, 1 - x))
+
+    def _near(self):
+        z, y, c, x = place()
+        return pltpu.make_async_copy(self.full.at[c], self.out, self.local)
+
+    def _both(self, act):
+        z, y, c, x = place()
+
+        @pl.when(c != x)
+        def _():
+            act(self._far())
+
+        @pl.when(c == x)
+        def _():
+            act(self._near())
+
+    def start(self):
+        self._both(lambda copy: copy.start())
+
+    def finish(self):
+        self._both(lambda copy: copy.wait())
+
+
+def attend_back(*args):
+    wide = pltpu.VMEM((1024, 1024), BF)
+    return pl.pallas_call(
+        back_kernel,
+        out_shape=[
+            jax.ShapeDtypeStruct((2, 512, 1024), BF),
+            jax.ShapeDtypeStruct((2, 4, 2, 128, 768), BF),
+            jax.ShapeDtypeStruct((2, 4, 2, 128, 256), BF),
+            jax.ShapeDtypeStruct((4, 128, 1024), BF),
+            jax.ShapeDtypeStruct((2, 64, 1024), F32),
+            jax.ShapeDtypeStruct((8, 1024), F32),
+            jax.ShapeDtypeStruct((2, 1, 768), F32),
+            jax.ShapeDtypeStruct((512, 1024), BF),
+        ],
+        in_specs=[IN_VMEM] * 6 + [IN_ANY] + [IN_VMEM] * 2 + [IN_ANY] * 2 + [IN_VMEM] + [IN_ANY],
+        out_specs=[IN_VMEM] * 7 + [IN_ANY],
+        scratch_shapes=[
+            pltpu.VMEM((2, 1024, 256), BF),
+            pltpu.VMEM((2, 1024, 768), BF),
+            pltpu.VMEM((2, 1024, 768), BF),
+            pltpu.VMEM((1024, 128), F32),
+            pltpu.VMEM((1024, 128), F32),
+            pltpu.VMEM((1024, 128), F32),
+            pltpu.VMEM((2, 4, 2, 128, 1024), BF),
+            *scatter_xy_buffers(1024),
+            pltpu.VMEM((3, 128, 1024), BF),
+            pltpu.VMEM((128, 1024), F32),
+            wide,
+            wide,
+            pltpu.VMEM((1024, 1024), F32),
+            pltpu.SemaphoreType.DMA((4, 8)),
+            pltpu.SemaphoreType.DMA((4, 8)),
+            pltpu.SemaphoreType.DMA((4,)),
+        ],
+        compiler_params=pltpu.CompilerParams(
+            collective_id=3, has_side_effects=True, vmem_limit_bytes=62 * MIB
+        ),
+        name="attend_back",
+    )(*args)
+
+
+class SmallScatter:
+    def __init__(self, part, near_c, near_x, near_y, near_z, send, recv):
+        self.part, self.near_c, self.near_x, self.near_y, self.near_z = part, near_c, near_x, near_y, near_z
+        self.send, self.recv = send, recv
+
+    def _copy(self, k):
+        z, y, c, x = place()
+        send, recv = self.send.at[k], self.recv.at[k]
+        if k == 0:
+            return remote(self.part.at[1 - c], self.near_c, send, recv, at(z, y, 1 - c, x))
+        if k == 1:
+            return remote(self.near_c.at[1 - x], self.near_x, send, recv, at(z, y, c, 1 - x))
+        if k == 2:
+            return remote(self.near_x.at[1 - y], self.near_y, send, recv, at(z, 1 - y, c, x))
+        d = k - 2
+        to = lax.rem(z + d, 4)
+        return remote(self.near_y.at[to], self.near_z.at[d - 1], send, recv, at(to, y, c, x))
+
+    def start(self):
+        self._copy(0).start()
+
+    def step(self, k):
+        z, y, c, x = place()
+        self._copy(k).wait()
+        if k == 0:
+            self.near_c[...] = self.near_c[...] + self.part[c]
+            self._copy(1).start()
+        elif k == 1:
+            self.near_x[...] = self.near_x[...] + self.near_c[x]
+            self._copy(2).start()
+        else:
+            self.near_y[...] = self.near_y[...] + self.near_x[y]
+            for j in (3, 4, 5):
+                self._copy(j).start()
+
+    def finish(self):
+        z, y, c, x = place()
+        for j in (3, 4, 5):
+            self._copy(j).wait()
+        return self.near_y[z] + self.near_z[0] + self.near_z[1] + self.near_z[2]
+
+
+def split_bf(values):
+    high = values.astype(BF)
+    return high, (values - high.astype(F32)).astype(BF)
+
+
+def exact_nn(values, chosen):
+    high, low = split_bf(values)
+    lower = (values - high.astype(F32) - low.astype(F32)).astype(BF)
+    return nn(high, chosen) + nn(low, chosen) + nn(lower, chosen)
+
+
+def narrow(vector, k):
+    device = lax.broadcasted_iota(jnp.int32, (32, 1024), 0)
+    lane = lax.broadcasted_iota(jnp.int32, (32, 1024), 1)
+    source = lax.broadcasted_iota(jnp.int32, (1024, 128), 0)
+    target = lax.broadcasted_iota(jnp.int32, (1024, 128), 1)
+    chosen = jnp.where(target == k * 32 + lax.rem(source, 32), 1.0, 0.0).astype(BF)
+    return exact_nn(jnp.where(lane // 32 == device, vector, 0.0), chosen)
+
+
+def finish_kernel(
+    stats_mlp, stats, sums, up_sums, silu, cond, ada, input_grad, qkv_grad, proj_grad, up_second,
+    input_out, q_out, p_out, u_out, ada_out, cond_out, ada_bias_out, bias_out,
+    q_a, q_b, q_second, q_third, q_total, p_a, p_b, p_second, p_third, p_total, u_third, u_total,
+    columns, bias_part, near_c, near_x, near_y, near_z, own_mods, mods, wide, tall,
+    found, other, spread_x, spread_c, spread_y, spread_z, picked, picked_other,
+    send, recv, local,
+):
+    z, y, c, x = place()
+    greet(partners(True))
+    q = Scatter(send.at[0], recv.at[0], qkv_grad, q_a, q_b, q_second, q_third, q_total, q_out)
+    p = Scatter(send.at[1], recv.at[1], proj_grad, p_a, p_b, p_second, p_third, p_total, p_out)
+    u = Scatter(send.at[2], recv.at[2], second=up_second, third=u_third, total=u_total, out=u_out)
+    swap = SwapBack(input_grad, input_out, send.at[3, 0], recv.at[3, 0], local.at[0])
+    q.start()
+    p.start()
+    u.start_z()
+    swap.start()
+    rows = (stats[0:1, :], stats[1:2, :], stats_mlp[4:5, :], stats_mlp[2:3, :], stats_mlp[3:4, :], stats_mlp[0:1, :])
+    own_mods[...] = jnp.zeros_like(own_mods)
+    for j in range(6):
+        for h in range(2):
+            own_mods[h, j : j + 1, :] = rows[j][:, h * 512 : (h + 1) * 512]
+    far = remote(own_mods.at[1 - x], mods.at[z, y, 1 - c], send.at[4, 0], recv.at[4, 0], at(z, y, 1 - c, 1 - x))
+
+    @pl.when(c != x)
+    def _():
+        far.start()
+
+    @pl.when(c == x)
+    def _():
+        mods[z, y, c] = own_mods[x]
+
+    columns[...] = jnp.zeros_like(columns)
+    bias_part[...] = jnp.zeros_like(bias_part)
+    for b in range(2):
+        spot = pl.ds(pl.multiple_of(b * 512 + c * 256, 256), 256)
+        columns[0:1, spot] = sums[b, :, 0:256]
+        columns[1:2, spot] = sums[b, :, 512:768]
+    columns[2:3, :] = stats_mlp[5:6, :]
+    columns[3:4, :] = stats_mlp[1:2, :]
+    pieces = narrow(columns[0:1, :], 0) + narrow(columns[1:2, :], 1)
+    pieces = pieces + narrow(columns[2:3, :], 2) + narrow(columns[3:4, :], 3)
+    for k in range(32):
+        bias_part[k // 2 % 2, k % 2, k // 4 % 2, k // 8, 0:1, :] = pieces[k : k + 1, :]
+    for b in range(2):
+        for i in range(8):
+            bias_part[i // 2 % 2, i % 2, i // 4, b * 2 + c, 1:2, :] = up_sums[b, :, i * 128 : (i + 1) * 128]
+    bias = SmallScatter(bias_part, near_c, near_x, near_y, near_z, send.at[5], recv.at[5])
+    bias.start()
+
+    @pl.when(c != x)
+    def _():
+        far.wait()
+
+    spot = mods.at[z, y, c]
+    core = remote(spot, spot, send.at[4, 1], recv.at[4, 1], at(z, y, 1 - c, x))
+    core.start()
+    bias.step(0)
+    core.wait()
+    spot_y = mods.at[z, y]
+    across = remote(spot_y, spot_y, send.at[4, 2], recv.at[4, 2], at(z, 1 - y, c, x))
+    across.start()
+    bias.step(1)
+    across.wait()
+    spot_z = mods.at[z]
+    along = [
+        remote(spot_z, spot_z, send.at[4, 2 + d], recv.at[4, 2 + d], at(lax.rem(z + d, 4), y, c, x)) for d in (1, 2, 3)
+    ]
+    for copy in along:
+        copy.start()
+    bias.step(2)
+    wide[...] = jnp.zeros_like(wide)
+    wide[block(c, 64), :] = ada[...]
+    silu_rows = silu[...].astype(BF)
+    for copy in along:
+        copy.wait()
+    total = jnp.zeros((16, 128), F32)
+    bias_rows = []
+    for j in range(6):
+        values = jnp.concatenate([mods[b // 4, b // 2 % 2, b % 2, j : j + 1, :] for b in range(16)], 0)
+        high, low = split_bf(values)
+        lanes = slice(j * 512, (j + 1) * 512)
+        tall[...] = tn(silu_rows, high) + tn(silu_rows, low)
+        ada_out[:, lanes] = tall[block(c, 64), :]
+        total = total + nt(high, wide[:, lanes]) + nt(low, wide[:, lanes])
+        bias_rows.append(jnp.sum(values, 0, keepdims=True))
+    found[...] = total
+    group = (lax.rem(z, 2) * 2 + y) * 2 + c
+    source = lax.broadcasted_iota(jnp.int32, (512, 128), 0)
+    target = lax.broadcasted_iota(jnp.int32, (512, 128), 1)
+    chosen = jnp.where((source == group * 64 + target) & (target < 64), 1.0, 0.0).astype(BF)
+    picked[...] = exact_nn(jnp.concatenate(bias_rows + [jnp.zeros((2, 512), F32)], 0), chosen)
+    to_x = at(z, y, c, 1 - x)
+    first = [
+        remote(found, other, send.at[6, 0], recv.at[6, 0], to_x),
+        remote(picked, picked_other, send.at[6, 1], recv.at[6, 1], to_x),
+    ]
+    for copy in first:
+        copy.start()
+    for copy in first:
+        copy.wait()
+    ada_bias_out[...] = jnp.where(z // 2 == x, picked[...], picked_other[...])
+    total = found[...] + other[...]
+    for b in range(16):
+        spread_x[b % 2, b // 2 % 2, b // 4] = total[b : b + 1, :]
+    second = remote(spread_x.at[1 - c], spread_c, send.at[6, 2], recv.at[6, 2], at(z, y, 1 - c, x))
+    second.start()
+    bias_out[...] = bias.finish()
+    second.wait()
+    spread_c[...] = spread_c[...] + spread_x[c]
+    third = remote(spread_c.at[1 - y], spread_y.at[y], send.at[6, 3], recv.at[6, 3], at(z, 1 - y, c, x))
+    third.start()
+    spread_y[y] = spread_c[y]
+    third.wait()
+    fourth = [
+        remote(
+            spread_y.at[:, lax.rem(z + d, 4)], spread_z.at[z], send.at[6, 3 + d], recv.at[6, 3 + d],
+            at(lax.rem(z + d, 4), y, c, x),
+        )
+        for d in (1, 2, 3)
+    ]
+    for copy in fourth:
+        copy.start()
+    spread_z[z] = spread_y[:, z]
+    for copy in fourth:
+        copy.wait()
+    v = cond[...]
+    gate = 1.0 / (1.0 + jnp.exp(-v))
+    row = jnp.concatenate([spread_z[b // 2, b % 2] for b in range(8)], 0)
+    cond_out[...] = row * gate * (1.0 + v * (1.0 - gate))
+    q.turn()
+    p.turn()
+    u.finish_z()
+    p.finish_xy()
+    p.start_z()
+    q.finish_xy()
+    q.start_z()
+    u.finish()
+    p.finish_z()
+    q.finish_z()
+    p.finish()
+    swap.finish()
+    q.finish()
+
+
+def scatter_rest(n):
+    return [
+        *scatter_xy_buffers(n),
+        pltpu.VMEM((4, 128, n), BF),
+        pltpu.VMEM((3, 128, n), BF),
+        pltpu.VMEM((128, n), F32),
+    ]
+
+
+def finish(*args):
+    small = lambda *shape: pltpu.VMEM(shape, F32)
+    out = lambda *shape: jax.ShapeDtypeStruct(shape, F32)
+    return pl.pallas_call(
+        finish_kernel,
+        out_shape=[
+            jax.ShapeDtypeStruct((512, 1024), BF),
+            out(2, 64, 768),
+            out(2, 64, 256),
+            out(2, 64, 1024),
+            out(64, 3072),
+            out(8, 128),
+            out(8, 128),
+            out(2, 128),
+        ],
+        in_specs=[IN_VMEM] * 7 + [IN_ANY] + [IN_VMEM] * 3,
+        out_specs=[IN_ANY] + [IN_VMEM] * 7,
+        scratch_shapes=[
+            *scatter_rest(768),
+            *scatter_rest(256),
+            pltpu.VMEM((3, 128, 1024), BF),
+            small(128, 1024),
+            small(8, 1024),
+            small(2, 2, 2, 4, 2, 128),
+            small(2, 2, 4, 2, 128),
+            small(2, 4, 2, 128),
+            small(4, 2, 128),
+            small(3, 2, 128),
+            small(2, 8, 512),
+            small(4, 2, 2, 8, 512),
+            pltpu.VMEM((128, 3072), BF),
+            small(128, 512),
+            small(16, 128),
+            small(16, 128),
+            small(2, 2, 4, 1, 128),
+            small(2, 4, 1, 128),
+            small(2, 4, 1, 128),
+            small(4, 2, 1, 128),
+            small(8, 128),
+            small(8, 128),
+            pltpu.SemaphoreType.DMA((7, 8)),
+            pltpu.SemaphoreType.DMA((7, 8)),
+            pltpu.SemaphoreType.DMA((1,)),
+        ],
+        compiler_params=pltpu.CompilerParams(
+            collective_id=4, has_side_effects=True, vmem_limit_bytes=60 * MIB
+        ),
+        name="finish",
+    )(*args)
+
+
+def on_device_pairs(
+    latents_in,
+    condition,
+    grad_out,
+    qkv_weight,
+    proj_weight,
+    up_weight,
+    down_weight,
+    ada_weight,
+    query_bias,
+    value_bias,
+    proj_bias,
+    up_bias,
+    down_bias,
+    ada_bias,
+):
+    x = lax.axis_index("tp")
+    wq = qkv_weight.reshape(64, 3, 2, 256).transpose(2, 0, 1, 3).reshape(2, 64, 768)
+    wp = proj_weight.T.reshape(64, 2, 256).transpose(1, 0, 2)
+    wu = up_weight.reshape(64, 2, 1024).transpose(1, 0, 2)
+    wd = down_weight.T.reshape(64, 2, 1024).transpose(1, 0, 2)
+    ada = ada_weight.reshape(64, 3072)
+    cond = condition.astype(F32).reshape(8, 128)
+    biases = [query_bias, value_bias, proj_bias, down_bias, up_bias, ada_bias.reshape(-1), jnp.zeros((576,), BF)]
+    small = jnp.concatenate(
+        [jax.nn.silu(cond).astype(BF).astype(F32), jnp.concatenate(biases).astype(F32).reshape(8, 128)], 0
+    )
+    lat_full, gq, gp, gu, gd, vectors, up_all, silu = start(
+        latents_in.reshape(512, 1024), wq, wp, wu, wd, small, ada
+    )
+    gq = gq.reshape(2, 1024, 768)
+    attn_in, packed, heads_out, lse, branch_one, middle, grad_full, gp, gu, gd = attend_pairs(
+        lat_full, vectors, gq, gp, gu, gd, grad_out.reshape(512, 1024)
+    )
+    gp, gu = gp.reshape(2, 1024, 256), gu.reshape(2, 1024, 1024)
+    block_out, middle_grad, g_one, up_grad, down_second, stats_mlp, up_sums, _ = mlp(
+        middle, grad_full, branch_one, vectors, up_all, gu, gd
+    )
+    input_grad, qkv_grad, proj_grad, up_second, down_out, stats, sums, block_mine = attend_back(
+        lat_full, vectors, g_one, gp, gq, attn_in, packed, heads_out, lse, middle_grad, up_grad, down_second,
+        block_out.reshape(2, 512, 1024),
+    )
+    input_mine, q_out, p_out, u_out, ada_out, cond_out, ada_bias_out, bias_out = finish(
+        stats_mlp, stats, sums, up_sums, silu, cond, ada, input_grad, qkv_grad, proj_grad, up_second
+    )
+    rows = lax.dynamic_slice_in_dim(cond_out, x * 4, 4, 0)
+    return (
+        block_mine.reshape(512, 1, 1024),
+        input_mine.astype(F32).reshape(512, 1, 1024),
+        rows.reshape(1, 512),
+        q_out.reshape(2, 64, 3, 256).transpose(1, 2, 0, 3).reshape(64, 3, 512),
+        p_out.transpose(1, 0, 2).reshape(64, 512).T,
+        u_out.transpose(1, 0, 2).reshape(64, 2048),
+        down_out.transpose(1, 0, 2).reshape(64, 2048).T,
+        ada_out.reshape(64, 6, 512),
+        bias_out[0, 0:32],
+        bias_out[0, 32:64],
+        bias_out[0, 64:96],
+        bias_out[1],
+        bias_out[0, 96:128],
+        lax.dynamic_slice_in_dim(ada_bias_out, x * 32, 32, 1)[:6],
+    )
+
+
 def solution(mesh):
+    shape = dict(mesh.shape)
+    pairs = shape["fsdp"] == 16 and shape["tp"] == 2
     return jax.shard_map(
-        on_device,
+        on_device_pairs if pairs else on_device_general,
         mesh=mesh,
         in_specs=(
             P("tp", "fsdp", None),

time: 1230 us -> 406 us (0.33)
  waiting for transfers between devices: 682 us -> 0 us
  Pallas kernels: 0 us -> 378 us
  blocking collectives: 221 us -> 0 us
  matrix products: 171 us -> 0 us
  other arithmetic: 77.1 us -> 2.81 us
  local copies, waits for them, and re-layouts: 54.4 us -> 23.3 us
  between operations: 15.4 us -> 0.79 us
    reduce_scatter x10 -> x0, waiting for transfers between devices: 390 us -> none  [the longest x1 86.8 us: on_device(): lax.psum_scatter(ada_grad.astype(jnp.bfloat16), 'fsdp', scatter_dimension...]
    pallas_call x0 -> x5, Pallas kernels: none -> 378 us  [the longest x1 96.4 us: finish(): pl.pallas_call(finish_kernel, out_shape=[jax.ShapeDtypeStruct((512, 1024)...]
    dot_general x28 -> x0, matrix products: 171 us -> none  [the longest x2 19.3 us: one_block(): jnp.einsum('qbhd,kbhd->bhqk', g_rows, value_rows, preferred_element_type=...]
    unnamed x23 -> x0, waiting for transfers between devices: 148 us -> none
    all_gather x9 -> x0, waiting for transfers between devices: 144 us -> none  [the longest x2 67 us: gather_grads(): return lax.all_gather(piece, 'tp', axis=0, tiled=True)]
    all_gather x3 -> x0, blocking collectives: 143 us -> none  [the longest x1 71.3 us: on_device(): lax.all_gather(ada_bias, ('fsdp', 'tp'), axis=1, tiled=True)]
    unnamed x2 -> x0, blocking collectives: 78.2 us -> none
    convert_element_type x15 -> x1, other arithmetic: 37.4 us -> 0.01 us  [on_device_pairs(): jax.nn.silu(cond).astype(BF).astype(F32)]
  transfers between devices with their start and end apart: 21 -> 0, of which waited for: 16 -> 0; matrix products, arithmetic and copies ran while one was open for 12% -> 0% of each run, Pallas kernels for 0% -> 0%
where the time goes in v2:
time: 406 us; the launch traced here: 404 us
  Pallas kernels  378 us (93%)
  local copies, waits for them, and re-layouts  23.3 us (6%)
    pallas_call x1, Pallas kernels, finish(): pl.pallas_call(finish_kernel, out_shape=[jax.ShapeDtypeStruct((512, 1024)...  96.4 us
    pallas_call x1, Pallas kernels, mlp(): pl.pallas_call(mlp_kernel, out_shape=[tokens(BF), tokens(F32), tokens(BF)...  83.6 us
    pallas_call x1, Pallas kernels, start(): pl.pallas_call(start_kernel, out_shape=outs, in_specs=[IN_ANY] * 5 + [IN_...  71.8 us
    pallas_call x1, Pallas kernels, attend_pairs(): pl.pallas_call(attend_kernel, out_shape=[tokens(BF), jax.ShapeDtypeStruct...  68.2 us
    pallas_call x1, Pallas kernels, attend_back(): pl.pallas_call(back_kernel, out_shape=[jax.ShapeDtypeStruct((2, 512, 1024...  57.5 us

profile of v2, /device:TPU:0, one launch (start us, length us, event | category | flops | bytes accessed | tf_op | source)
XLA Modules:
  0.0 404.5 jit_solution(1270474292395881850)
XLA Ops:
  0.6 0.0 copy-start.5
  0.7 1.9 bitcast_bitcast_fusion
  2.5 1.8 copy.62
  4.3 0.7 reshape.131
  5.0 0.0 copy-start.6
  5.0 0.8 reshape.114
  5.8 3.4 concatenate.8
  9.2 0.6 maximum_convert_fusion.small
  9.8 1.0 reshape.107
  10.8 0.2 copy.72
  11.0 0.9 reshape.108.wq
  11.9 0.0 copy-done.5
  11.9 0.6 copy.73
  12.5 71.8 %start.1 = (bf16[2,512,1024]{2,1,0:T(8,128)(2,1)}, bf16[2,4,2,128,768]{4,3,2,1,0:T(8,128)(2,1)}, bf16[2,4,2,128,256]{4,3,2,1,0:T(8,128)(2,1)}, bf16[2,4,2,128,10...) custom-call(bf16[512,1024]{1,0:T(8,128)(2,1)} %bitcast.79, ...), custom_call_target="tpu_custom_call" | custom-call | tf_op jit(solution)/shard_map/start/pallas_call | solution.py:667
  84.4 68.2 %attend.1 = (bf16[1024,1024]{1,0:T(8,128)(2,1)}, bf16[2,1024,768]{2,1,0:T(8,128)(2,1)}, bf16[2,1024,256]{2,1,0:T(8,128)(2,1)}, f32[1024,128]{1,0:T(8,128)}, bf16...) custom-call(bf16[2,512,1024]{2,1,0:T(8,128)(2,1)} %get-tuple-element, ...), custom_call_target="tpu_custom_call", output_to_operand_aliasing={{7}: (3, {}), {8}: (4, {}), {9}: (5, {})} | custom-call | tf_op jit(solution)/shard_map/attend/pallas_call | solution.py:829
  152.5 0.0 copy-done.6
  152.5 83.6 %mlp.1 = (bf16[1024,1024]{1,0:T(8,128)(2,1)}, f32[1024,1024]{1,0:T(8,128)}, bf16[1024,1024]{1,0:T(8,128)(2,1)}, bf16[2,4,2,128,1024]{4,3,2,1,0:T(8,128)(2,1)}, b...) custom-call(f32[1024,1024]{1,0:T(8,128)} %get-tuple-element.61.middl, ...), custom_call_target="tpu_custom_call", output_to_operand_aliasing={{7}: (6, {})} | custom-call | tf_op jit(solution)/shard_map/mlp/pallas_call | solution.py:1078
  236.2 57.5 %attend_back.1 = (bf16[2,512,1024]{2,1,0:T(8,128)(2,1)}, bf16[2,4,2,128,768]{4,3,2,1,0:T(8,128)(2,1)}, bf16[2,4,2,128,256]{4,3,2,1,0:T(8,128)(2,1)}, bf16[4,128,...) custom-call(bf16[2,512,1024]{2,1,0:T(8,128)(2,1)} %get-tuple-element, ...), custom_call_target="tpu_custom_call" | custom-call | tf_op jit(solution)/shard_map/attend_back/pallas_call | solution.py:1271
  293.7 96.4 %finish.1 = (bf16[512,1024]{1,0:T(8,128)(2,1)}, f32[2,64,768]{2,1,0:T(8,128)}, f32[2,64,256]{2,1,0:T(8,128)}, f32[2,64,1024]{2,1,0:T(8,128)}, f32[64,3072]{1,0:T...) custom-call(f32[8,1024]{1,0:T(8,128)} %get-tuple-element.78.stats_mlp, ...), custom_call_target="tpu_custom_call" | custom-call | tf_op jit(solution)/shard_map/finish/pallas_call | solution.py:1530
  390.1 0.0 copy-start.3
  390.2 1.5 bitcast_convert_fusion
  391.7 0.0 copy-start.1
  391.7 3.5 copy.56
  395.2 0.0 copy-start.4
  395.2 0.0 copy-start.7
  395.2 0.0 copy-start.9
  395.2 0.0 copy-start.2
  395.2 0.0 copy-done.3
  395.2 0.0 copy-start
  395.2 0.2 reshape.125
  395.4 0.3 copy.52
  395.7 1.1 reshape.126
  396.8 0.0 copy-done.1
  396.8 0.9 copy.71
  397.7 1.9 copy.64
  399.6 0.0 copy-done.4
  399.6 0.7 copy.63
  400.3 0.0 copy-done.7
  400.3 0.7 constant_dynamic-slice_fusion
  401.0 0.0 copy-done.9
  401.0 0.6 constant_dynamic-slice_fusion.1
  401.5 0.0 copy-done.8
  401.5 0.6 slice_bitcast_fusion
  402.1 0.5 slice_bitcast_fusion.1
  402.7 0.0 copy-done.2
  402.7 0.8 copy.65
  403.5 0.0 copy-done
  403.5 1.0 copy.79
  (3 shorter events, 0.0 us)
Async XLA Ops:
  0.6 11.2 %copy-start.5 = (bf16[512,64]{0,1:T(8,128)(2,1)S(1)}, bf16[512,64]{0,1:T(8,128)(2,1)}, u32[]{:S(2)}) copy-start(bf16[512,64]{0,1:T(8,128)(2,1)} %param.18) | copy-start | bytes 196612
  5.0 147.5 %copy-start.6 = (f32[1,1024]{1,0:T(1,128)}, f32[1,1024]{1,0:T(1,128)S(1)}, u32[]{:S(2)}) copy-start(f32[1,1024]{1,0:T(1,128)S(1)} %reshape.131) | copy-start | bytes 12292
  390.1 5.0 %copy-start.3 = (f32[2,64,768]{2,1,0:T(8,128)S(1)}, f32[2,64,768]{2,1,0:T(8,128)}, u32[]{:S(2)}) copy-start(f32[2,64,768]{2,1,0:T(8,128)} %get-tuple-element.89) | copy-start | bytes 1179652
  391.7 5.1 %copy-start.1 = (f32[64,3072]{1,0:T(8,128)S(1)}, f32[64,3072]{1,0:T(8,128)}, u32[]{:S(2)}) copy-start(f32[64,3072]{1,0:T(8,128)} %get-tuple-element.93) | copy-start | bytes 2359300
  395.2 4.5 %copy-start.4 = (f32[2,64,256]{2,1,0:T(8,128)S(1)}, f32[2,64,256]{2,1,0:T(8,128)}, u32[]{:S(2)}) copy-start(f32[2,64,256]{2,1,0:T(8,128)} %get-tuple-element.90) | copy-start | bytes 393220
  395.2 5.1 %copy-start.7 = (f32[8,128]{1,0:T(8,128)S(1)}, f32[8,128]{1,0:T(8,128)}, u32[]{:S(2)}) copy-start(f32[8,128]{1,0:T(8,128)} %get-tuple-element.95) | copy-start | bytes 12292
  395.2 5.8 %copy-start.9 = (f32[8,128]{1,0:T(8,128)S(1)}, f32[8,128]{1,0:T(8,128)}, u32[]{:S(2)}) copy-start(f32[8,128]{1,0:T(8,128)} %get-tuple-element.88) | copy-start | bytes 12292
  395.2 6.4 %copy-start.8 = (f32[2,128]{1,0:T(2,128)S(1)}, f32[2,128]{1,0:T(2,128)}, u32[]{:S(2)}) copy-start(f32[2,128]{1,0:T(2,128)} %get-tuple-element.94) | copy-start | bytes 3076
  395.2 7.5 %copy-start.2 = (f32[2,64,1024]{2,1,0:T(8,128)S(1)}, f32[2,64,1024]{2,1,0:T(8,128)}, u32[]{:S(2)}) copy-start(f32[2,64,1024]{2,1,0:T(8,128)} %get-tuple-element.92) | copy-start | bytes 1572868
  395.2 8.3 %copy-start = (bf16[512,1024]{1,0:T(8,128)(2,1)S(1)}, bf16[512,1024]{1,0:T(8,128)(2,1)}, u32[]{:S(2)}) copy-start(bf16[512,1024]{1,0:T(8,128)(2,1)} %get-tuple-element.77) | copy-start | bytes 3145732

commit v3 on v0

--- a/solution.py
+++ b/solution.py
@@ -1,9 +1,13 @@
+import functools
 import math
 
 import jax
 import jax.numpy as jnp
 from jax import lax
+from jax.experimental import pallas as pl
+from jax.experimental.pallas import tpu as pltpu
 from jax.sharding import PartitionSpec as P
+
 
 HD = 64
 
@@ -136,7 +140,7 @@
     return stacked.astype(jnp.bfloat16)
 
 
-def on_device(
+def on_device_general(
     latents_in,
     condition,
     grad_out,
@@ -344,9 +348,1145 @@
     )
 
 
+MESH = pl.DeviceIdType.MESH
+ANY = pl.ANY
+BF = jnp.bfloat16
+F32 = jnp.float32
+MIB = 2**20
+IN_VMEM = pl.BlockSpec(memory_space=pltpu.VMEM)
+IN_ANY = pl.BlockSpec(memory_space=ANY)
+SPLIT = 80
+
+
+def place():
+    f, x = lax.axis_index("fsdp"), lax.axis_index("tp")
+    z, y, c = f // 4, lax.rem(f // 2, 2), lax.rem(f, 2)
+    return z, y, c, x
+
+
+def at(z, y, c, x):
+    return ((z * 2 + y) * 2 + c, x)
+
+
+def block(index, size):
+    return pl.ds(pl.multiple_of(index * size, size), size)
+
+
+def remote(src, dst, send, recv, device):
+    return pltpu.make_async_remote_copy(
+        src_ref=src, dst_ref=dst, send_sem=send, recv_sem=recv, device_id=device, device_id_type=MESH
+    )
+
+
+def loop(count, body):
+    def step(i, carry):
+        body(i)
+        return carry
+
+    lax.fori_loop(0, count, step, 0)
+
+
+def greet(devices):
+    barrier = pltpu.get_barrier_semaphore()
+    for device in devices:
+        pl.semaphore_signal(barrier, inc=1, device_id=device, device_id_type=MESH)
+    pl.semaphore_wait(barrier, len(devices))
+
+
+def partners():
+    z, y, c, x = place()
+    out = [at(z, y, 1 - c, x), at(z, 1 - y, c, x), at(z, y, c, 1 - x), at(z, y, 1 - c, 1 - x)]
+    return out + [at(lax.rem(z + d, 4), y, c, x) for d in (1, 2, 3)]
+
+
+class Gather:
+    def __init__(self, own, full, lanes, send, recv, local):
+        self.own, self.full, self.lanes = own, full, pl.ds(*lanes)
+        self.send, self.recv, self.local = send, recv, local
+
+    def _core(self):
+        z, y, c, x = place()
+        copies = []
+        for i, ((near, first, width), (far, _, _)) in enumerate(zip(self.own(c), self.own(1 - c))):
+            spot = self.full.at[x, z, y, block(c, 64), pl.ds(first, width)]
+            copies.append(pltpu.make_async_copy(near, spot, self.local.at[i]))
+            copies.append(remote(far, spot, self.send.at[i], self.recv.at[i], at(z, y, 1 - c, x)))
+        return copies
+
+    def _copy(self, kind, d):
+        z, y, c, x = place()
+        a, b, from_z = pl.ds(0, SPLIT), pl.ds(SPLIT, 128 - SPLIT), lax.rem(z - d + 4, 4)
+        if kind == 0:
+            spot, to = self.full.at[x, z, y, :, self.lanes], at(lax.rem(z + d, 4), y, c, x)
+        elif kind == 1:
+            spot, to = self.full.at[x, from_z, y, a, self.lanes], at(z, y, c, 1 - x)
+        elif kind == 2:
+            spot, to = self.full.at[x, from_z, y, b, self.lanes], at(z, 1 - y, c, x)
+        elif kind == 3:
+            spot, to = self.full.at[:, from_z, y, a, self.lanes], at(z, 1 - y, c, x)
+        else:
+            spot, to = self.full.at[x, from_z, :, b, self.lanes], at(z, y, c, 1 - x)
+        return remote(spot, spot, self.send.at[4 + 4 * kind + d], self.recv.at[4 + 4 * kind + d], to)
+
+    def start_core(self):
+        for copy in self._core():
+            copy.start()
+
+    def enter(self):
+        for copy in self._core():
+            copy.wait()
+        for d in (2, 1, 3):
+            self._copy(0, d).start()
+        self._copy(1, 0).start()
+        self._copy(2, 0).start()
+
+    def arrived(self, d):
+        self._copy(0, d).wait()
+        self._copy(1, d).start()
+        self._copy(2, d).start()
+
+    def turn(self, d):
+        self._copy(1, d).wait()
+        self._copy(3, d).start()
+        self._copy(2, d).wait()
+        self._copy(4, d).start()
+
+    def finish(self):
+        for d in range(4):
+            self._copy(3, d).wait()
+            self._copy(4, d).wait()
+
+
+class Scatter:
+    def __init__(self, part, first_a, first_b, second, third, total, out, send, recv):
+        self.part, self.first_a, self.first_b = part, first_a, first_b
+        self.second, self.third, self.total, self.out = second, third, total, out
+        self.send, self.recv = send, recv
+
+    def _copy(self, kind, d):
+        z, y, c, x = place()
+        a, b, to_z = pl.ds(0, SPLIT), pl.ds(SPLIT, 128 - SPLIT), lax.rem(z + d, 4)
+        send, recv = self.send.at[4 * kind + d], self.recv.at[4 * kind + d]
+        to_x, to_y = at(z, y, c, 1 - x), at(z, 1 - y, c, x)
+        if kind == 0:
+            return remote(self.part.at[:, to_z, 1 - y, a], self.first_a.at[to_z], send, recv, to_y)
+        if kind == 1:
+            return remote(self.part.at[1 - x, to_z, :, b], self.first_b.at[to_z], send, recv, to_x)
+        if kind == 2:
+            return remote(self.first_a.at[to_z, 1 - x], self.second.at[to_z, a], send, recv, to_x)
+        if kind == 3:
+            return remote(self.first_b.at[to_z, 1 - y], self.second.at[to_z, b], send, recv, to_y)
+        return remote(self.second.at[to_z], self.third.at[d - 1], send, recv, at(to_z, y, c, x))
+
+    def _core(self):
+        z, y, c, x = place()
+        copies = []
+        for i, (target, first, width) in enumerate(self.out(c)):
+            lanes = pl.ds(first, width)
+            copies.append(
+                remote(
+                    self.total.at[block(1 - c, 64), lanes], target, self.send.at[20 + i], self.recv.at[20 + i],
+                    at(z, y, 1 - c, x),
+                )
+            )
+            copies.append(pltpu.make_async_copy(self.total.at[block(c, 64), lanes], target, self.send.at[24 + i]))
+        return copies
+
+    def start(self):
+        for d in (2, 1, 3, 0):
+            self._copy(0, d).start()
+            self._copy(1, d).start()
+
+    def turn(self, d):
+        z, y, c, x = place()
+        to_z = lax.rem(z + d, 4)
+        a, b = pl.ds(0, SPLIT), pl.ds(SPLIT, 128 - SPLIT)
+        self._copy(0, d).wait()
+        for k in range(2):
+            total = self.first_a[to_z, k].astype(F32) + self.part[k, to_z, y, a].astype(F32)
+            self.first_a[to_z, k] = total.astype(BF)
+        self._copy(2, d).start()
+        self._copy(1, d).wait()
+        for k in range(2):
+            total = self.first_b[to_z, k].astype(F32) + self.part[x, to_z, k, b].astype(F32)
+            self.first_b[to_z, k] = total.astype(BF)
+        self._copy(3, d).start()
+
+    def leave(self, d):
+        z, y, c, x = place()
+        to_z = lax.rem(z + d, 4)
+        a, b = pl.ds(0, SPLIT), pl.ds(SPLIT, 128 - SPLIT)
+        self._copy(2, d).wait()
+        self.second[to_z, a] = (self.second[to_z, a].astype(F32) + self.first_a[to_z, x].astype(F32)).astype(BF)
+        self._copy(3, d).wait()
+        self.second[to_z, b] = (self.second[to_z, b].astype(F32) + self.first_b[to_z, y].astype(F32)).astype(BF)
+        if d:
+            self._copy(4, d).start()
+
+    def last(self):
+        z, y, c, x = place()
+        for d in (1, 2, 3):
+            self._copy(4, d).wait()
+
+        def add(i):
+            rows = block(i, 64)
+            total = self.second[z, rows].astype(F32)
+            for d in range(3):
+                total = total + self.third[d, rows].astype(F32)
+            self.total[rows] = total
+
+        loop(2, add)
+        for copy in self._core():
+            copy.start()
+
+    def finish(self):
+        for copy in self._core():
+            copy.wait()
+
+
+class Swap:
+    def __init__(self, own, full, send, recv, local):
+        self.own, self.full, self.send, self.recv, self.local = own, full, send, recv, local
+
+    def _both(self, act):
+        z, y, c, x = place()
+
+        @pl.when(c != x)
+        def _():
+            to = at(z, y, 1 - c, 1 - x)
+            act(remote(self.own, self.full.at[block(1 - c, 512)], self.send.at[0], self.recv.at[0], to))
+
+        @pl.when(c == x)
+        def _():
+            act(pltpu.make_async_copy(self.own, self.full.at[block(c, 512)], self.local))
+
+    def _core(self):
+        z, y, c, x = place()
+        spot = self.full.at[block(c, 512)]
+        return remote(spot, spot, self.send.at[1], self.recv.at[1], at(z, y, 1 - c, x))
+
+    def start(self):
+        self._both(lambda copy: copy.start())
+
+    def share(self):
+        self._both(lambda copy: copy.wait())
+        self._core().start()
+
+    def finish(self):
+        self._core().wait()
+
+
+class SwapBack:
+    def __init__(self, full, out, send, recv, local):
+        self.full, self.out, self.send, self.recv, self.local = full, out, send, recv, local
+
+    def _both(self, act):
+        z, y, c, x = place()
+        rows = self.full.at[block(c, 512)]
+
+        @pl.when(c != x)
+        def _():
+            act(remote(rows, self.out, self.send, self.recv, at(z, y, 1 - c, 1 - x)))
+
+        @pl.when(c == x)
+        def _():
+            act(pltpu.make_async_copy(rows, self.out, self.local))
+
+    def start(self):
+        self._both(lambda copy: copy.start())
+
+    def finish(self):
+        self._both(lambda copy: copy.wait())
+
+
+class SmallGather:
+    def __init__(self, own, full, send, recv):
+        self.own, self.full, self.send, self.recv = own, full, send, recv
+
+    def _copy(self, k):
+        z, y, c, x = place()
+        send, recv = self.send.at[k], self.recv.at[k]
+        if k == 0:
+            return remote(self.own, self.full.at[x, z, y, c], send, recv, at(z, y, 1 - c, x))
+        if k <= 3:
+            spot = self.full.at[x, z, y]
+            return remote(spot, spot, send, recv, at(lax.rem(z + k, 4), y, c, x))
+        if k == 4:
+            spot = self.full.at[x, :, y]
+            return remote(spot, spot, send, recv, at(z, 1 - y, c, x))
+        spot = self.full.at[x]
+        return remote(spot, spot, send, recv, at(z, y, c, 1 - x))
+
+    def start(self):
+        z, y, c, x = place()
+        self.full[x, z, y, c] = self.own[...]
+        self._copy(0).start()
+
+    def step(self, done, begin):
+        for k in done:
+            self._copy(k).wait()
+        for k in begin:
+            self._copy(k).start()
+
+
+class SmallScatter:
+    def __init__(self, part, near_c, near_x, near_y, near_z, send, recv):
+        self.part, self.near_c, self.near_x, self.near_y, self.near_z = part, near_c, near_x, near_y, near_z
+        self.send, self.recv = send, recv
+
+    def _copy(self, k):
+        z, y, c, x = place()
+        send, recv = self.send.at[k], self.recv.at[k]
+        if k == 0:
+            return remote(self.part.at[1 - c], self.near_c, send, recv, at(z, y, 1 - c, x))
+        if k == 1:
+            return remote(self.near_c.at[1 - x], self.near_x, send, recv, at(z, y, c, 1 - x))
+        if k == 2:
+            return remote(self.near_x.at[1 - y], self.near_y, send, recv, at(z, 1 - y, c, x))
+        to = lax.rem(z + k - 2, 4)
+        return remote(self.near_y.at[to], self.near_z.at[k - 3], send, recv, at(to, y, c, x))
+
+    def start(self):
+        self._copy(0).start()
+
+    def step(self, k):
+        z, y, c, x = place()
+        self._copy(k).wait()
+        if k == 0:
+            self.near_c[...] = self.near_c[...] + self.part[c]
+            self._copy(1).start()
+        elif k == 1:
+            self.near_x[...] = self.near_x[...] + self.near_c[x]
+            self._copy(2).start()
+        else:
+            self.near_y[...] = self.near_y[...] + self.near_x[y]
+            for j in (3, 4, 5):
+                self._copy(j).start()
+
+    def finish(self):
+        z, y, c, x = place()
+        for j in (3, 4, 5):
+            self._copy(j).wait()
+        return self.near_y[z] + self.near_z[0] + self.near_z[1] + self.near_z[2]
+
+
+class Pair:
+    def __init__(self, mine, theirs, send, recv):
+        self.mine, self.theirs, self.send, self.recv = mine, theirs, send, recv
+
+    def _copy(self, i):
+        z, y, c, x = place()
+        rows = block(i, 256)
+        return remote(
+            self.mine.at[rows], self.theirs.at[rows], self.send.at[i], self.recv.at[i], at(z, y, 1 - c, x)
+        )
+
+    def give(self, i, partial):
+        self.mine[block(i, 256), :] = partial.astype(BF)
+        self._copy(i).start()
+
+    def take(self, i):
+        self._copy(i).wait()
+        rows = block(i, 256)
+        return self.mine[rows, :].astype(F32) + self.theirs[rows, :].astype(F32)
+
+
+def normalise(values):
+    centred = values - jnp.mean(values, axis=-1, keepdims=True)
+    scale = lax.rsqrt(jnp.mean(centred * centred, axis=-1, keepdims=True) + epsilon)
+    return centred * scale, scale
+
+
+def nn(a, b):
+    return jnp.dot(a, b, preferred_element_type=F32)
+
+
+def nt(a, b):
+    return lax.dot_general(a, b, (((1,), (1,)), ((), ())), preferred_element_type=F32)
+
+
+def tn(a, b):
+    return lax.dot_general(a, b, (((0,), (0,)), ((), ())), preferred_element_type=F32)
+
+
+def in_half(h):
+    return lax.broadcasted_iota(jnp.int32, (1, 128), 1) // 64 == h
+
+
+def column_sum(values):
+    return jnp.sum(values, 0, keepdims=True)
+
+
+def gelu_parts(v):
+    k = math.sqrt(2.0 / math.pi)
+    square = v * v
+    t = jnp.tanh(k * v * (1.0 + 0.044715 * square))
+    half = 0.5 * (1.0 + t)
+    return v * half, half + 0.5 * k * v * (1.0 - t * t) * (1.0 + 3.0 * 0.044715 * square)
+
+
+def split_bf(values):
+    high = values.astype(BF)
+    return high, (values - high.astype(F32)).astype(BF)
+
+
+def exact_nn(values, chosen):
+    high, low = split_bf(values)
+    lower = (values - high.astype(F32) - low.astype(F32)).astype(BF)
+    return nn(high, chosen) + nn(low, chosen) + nn(lower, chosen)
+
+
+def devices():
+    return [(zz, yy, cc, xx) for zz in range(4) for yy in range(2) for cc in range(2) for xx in range(2)]
+
+
+def widen(small_full, row, k, width=1024):
+    pieces = jnp.concatenate([small_full[xx, zz, yy, cc, row : row + 1, :] for zz, yy, cc, xx in devices()], 0)
+    lane = lax.broadcasted_iota(jnp.int32, (128, width), 1)
+    source = lax.broadcasted_iota(jnp.int32, (128, width), 0)
+    pick = jnp.where(source == k * 32 + lax.rem(lane, 32), 1.0, 0.0).astype(BF)
+    spread_out = nn(pieces.astype(BF), pick)
+    device = lax.broadcasted_iota(jnp.int32, (32, width), 0)
+    lane = lax.broadcasted_iota(jnp.int32, (32, width), 1)
+    return column_sum(jnp.where(lane // 32 == device, spread_out, 0.0))
+
+
+def narrow(vector, k):
+    device = lax.broadcasted_iota(jnp.int32, (32, 1024), 0)
+    lane = lax.broadcasted_iota(jnp.int32, (32, 1024), 1)
+    source = lax.broadcasted_iota(jnp.int32, (1024, 128), 0)
+    target = lax.broadcasted_iota(jnp.int32, (1024, 128), 1)
+    chosen = jnp.where(target == k * 32 + lax.rem(source, 32), 1.0, 0.0).astype(BF)
+    return exact_nn(jnp.where(lane // 32 == device, vector, 0.0), chosen)
+
+
+def flat(value):
+    return value.reshape(-1, value.shape[-1])
+
+
+INPUTS = """lat_own grad_own wq wp wu wd ada cond q_bias v_bias p_bias d_bias u_bias a_bias"""
+OUTPUTS = """block_mine input_mine q_out p_out u_out d_out held_a held_b held_d
+    ada_out cond_out ada_bias_out bias_out"""
+GROUP = (2, 4, 2, 128, 1024)
+TOKENS = (1024, 1024)
+
+
+def scratch():
+    v, f = (lambda *s: pltpu.VMEM(s, BF)), (lambda *s: pltpu.VMEM(s, F32))
+    dma, regular = pltpu.SemaphoreType.DMA, pltpu.SemaphoreType.REGULAR
+    out = dict(lat=v(*TOKENS), grad=v(*TOKENS), attn_in=v(*TOKENS), mid=f(*TOKENS), branch_one=v(*TOKENS))
+    out.update(mlp_in=v(*TOKENS), g_two=v(*TOKENS), mine=v(*TOKENS), theirs_a=v(*TOKENS), theirs_b=v(*TOKENS))
+    out.update(buf_a=v(*GROUP), buf_b=v(*GROUP), gu=v(*GROUP), buf_c=v(*GROUP), buf_d=v(*GROUP))
+    for i in range(2):
+        out[f"first_a{i}"], out[f"first_b{i}"] = v(4, 2, SPLIT, 1024), v(4, 2, 128 - SPLIT, 1024)
+    for i in range(3):
+        out[f"second{i}"], out[f"third{i}"] = v(4, 128, 1024), v(3, 128, 1024)
+    out.update(total=f(128, 1024), heads_grad=v(2, 1024, 256), lse=f(1024, 128))
+    out.update(key_total=f(1024, 128), value_total=f(1024, 128))
+    out.update(small=f(16, 128), small_full=f(2, 4, 2, 2, 16, 128), wide=v(128, 3072), silu=f(16, 128))
+    out.update(part=f(4, 2, 2, 8, 512), near_c=f(4, 2, 8, 512), near_y=f(4, 8, 512), near_z=f(4, 8, 512))
+    out.update(mods=f(2, 8, 512), vectors=f(16, 1024), up_bias=f(1, 4096), stats=f(8, 1024), columns=f(8, 1024))
+    out.update(up_sums=f(2, 1, 1024), sums=f(2, 1, 768), all_mods=f(4, 2, 2, 8, 512), tall=f(128, 512))
+    out.update(bias_part=f(2, 2, 2, 4, 2, 128), bias_c=f(2, 2, 4, 2, 128), bias_x=f(2, 4, 2, 128))
+    out.update(bias_y=f(4, 2, 128), bias_z=f(3, 2, 128), found=f(16, 128), other=f(16, 128))
+    out.update(spread_x=f(2, 2, 4, 1, 128), spread_c=f(2, 4, 1, 128), spread_y=f(2, 4, 1, 128))
+    out.update(spread_z=f(4, 2, 1, 128), picked=f(8, 128), picked_other=f(8, 128))
+    out.update(gather_send=dma((4, 24)), gather_recv=dma((4, 24)), gather_local=dma((4, 4)))
+    out.update(scatter_send=dma((3, 28)), scatter_recv=dma((3, 28)), pair_send=dma((4, 4)), pair_recv=dma((4, 4)))
+    out.update(swap_send=dma((4, 2)), swap_recv=dma((4, 2)), swap_local=dma((4,)))
+    out.update(small_send=dma((4, 8)), small_recv=dma((4, 8)), load_sem=dma((12,)), free=regular)
+    return out
+
+
+def pairs_kernel(*refs):
+    names = INPUTS.split() + OUTPUTS.split() + list(scratch())
+    r = dict(zip(names, refs))
+    Block(r).run()
+
+
+class Block:
+    def __init__(self, r):
+        for name, ref in r.items():
+            setattr(self, name, ref)
+
+    def run(self):
+        self.set_up()
+        self.begin()
+        self.attend()
+        self.mlp()
+        self.attend_back()
+        self.end()
+
+    def set_up(self):
+        gather = lambda i, own, full, lanes: Gather(
+            own, full, lanes, self.gather_send.at[i], self.gather_recv.at[i], self.gather_local.at[i]
+        )
+        self.q = gather(
+            0, lambda h: [(self.wq.at[j, :, block(h, 256)], 256 * j, 256) for j in range(3)], self.buf_a, (0, 768)
+        )
+        self.p = gather(1, lambda h: [(self.wp.at[:, block(h, 256)], 768, 256)], self.buf_a, (768, 256))
+        self.u = gather(2, lambda h: [(self.wu.at[:, block(h, 1024)], 0, 1024)], self.gu, (0, 1024))
+        self.d = gather(3, lambda h: [(self.wd.at[:, block(h, 1024)], 0, 1024)], self.held_d, (0, 1024))
+        outs = (
+            lambda h: [(self.d_out.at[:, block(h, 1024)], 0, 1024)],
+            lambda h: [(self.u_out.at[:, block(h, 1024)], 0, 1024)],
+            lambda h: [(self.q_out.at[j, :, block(h, 256)], 256 * j, 256) for j in range(3)]
+            + [(self.p_out.at[:, block(h, 256)], 768, 256)],
+        )
+        parts = (self.buf_d, self.buf_c, self.buf_d)
+        firsts = ((self.first_a0, self.first_b0), (self.first_a1, self.first_b1), (self.first_a0, self.first_b0))
+        rest = ((self.second0, self.third0), (self.second1, self.third1), (self.second2, self.third2))
+        self.down, self.up, self.attn = [
+            Scatter(
+                parts[i], *firsts[i], *rest[i], self.total, outs[i], self.scatter_send.at[i], self.scatter_recv.at[i]
+            )
+            for i in range(3)
+        ]
+        swaps = [(self.lat_own, self.lat), (self.grad_own, self.grad)]
+        self.swap_lat, self.swap_grad = [
+            Swap(own, full, self.swap_send.at[i], self.swap_recv.at[i], self.swap_local.at[i])
+            for i, (own, full) in enumerate(swaps)
+        ]
+        backs = [(self.g_two, self.block_mine), (self.branch_one, self.input_mine)]
+        self.swap_block, self.swap_input = [
+            SwapBack(full, out, self.swap_send.at[2 + i, 0], self.swap_recv.at[2 + i, 0], self.swap_local.at[2 + i])
+            for i, (full, out) in enumerate(backs)
+        ]
+        self.pairs = [
+            Pair(self.mine, theirs, self.pair_send.at[i], self.pair_recv.at[i])
+            for i, theirs in enumerate((self.theirs_a, self.theirs_b, self.theirs_a, self.theirs_b))
+        ]
+
+    def load(self, i, source, target):
+        return pltpu.make_async_copy(source, target, self.load_sem.at[i])
+
+    def begin(self):
+        z, y, c, x = place()
+        q, p, u, d = self.q, self.p, self.u, self.d
+        send, recv = self.small_send, self.small_recv
+        little = SmallGather(self.small, self.small_full, send.at[0], recv.at[0])
+        v = self.cond[...].astype(F32)
+        silu = (v / (1.0 + jnp.exp(-v))).astype(BF).astype(F32)
+        self.small[...] = jnp.zeros_like(self.small)
+        for k in range(8):
+            self.small[k : k + 1, :] = silu[:, k * 128 : (k + 1) * 128]
+        for k, bias in enumerate((self.q_bias, self.v_bias, self.p_bias, self.d_bias)):
+            self.small[8:9, k * 32 : (k + 1) * 32] = bias[...].astype(F32)
+        self.small[9:10, :] = self.u_bias[...].astype(F32)
+        a_bias = self.a_bias[...].astype(F32)
+        for j in range(6):
+            self.small[10 + j // 4 : 11 + j // 4, j % 4 * 32 : j % 4 * 32 + 32] = a_bias[j : j + 1, :]
+        greet(partners())
+        q.start_core()
+        little.start()
+        for group in (p, u, d):
+            group.start_core()
+        self.swap_lat.start()
+        self.wide[...] = jnp.zeros_like(self.wide)
+        ada = [self.load(j, self.ada.at[j], self.wide.at[block(c, 64), pl.ds(j * 512, 512)]) for j in range(6)]
+        for copy in ada:
+            copy.start()
+        q.enter()
+        little.step((0,), (1, 2, 3))
+        self.part[...] = jnp.zeros_like(self.part)
+        little.step((1, 2, 3), (4,))
+        for copy in ada:
+            copy.wait()
+        little.step((4,), (5,))
+        row = z * 2 + y
+        lhs = [self.small_full[x, b // 4, b // 2 % 2, b % 2, pl.ds(row, 1), :] for b in range(16)]
+        lhs = jnp.concatenate(lhs, 0)
+        self.silu[...] = lhs
+        for j in range(6):
+            product = nn(lhs.astype(BF), self.wide[:, j * 512 : (j + 1) * 512])
+            for b in range(16):
+                self.part[b // 4, b // 2 % 2, b % 2, j : j + 1, :] = product[b : b + 1, :]
+        near_c, near_y, near_z = self.near_c, self.near_y, self.near_z
+        first = remote(self.part.at[:, :, 1 - c], near_c, send.at[1, 0], recv.at[1, 0], at(z, y, 1 - c, x))
+        first.start()
+        q.arrived(2)
+        first.wait()
+        for zz in range(4):
+            for yy in range(2):
+                near_c[zz, yy] = near_c[zz, yy] + self.part[zz, yy, c]
+        second = remote(near_c.at[:, 1 - y], near_y, send.at[1, 1], recv.at[1, 1], at(z, 1 - y, c, x))
+        second.start()
+        q.turn(0)
+        second.wait()
+        for zz in range(4):
+            near_y[zz] = near_y[zz] + near_c[zz, y]
+        thirds = []
+        for s in (1, 2, 3):
+            to = lax.rem(z + s, 4)
+            thirds.append(
+                remote(near_y.at[to], near_z.at[s - 1], send.at[1, 1 + s], recv.at[1, 1 + s], at(to, y, c, x))
+            )
+            thirds[-1].start()
+        q.arrived(1)
+        for copy in thirds:
+            copy.wait()
+        near_z[3] = near_y[z] + near_z[0] + near_z[1] + near_z[2]
+        fourth = remote(near_z.at[3], self.mods.at[1 - c], send.at[1, 5], recv.at[1, 5], at(z, y, 1 - c, 1 - x))
+
+        @pl.when(c != x)
+        def _():
+            fourth.start()
+
+        q.arrived(3)
+        self.swap_lat.share()
+        q.turn(2)
+
+        @pl.when(c != x)
+        def _():
+            fourth.wait()
+
+        @pl.when(c == x)
+        def _():
+            self.mods[c] = near_z[3]
+
+        fifth = remote(self.mods.at[c], self.mods.at[c], send.at[1, 6], recv.at[1, 6], at(z, y, 1 - c, x))
+        fifth.start()
+        little.step((5,), ())
+        bias = [widen(self.small_full, 8, k) for k in range(4)]
+        ada_bias = [widen(self.small_full, 10 + j // 4, j % 4) for j in range(6)]
+        for k, (zz, yy, cc, xx) in enumerate(devices()):
+            self.up_bias[:, k * 128 : (k + 1) * 128] = self.small_full[xx, zz, yy, cc, 9:10, :]
+        q.turn(1)
+        fifth.wait()
+        for j in range(6):
+            for h in range(2):
+                lanes = slice(h * 512, (h + 1) * 512)
+                self.vectors[j : j + 1, lanes] = self.mods[h, j : j + 1, :] + ada_bias[j][:, lanes]
+        for k in range(4):
+            self.vectors[6 + k : 7 + k, :] = bias[k]
+        q.turn(3)
+        p.enter()
+        u.enter()
+        self.swap_lat.finish()
+
+    def attend(self):
+        z, y, c, x = place()
+        q, p, u, d, vectors = self.q, self.p, self.u, self.d, self.vectors
+
+        def modulated(i):
+            rows = block(i, 256)
+            normal, _ = normalise(self.lat[rows, :].astype(F32))
+            self.attn_in[rows, :] = (normal * (1.0 + vectors[1:2, :]) + vectors[0:1, :]).astype(BF)
+
+        loop(4, modulated)
+        q.finish()
+        self.swap_grad.start()
+
+        def project(i):
+            b, quarter = i // 4, lax.rem(i, 4)
+            columns = pl.ds(pl.multiple_of(b * 512 + c * 256, 256), 256)
+            values = nn(self.attn_in[block(quarter, 256), :], flat(self.buf_a[b, :, :, :, 0:768]))
+            query = values[:, 0:256] + vectors[6:7, columns]
+            value = values[:, 512:768] + vectors[7:8, columns]
+            self.buf_b[b, quarter, :, :, 0:256] = query.astype(BF).reshape(2, 128, 256)
+            self.buf_b[b, quarter, :, :, 256:512] = values[:, 256:512].astype(BF).reshape(2, 128, 256)
+            self.buf_b[b, quarter, :, :, 512:768] = value.astype(BF).reshape(2, 128, 256)
+
+        loop(8, project)
+        for k in (2, 1, 3):
+            p.arrived(k)
+        for k in (0, 2, 1, 3):
+            p.turn(k)
+        lane = lax.broadcasted_iota(jnp.int32, (1, 128), 1)
+        self.lse[...] = jnp.zeros_like(self.lse)
+
+        def attend(i):
+            pair, half = i // 2, lax.rem(i, 2)
+            rows, zz = block(half, 512), pl.ds(half * 2, 2)
+            b, q_at = pair // 2, pl.multiple_of(lax.rem(pair, 2) * 128, 128)
+            queries = flat(self.buf_b[b, zz, :, :, pl.ds(q_at, 128)]) * BF(0.125)
+            keys = flat(self.buf_b[b, :, :, :, pl.ds(q_at + 256, 128)])
+            values = flat(self.buf_b[b, :, :, :, pl.ds(q_at + 512, 128)])
+            result = None
+            logs = self.lse[rows, :]
+            for h in range(2):
+                scores = nt(jnp.where(in_half(h), queries, jnp.zeros_like(queries)), keys)
+                largest = jnp.max(scores, -1, keepdims=True)
+                exponent = jnp.exp(scores - largest)
+                summed = jnp.sum(exponent, -1, keepdims=True)
+                mixture = nn(exponent.astype(BF), values) * (1.0 / summed)
+                result = mixture if h == 0 else jnp.where(in_half(0), result, mixture)
+                logs = jnp.where(lane == pair * 2 + h, largest + jnp.log(summed), logs)
+            self.buf_b[b, zz, :, :, pl.ds(q_at + 768, 128)] = result.astype(BF).reshape(2, 2, 128, 128)
+            self.lse[rows, :] = logs
+
+            @pl.when(i == 1)
+            def _():
+                u.arrived(2)
+                u.arrived(1)
+                u.arrived(3)
+
+            @pl.when(i == 3)
+            def _():
+                u.turn(0)
+                d.enter()
+
+            @pl.when(i == 5)
+            def _():
+                u.turn(2)
+                u.turn(1)
+                u.turn(3)
+
+        loop(8, attend)
+        p.finish()
+        self.load(0, self.buf_a, self.held_a).start()
+        pair = self.pairs[0]
+
+        def out(i):
+            zz = i
+            partial = nt(flat(self.buf_b[0, zz, :, :, 768:1024]), flat(self.buf_a[0, :, :, :, 768:1024]))
+            partial += nt(flat(self.buf_b[1, zz, :, :, 768:1024]), flat(self.buf_a[1, :, :, :, 768:1024]))
+            pair.give(i, partial)
+
+        loop(4, out)
+        self.load(1, self.buf_b, self.held_b).start()
+        self.swap_grad.share()
+
+        def residual(i):
+            rows = block(i, 256)
+            branch = pair.take(i) + vectors[8:9, :]
+            self.branch_one[rows, :] = branch.astype(BF)
+            self.mid[rows, :] = self.lat[rows, :].astype(F32) + vectors[2:3, :] * branch
+
+        loop(4, residual)
+
+    def mlp(self):
+        z, y, c, x = place()
+        u, d, vectors, stats, down, up = self.u, self.d, self.vectors, self.stats, self.down, self.up
+        active, up_grad, slope, hidden_grad = self.buf_c, self.buf_c, self.buf_a, self.buf_a
+        wd, gu, mid, mlp_in, g_two, grad = self.buf_b, self.gu, self.mid, self.mlp_in, self.g_two, self.grad
+        self.swap_grad.finish()
+        stats[...] = jnp.zeros_like(stats)
+        self.up_sums[...] = jnp.zeros_like(self.up_sums)
+
+        def enter(i):
+            rows = block(i, 256)
+            normal, _ = normalise(mid[rows, :])
+            mlp_in[rows, :] = (normal * (1.0 + vectors[4:5, :]) + vectors[3:4, :]).astype(BF)
+            g = (grad[rows, :].astype(F32) * vectors[5:6, :]).astype(BF)
+            g_two[rows, :] = g
+            mine_too = jnp.where(i // 2 == c, 1.0, 0.0)
+            stats[1:2, :] += column_sum(g.astype(F32)) * mine_too
+
+        loop(4, enter)
+        for k in (2, 1, 3):
+            d.arrived(k)
+        u.finish()
+        self.load(0, self.buf_a, self.held_a).wait()
+        d.turn(0)
+
+        def ascend(i):
+            b, quarter = i // 4, lax.rem(i, 4)
+            columns = pl.ds(pl.multiple_of(b * 2048 + c * 1024, 1024), 1024)
+            hidden = nn(mlp_in[block(quarter, 256), :], flat(gu[b])) + self.up_bias[:, columns]
+            value, gradient = gelu_parts(hidden)
+            active[b, quarter] = value.astype(BF).reshape(2, 128, 1024)
+            slope[b, quarter] = gradient.astype(BF).reshape(2, 128, 1024)
+
+            @pl.when(i == 5)
+            def _():
+                d.turn(2)
+                d.turn(1)
+
+        loop(8, ascend)
+        d.turn(3)
+
+        def down_gradient(i):
+            b, half = i // 2, lax.rem(i, 2)
+            value = tn(g_two[:, block(half, 512)], flat(active[b]))
+            self.buf_d[b, pl.ds(half * 2, 2)] = value.astype(BF).reshape(2, 2, 128, 1024)
+
+        loop(4, down_gradient)
+        down.start()
+        d.finish()
+        self.load(1, self.buf_b, self.held_b).wait()
+        load = self.load(2, self.held_d, wd)
+        load.start()
+        load.wait()
+        pair, back = self.pairs[1], self.pairs[2]
+
+        def descend(i):
+            pair.give(i, nt(flat(active[0, i]), flat(wd[0])) + nt(flat(active[1, i]), flat(wd[1])))
+
+        loop(4, descend)
+
+        def hidden_gradient(i):
+            b, quarter = i // 4, lax.rem(i, 4)
+            value = nn(g_two[block(quarter, 256), :], flat(wd[b])) * flat(slope[b, quarter]).astype(F32)
+            value = value.astype(BF)
+            hidden_grad[b, quarter] = value.reshape(2, 128, 1024)
+            self.up_sums[b] += column_sum(value.astype(F32))
+
+        loop(8, hidden_gradient)
+        self.load(3, self.held_b, self.buf_b).start()
+
+        def leave(i):
+            rows = block(i, 256)
+            branch_two = pair.take(i) + vectors[9:10, :]
+            g_two[rows, :] = (mid[rows, :] + vectors[5:6, :] * branch_two).astype(BF)
+            stats[0:1, :] += column_sum(grad[rows, :].astype(F32) * branch_two)
+
+        loop(4, leave)
+
+        def descend_back(i):
+            back.give(i, nt(flat(hidden_grad[0, i]), flat(gu[0])) + nt(flat(hidden_grad[1, i]), flat(gu[1])))
+
+        loop(4, descend_back)
+        down.turn(2)
+        down.turn(1)
+
+        def up_gradient(i):
+            b, half = i // 2, lax.rem(i, 2)
+            value = tn(mlp_in[:, block(half, 512)], flat(hidden_grad[b]))
+            up_grad[b, pl.ds(half * 2, 2)] = value.astype(BF).reshape(2, 2, 128, 1024)
+
+        loop(4, up_gradient)
+        self.load(4, self.held_a, self.buf_a).start()
+        up.start()
+        down.turn(3)
+        down.turn(0)
+
+        def residual(i):
+            rows = block(i, 256)
+            dy = back.take(i)
+            normal, scale = normalise(mid[rows, :])
+            stats[2:3, :] += column_sum(dy)
+            stats[3:4, :] += column_sum(dy * normal)
+            dn = dy * (1.0 + vectors[4:5, :])
+            dn = dn - jnp.mean(dn, -1, keepdims=True) - normal * jnp.mean(dn * normal, -1, keepdims=True)
+            total = grad[rows, :].astype(F32) + scale * dn
+            mid[rows, :] = total
+            stats[4:5, :] += column_sum(total * self.branch_one[rows, :].astype(F32))
+            g = (total * vectors[2:3, :]).astype(BF)
+            mlp_in[rows, :] = g
+            mine_too = jnp.where(i // 2 == c, 1.0, 0.0)
+            stats[5:6, :] += column_sum(g.astype(F32)) * mine_too
+
+        loop(4, residual)
+        down.leave(2)
+
+    def attend_back(self):
+        z, y, c, x = place()
+        vectors, stats, down, up, attn = self.vectors, self.stats, self.down, self.up, self.attn
+        acts, g_one, heads_grad, sums = self.buf_b, self.mlp_in, self.heads_grad, self.sums
+        weights = self.buf_a
+        sums[...] = jnp.zeros_like(sums)
+        self.load(3, self.held_b, self.buf_b).wait()
+        self.load(4, self.held_a, self.buf_a).wait()
+        down.leave(1)
+
+        def enter(i):
+            b, half = i // 2, lax.rem(i, 2)
+            value = nn(g_one[block(half, 512), :], flat(weights[b, :, :, :, 768:1024]))
+            heads_grad[b, block(half, 512), :] = value.astype(BF)
+
+        loop(4, enter)
+
+        def proj_gradient(i):
+            b, half = i // 2, lax.rem(i, 2)
+            value = tn(g_one[:, block(half, 512)], flat(acts[b, :, :, :, 768:1024]))
+            self.buf_d[b, pl.ds(half * 2, 2), :, :, 768:1024] = value.astype(BF).reshape(2, 2, 128, 256)
+
+        loop(4, proj_gradient)
+        down.leave(3)
+        lane = lax.broadcasted_iota(jnp.int32, (1, 128), 1)
+
+        def attend(i):
+            pair, quarter = i // 4, lax.rem(i, 4)
+            rows = block(quarter, 256)
+            b, at_lane = pair // 2, pl.multiple_of(lax.rem(pair, 2) * 128, 128)
+            queries = flat(acts[b, quarter, :, :, pl.ds(at_lane, 128)]) * BF(0.125)
+            keys = flat(acts[b, :, :, :, pl.ds(at_lane + 256, 128)])
+            values = flat(acts[b, :, :, :, pl.ds(at_lane + 512, 128)])
+            grads = heads_grad[b, rows, pl.ds(at_lane, 128)]
+
+            @pl.when(quarter == 0)
+            def _():
+                self.key_total[...] = jnp.zeros_like(self.key_total)
+                self.value_total[...] = jnp.zeros_like(self.value_total)
+
+            result = None
+            logs = self.lse[rows, :]
+            for h in range(2):
+                log = jnp.sum(jnp.where(lane == pair * 2 + h, logs, 0.0), -1, keepdims=True)
+                query = jnp.where(in_half(h), queries, jnp.zeros_like(queries))
+                grad = jnp.where(in_half(h), grads, jnp.zeros_like(grads))
+                probs = jnp.exp(nt(query, keys) - log)
+                probs_grad = nt(grad, values)
+                inner = jnp.sum(probs * probs_grad, -1, keepdims=True)
+                score_grad = (probs * (probs_grad - inner)).astype(BF)
+                query_grad = nn(score_grad, keys)
+                result = query_grad if h == 0 else jnp.where(in_half(0), result, query_grad)
+                self.key_total[...] += tn(score_grad, query)
+                self.value_total[...] += tn(probs.astype(BF), grad)
+            result = (result * 0.125).astype(BF)
+            acts[b, quarter, :, :, pl.ds(at_lane, 128)] = result.reshape(2, 128, 128)
+            sums[b, :, pl.ds(at_lane, 128)] += column_sum(result.astype(F32))
+
+            @pl.when(quarter == 3)
+            def _():
+                total = self.key_total[...].astype(BF)
+                acts[b, :, :, :, pl.ds(at_lane + 256, 128)] = total.reshape(4, 2, 128, 128)
+                total = self.value_total[...].astype(BF)
+                acts[b, :, :, :, pl.ds(at_lane + 512, 128)] = total.reshape(4, 2, 128, 128)
+                sums[b, :, pl.ds(at_lane + 512, 128)] = column_sum(total.astype(F32))
+
+            @pl.when(i == 1)
+            def _():
+                down.leave(0)
+                for to in (at(z, 1 - y, c, x), at(z, y, c, 1 - x)):
+                    pl.semaphore_signal(self.free, inc=1, device_id=to, device_id_type=MESH)
+                self.swap_block.start()
+
+            @pl.when(i == 5)
+            def _():
+                up.turn(2)
+                up.turn(1)
+
+            @pl.when(i == 9)
+            def _():
+                up.turn(3)
+                up.turn(0)
+                down.last()
+
+            @pl.when(i == 13)
+            def _():
+                up.leave(2)
+                up.leave(1)
+
+        loop(16, attend)
+        up.leave(3)
+        up.leave(0)
+
+        def qkv_gradient(i):
+            b, half = i // 2, lax.rem(i, 2)
+            value = tn(self.attn_in[:, block(half, 512)], flat(acts[b, :, :, :, 0:768]))
+            self.buf_d[b, pl.ds(half * 2, 2), :, :, 0:768] = value.astype(BF).reshape(2, 2, 128, 768)
+
+        loop(4, qkv_gradient)
+        down.finish()
+        pl.semaphore_wait(self.free, 2)
+        attn.start()
+        pair = self.pairs[3]
+
+        def descend(i):
+            partial = nt(flat(acts[0, i, :, :, 0:768]), flat(weights[0, :, :, :, 0:768]))
+            pair.give(i, partial + nt(flat(acts[1, i, :, :, 0:768]), flat(weights[1, :, :, :, 0:768])))
+
+        loop(4, descend)
+        up.last()
+
+        def leave(i):
+            rows = block(i, 256)
+            dy = pair.take(i)
+            normal, scale = normalise(self.lat[rows, :].astype(F32))
+            stats[6:7, :] += column_sum(dy)
+            stats[7:8, :] += column_sum(dy * normal)
+            dn = dy * (1.0 + vectors[1:2, :])
+            dn = dn - jnp.mean(dn, -1, keepdims=True) - normal * jnp.mean(dn * normal, -1, keepdims=True)
+            self.branch_one[rows, :] = (self.mid[rows, :] + scale * dn).astype(BF)
+
+        loop(4, leave)
+        self.swap_input.start()
+        self.swap_block.finish()
+
+    def end(self):
+        z, y, c, x = place()
+        stats, sums, up_sums, attn, up = self.stats, self.sums, self.up_sums, self.attn, self.up
+        send, recv, mods = self.small_send, self.small_recv, self.all_mods
+        rows = [stats[k : k + 1, :] for k in (6, 7, 4, 2, 3, 0)]
+        for j in range(6):
+            for h in range(2):
+                self.mods[h, j : j + 1, :] = rows[j][:, h * 512 : (h + 1) * 512]
+        far = remote(self.mods.at[1 - x], mods.at[z, y, 1 - c], send.at[2, 0], recv.at[2, 0], at(z, y, 1 - c, 1 - x))
+
+        @pl.when(c != x)
+        def _():
+            far.start()
+
+        @pl.when(c == x)
+        def _():
+            mods[z, y, c] = self.mods[x]
+
+        columns, bias_part = self.columns, self.bias_part
+        columns[...] = jnp.zeros_like(columns)
+        bias_part[...] = jnp.zeros_like(bias_part)
+        for b in range(2):
+            spot = pl.ds(pl.multiple_of(b * 512 + c * 256, 256), 256)
+            columns[0:1, spot] = sums[b, :, 0:256]
+            columns[1:2, spot] = sums[b, :, 512:768]
+        columns[2:3, :] = stats[5:6, :]
+        columns[3:4, :] = stats[1:2, :]
+        pieces = narrow(columns[0:1, :], 0) + narrow(columns[1:2, :], 1)
+        pieces = pieces + narrow(columns[2:3, :], 2) + narrow(columns[3:4, :], 3)
+        for k, (zz, yy, cc, xx) in enumerate(devices()):
+            bias_part[cc, xx, yy, zz, 0:1, :] = pieces[k : k + 1, :]
+        for b in range(2):
+            for i in range(8):
+                bias_part[i // 2 % 2, i % 2, i // 4, b * 2 + c, 1:2, :] = up_sums[b, :, i * 128 : (i + 1) * 128]
+        bias = SmallScatter(
+            bias_part, self.bias_c, self.bias_x, self.bias_y, self.bias_z, self.small_send.at[0], self.small_recv.at[3]
+        )
+        bias.start()
+
+        @pl.when(c != x)
+        def _():
+            far.wait()
+
+        spot = mods.at[z, y, c]
+        core = remote(spot, spot, send.at[2, 1], recv.at[2, 1], at(z, y, 1 - c, x))
+        core.start()
+        bias.step(0)
+        core.wait()
+        spot_y = mods.at[z, y]
+        across = remote(spot_y, spot_y, send.at[2, 2], recv.at[2, 2], at(z, 1 - y, c, x))
+        across.start()
+        bias.step(1)
+        attn.turn(2)
+        across.wait()
+        spot_z = mods.at[z]
+        along = [
+            remote(spot_z, spot_z, send.at[2, 2 + k], recv.at[2, 2 + k], at(lax.rem(z + k, 4), y, c, x))
+            for k in (1, 2, 3)
+        ]
+        for copy in along:
+            copy.start()
+        bias.step(2)
+        attn.turn(1)
+        silu_rows = self.silu[...].astype(BF)
+        for copy in along:
+            copy.wait()
+        total = jnp.zeros((16, 128), F32)
+        bias_rows = []
+        for j in range(6):
+            values = jnp.concatenate([mods[b // 4, b // 2 % 2, b % 2, j : j + 1, :] for b in range(16)], 0)
+            high, low = split_bf(values)
+            weights = self.wide[:, j * 512 : (j + 1) * 512]
+            self.tall[...] = tn(silu_rows, high) + tn(silu_rows, low)
+            self.ada_out[j] = self.tall[block(c, 64), :]
+            total = total + nt(high, weights) + nt(low, weights)
+            bias_rows.append(column_sum(values))
+        self.found[...] = total
+        group = (lax.rem(z, 2) * 2 + y) * 2 + c
+        source = lax.broadcasted_iota(jnp.int32, (512, 128), 0)
+        target = lax.broadcasted_iota(jnp.int32, (512, 128), 1)
+        chosen = jnp.where((source == group * 64 + target) & (target < 64), 1.0, 0.0).astype(BF)
+        self.picked[...] = exact_nn(jnp.concatenate(bias_rows + [jnp.zeros((2, 512), F32)], 0), chosen)
+        first = [
+            remote(self.found, self.other, send.at[3, 0], recv.at[1, 0], at(z, y, c, 1 - x)),
+            remote(self.picked, self.picked_other, send.at[3, 1], recv.at[1, 1], at(z, y, c, 1 - x)),
+        ]
+        for copy in first:
+            copy.start()
+        attn.turn(3)
+        for copy in first:
+            copy.wait()
+        self.ada_bias_out[...] = jnp.where(z // 2 == x, self.picked[...], self.picked_other[...])
+        total = self.found[...] + self.other[...]
+        spread_x, spread_c, spread_y, spread_z = self.spread_x, self.spread_c, self.spread_y, self.spread_z
+        for b in range(16):
+            spread_x[b % 2, b // 2 % 2, b // 4] = total[b : b + 1, :]
+        second = remote(spread_x.at[1 - c], spread_c, send.at[3, 2], recv.at[1, 2], at(z, y, 1 - c, x))
+        second.start()
+        self.bias_out[...] = bias.finish()
+        attn.turn(0)
+        second.wait()
+        spread_c[...] = spread_c[...] + spread_x[c]
+        third = remote(spread_c.at[1 - y], spread_y.at[y], send.at[3, 3], recv.at[1, 3], at(z, 1 - y, c, x))
+        third.start()
+        spread_y[y] = spread_c[y]
+        attn.leave(2)
+        third.wait()
+        fourth = []
+        for k in (1, 2, 3):
+            to = lax.rem(z + k, 4)
+            fourth.append(
+                remote(spread_y.at[:, to], spread_z.at[z], send.at[3, 3 + k], recv.at[1, 3 + k], at(to, y, c, x))
+            )
+            fourth[-1].start()
+        spread_z[z] = spread_y[:, z]
+        attn.leave(1)
+        for copy in fourth:
+            copy.wait()
+        v = self.cond[...].astype(F32)
+        v = jnp.concatenate([v[:, k * 128 : (k + 1) * 128] for k in range(8)], 0)
+        gate = 1.0 / (1.0 + jnp.exp(-v))
+        row = jnp.concatenate([spread_z[b // 2, b % 2] for b in range(8)], 0)
+        self.cond_out[...] = row * gate * (1.0 + v * (1.0 - gate))
+        attn.leave(3)
+        attn.leave(0)
+        up.finish()
+        attn.last()
+        self.swap_input.finish()
+        attn.finish()
+
+
+def on_device_pairs(
+    latents_in,
+    condition,
+    grad_out,
+    qkv_weight,
+    proj_weight,
+    up_weight,
+    down_weight,
+    ada_weight,
+    query_bias,
+    value_bias,
+    proj_bias,
+    up_bias,
+    down_bias,
+    ada_bias,
+):
+    x = lax.axis_index("tp")
+    small = [b.reshape(1, -1) for b in (query_bias, value_bias, proj_bias, down_bias, up_bias)]
+    out = lambda *shape: jax.ShapeDtypeStruct(shape, F32)
+    group = jax.ShapeDtypeStruct(GROUP, BF)
+    rows = jax.ShapeDtypeStruct((512, 1024), BF)
+    results = pl.pallas_call(
+        pairs_kernel,
+        out_shape=[rows, rows, out(3, 64, 512), out(64, 512), out(64, 2048), out(64, 2048)]
+        + [group] * 3
+        + [out(6, 64, 512), out(8, 128), out(8, 128), out(2, 128)],
+        in_specs=[IN_ANY] * 7 + [IN_VMEM] * 7,
+        out_specs=[IN_ANY] * 9 + [IN_VMEM] * 4,
+        scratch_shapes=list(scratch().values()),
+        compiler_params=pltpu.CompilerParams(
+            collective_id=0, has_side_effects=True, vmem_limit_bytes=63 * MIB
+        ),
+        name="dit_block",
+    )(
+        latents_in.reshape(512, 1024), grad_out.reshape(512, 1024), qkv_weight.transpose(1, 0, 2), proj_weight.T,
+        up_weight, down_weight.T, ada_weight.transpose(1, 0, 2), condition, *small, ada_bias,
+    )
+    block_mine, input_mine, q_out, p_out, u_out, d_out, _, _, _, ada_out, cond_out, ada_bias_out, bias_out = results
+    return (
+        block_mine.reshape(512, 1, 1024),
+        input_mine.astype(F32).reshape(512, 1, 1024),
+        lax.dynamic_slice_in_dim(cond_out, x * 4, 4, 0).reshape(1, 512),
+        q_out.transpose(1, 0, 2),
+        p_out.T,
+        u_out,
+        d_out.T,
+        ada_out.transpose(1, 0, 2),
+        bias_out[0, 0:32],
+        bias_out[0, 32:64],
+        bias_out[0, 64:96],
+        bias_out[1],
+        bias_out[0, 96:128],
+        lax.dynamic_slice_in_dim(ada_bias_out, x * 32, 32, 1)[:6],
+    )
+
+
 def solution(mesh):
+    shape = dict(mesh.shape)
+    pairs = shape["fsdp"] == 16 and shape["tp"] == 2
     return jax.shard_map(
-        on_device,
+        on_device_pairs if pairs else on_device_general,
         mesh=mesh,
         in_specs=(
             P("tp", "fsdp", None),

time: 1230 us -> 349 us (0.28)
  waiting for transfers between devices: 682 us -> 0 us
  Pallas kernels: 0 us -> 333 us
  blocking collectives: 221 us -> 0 us
  matrix products: 171 us -> 0 us
  other arithmetic: 77.1 us -> 1.51 us
  local copies, waits for them, and re-layouts: 54.4 us -> 13.6 us
  between operations: 15.4 us -> 0.72 us
    reduce_scatter x10 -> x0, waiting for transfers between devices: 390 us -> none  [the longest x1 86.8 us: on_device(): lax.psum_scatter(ada_grad.astype(jnp.bfloat16), 'fsdp', scatter_dimension...]
    pallas_call x0 -> x1, Pallas kernels: none -> 333 us  [on_device_pairs(): pl.pallas_call(pairs_kernel, out_shape=[rows, rows, out(3, 64, 512), out(...]
    dot_general x28 -> x0, matrix products: 171 us -> none  [the longest x2 19.3 us: one_block(): jnp.einsum('qbhd,kbhd->bhqk', g_rows, value_rows, preferred_element_type=...]
    unnamed x23 -> x0, waiting for transfers between devices: 148 us -> none
    all_gather x9 -> x0, waiting for transfers between devices: 144 us -> none  [the longest x2 67 us: gather_grads(): return lax.all_gather(piece, 'tp', axis=0, tiled=True)]
    all_gather x3 -> x0, blocking collectives: 143 us -> none  [the longest x1 71.3 us: on_device(): lax.all_gather(ada_bias, ('fsdp', 'tp'), axis=1, tiled=True)]
    unnamed x2 -> x0, blocking collectives: 78.2 us -> none
    convert_element_type x15 -> x0, other arithmetic: 37.4 us -> none  [the longest x2 20.9 us: one_block(): score_grad = (weights_soft * (soft_grad - inner_sum)).astype(jnp.bfloat16)]
  transfers between devices with their start and end apart: 21 -> 0, of which waited for: 16 -> 0; matrix products, arithmetic and copies ran while one was open for 12% -> 0% of each run, Pallas kernels for 0% -> 0%
where the time goes in v3:
time: 349 us
  Pallas kernels  333 us (95%)
  local copies, waits for them, and re-layouts  13.6 us (4%)
    pallas_call x1, Pallas kernels, on_device_pairs(): pl.pallas_call(pairs_kernel, out_shape=[rows, rows, out(3, 64, 512), out(...  333 us
    unnamed x19, local copies, waits for them, and re-layouts  8.34 us

profile of v3, /device:TPU:0, one launch (start us, length us, event | category | flops | bytes accessed | tf_op | source)
XLA Modules:
  0.0 349.0 jit_solution(16213551077987268805)
XLA Ops:
  0.7 333.1 %dit_block.1 = (bf16[512,1024]{1,0:T(8,128)(2,1)}, bf16[512,1024]{1,0:T(8,128)(2,1)}, f32[3,64,512]{2,1,0:T(8,128)}, f32[64,512]{1,0:T(8,128)}, f32[64,2048]{1,0...) custom-call(bf16[512,1024]{1,0:T(8,128)(2,1)} %bitcast.31, ...), custom_call_target="tpu_custom_call" | custom-call | tf_op jit(solution)/shard_map/dit_block/pallas_call | solution.py:1450
  333.8 0.0 copy-start
  333.8 1.4 constant_dynamic-slice_fusion
  335.2 1.3 constant_dynamic-slice_fusion.1
  336.5 1.4 slice_bitcast_fusion
  337.9 1.2 slice_bitcast_fusion.1
  339.1 0.0 copy-start.4
  339.1 1.5 bitcast_convert_fusion
  340.6 0.0 copy-start.5
  340.6 0.0 copy-start.3
  340.6 0.0 copy-start.2
  340.6 0.0 copy-start.1
  340.6 3.5 copy.28
  344.1 0.0 copy-done
  344.1 1.0 copy.35
  345.1 0.0 copy-done.4
  345.1 0.7 copy.36
  345.8 0.0 copy-done.5
  345.8 0.7 copy.37
  346.5 0.0 copy-done.3
  346.5 0.8 copy.38
  347.3 0.0 copy-done.2
  347.3 0.8 copy.39
  348.1 0.0 copy-done.1
  348.1 0.9 copy.40
Async XLA Ops:
  333.8 10.3 %copy-start = (bf16[512,1024]{1,0:T(8,128)(2,1)S(1)}, bf16[512,1024]{1,0:T(8,128)(2,1)}, u32[]{:S(2)}) copy-start(bf16[512,1024]{1,0:T(8,128)(2,1)} %get-tuple-element.24) | copy-start | bytes 3145732
  339.1 6.0 %copy-start.4 = (f32[3,64,512]{2,1,0:T(8,128)S(1)}, f32[3,64,512]{2,1,0:T(8,128)}, u32[]{:S(2)}) copy-start(f32[3,64,512]{2,1,0:T(8,128)} %get-tuple-element.27) | copy-start | bytes 1179652
  340.6 5.2 %copy-start.5 = (f32[64,512]{1,0:T(8,128)S(1)}, f32[64,512]{1,0:T(8,128)}, u32[]{:S(2)}) copy-start(f32[64,512]{1,0:T(8,128)} %get-tuple-element.28) | copy-start | bytes 393220
  340.6 5.9 %copy-start.3 = (f32[64,2048]{1,0:T(8,128)S(1)}, f32[64,2048]{1,0:T(8,128)}, u32[]{:S(2)}) copy-start(f32[64,2048]{1,0:T(8,128)} %get-tuple-element.71) | copy-start | bytes 1572868
  340.6 6.7 %copy-start.2 = (f32[64,2048]{1,0:T(8,128)S(1)}, f32[64,2048]{1,0:T(8,128)}, u32[]{:S(2)}) copy-start(f32[64,2048]{1,0:T(8,128)} %get-tuple-element.30) | copy-start | bytes 1572868
  340.6 7.5 %copy-start.1 = (f32[6,64,512]{2,1,0:T(8,128)S(1)}, f32[6,64,512]{2,1,0:T(8,128)}, u32[]{:S(2)}) copy-start(f32[6,64,512]{2,1,0:T(8,128)} %get-tuple-element.31) | copy-start | bytes 2359300

commit v4 on v3

--- a/solution.py
+++ b/solution.py
@@ -378,9 +378,15 @@
     )
 
 
-def loop(count, body):
+def loop(count, body, ticks=None):
     def step(i, carry):
         body(i)
+        for k, tick in (ticks or {}).items():
+
+            @pl.when(i == k)
+            def _(tick=tick):
+                tick()
+
         return carry
 
     lax.fori_loop(0, count, step, 0)
@@ -396,6 +402,7 @@
 def partners():
     z, y, c, x = place()
     out = [at(z, y, 1 - c, x), at(z, 1 - y, c, x), at(z, y, c, 1 - x), at(z, y, 1 - c, 1 - x)]
+    out.append(at(z, 1 - y, c, 1 - x))
     return out + [at(lax.rem(z + d, 4), y, c, x) for d in (1, 2, 3)]
 
 
@@ -426,7 +433,7 @@
             spot, to = self.full.at[:, from_z, y, a, self.lanes], at(z, 1 - y, c, x)
         else:
             spot, to = self.full.at[x, from_z, :, b, self.lanes], at(z, y, c, 1 - x)
-        return remote(spot, spot, self.send.at[4 + 4 * kind + d], self.recv.at[4 + 4 * kind + d], to)
+        return remote(spot, spot, self.send.at[8 + 4 * kind + d], self.recv.at[8 + 4 * kind + d], to)
 
     def start_core(self):
         for copy in self._core():
@@ -437,6 +444,8 @@
             copy.wait()
         for d in (2, 1, 3):
             self._copy(0, d).start()
+
+    def first(self):
         self._copy(1, 0).start()
         self._copy(2, 0).start()
 
@@ -458,25 +467,25 @@
 
 
 class Scatter:
-    def __init__(self, part, first_a, first_b, second, third, total, out, send, recv):
+    def __init__(self, part, first_a, first_b, second, third, total, lanes, out, send, recv):
         self.part, self.first_a, self.first_b = part, first_a, first_b
         self.second, self.third, self.total, self.out = second, third, total, out
-        self.send, self.recv = send, recv
+        self.lanes, self.send, self.recv = pl.ds(*lanes), send, recv
 
     def _copy(self, kind, d):
         z, y, c, x = place()
-        a, b, to_z = pl.ds(0, SPLIT), pl.ds(SPLIT, 128 - SPLIT), lax.rem(z + d, 4)
+        a, b, n, to_z = pl.ds(0, SPLIT), pl.ds(SPLIT, 128 - SPLIT), self.lanes, lax.rem(z + d, 4)
         send, recv = self.send.at[4 * kind + d], self.recv.at[4 * kind + d]
         to_x, to_y = at(z, y, c, 1 - x), at(z, 1 - y, c, x)
         if kind == 0:
-            return remote(self.part.at[:, to_z, 1 - y, a], self.first_a.at[to_z], send, recv, to_y)
+            return remote(self.part.at[:, to_z, 1 - y, a, n], self.first_a.at[to_z, :, :, n], send, recv, to_y)
         if kind == 1:
-            return remote(self.part.at[1 - x, to_z, :, b], self.first_b.at[to_z], send, recv, to_x)
+            return remote(self.part.at[1 - x, to_z, :, b, n], self.first_b.at[to_z, :, :, n], send, recv, to_x)
         if kind == 2:
-            return remote(self.first_a.at[to_z, 1 - x], self.second.at[to_z, a], send, recv, to_x)
+            return remote(self.first_a.at[to_z, 1 - x, :, n], self.second.at[to_z, a, n], send, recv, to_x)
         if kind == 3:
-            return remote(self.first_b.at[to_z, 1 - y], self.second.at[to_z, b], send, recv, to_y)
-        return remote(self.second.at[to_z], self.third.at[d - 1], send, recv, at(to_z, y, c, x))
+            return remote(self.first_b.at[to_z, 1 - y, :, n], self.second.at[to_z, b, n], send, recv, to_y)
+        return remote(self.second.at[to_z, :, n], self.third.at[d - 1, :, n], send, recv, at(to_z, y, c, x))
 
     def _core(self):
         z, y, c, x = place()
@@ -492,34 +501,41 @@
             copies.append(pltpu.make_async_copy(self.total.at[block(c, 64), lanes], target, self.send.at[24 + i]))
         return copies
 
+    def _start(self, d):
+        self._copy(0, d).start()
+        self._copy(1, d).start()
+
     def start(self):
-        for d in (2, 1, 3, 0):
-            self._copy(0, d).start()
-            self._copy(1, d).start()
+        self._start(2)
+        self._start(1)
 
     def turn(self, d):
         z, y, c, x = place()
-        to_z = lax.rem(z + d, 4)
+        to_z, n = lax.rem(z + d, 4), self.lanes
         a, b = pl.ds(0, SPLIT), pl.ds(SPLIT, 128 - SPLIT)
         self._copy(0, d).wait()
         for k in range(2):
-            total = self.first_a[to_z, k].astype(F32) + self.part[k, to_z, y, a].astype(F32)
-            self.first_a[to_z, k] = total.astype(BF)
+            total = self.first_a[to_z, k, :, n].astype(F32) + self.part[k, to_z, y, a, n].astype(F32)
+            self.first_a[to_z, k, :, n] = total.astype(BF)
         self._copy(2, d).start()
         self._copy(1, d).wait()
         for k in range(2):
-            total = self.first_b[to_z, k].astype(F32) + self.part[x, to_z, k, b].astype(F32)
-            self.first_b[to_z, k] = total.astype(BF)
+            total = self.first_b[to_z, k, :, n].astype(F32) + self.part[x, to_z, k, b, n].astype(F32)
+            self.first_b[to_z, k, :, n] = total.astype(BF)
         self._copy(3, d).start()
+        if d in (1, 2):
+            self._start({2: 3, 1: 0}[d])
 
     def leave(self, d):
         z, y, c, x = place()
-        to_z = lax.rem(z + d, 4)
+        to_z, n = lax.rem(z + d, 4), self.lanes
         a, b = pl.ds(0, SPLIT), pl.ds(SPLIT, 128 - SPLIT)
         self._copy(2, d).wait()
-        self.second[to_z, a] = (self.second[to_z, a].astype(F32) + self.first_a[to_z, x].astype(F32)).astype(BF)
+        total = self.second[to_z, a, n].astype(F32) + self.first_a[to_z, x, :, n].astype(F32)
+        self.second[to_z, a, n] = total.astype(BF)
         self._copy(3, d).wait()
-        self.second[to_z, b] = (self.second[to_z, b].astype(F32) + self.first_b[to_z, y].astype(F32)).astype(BF)
+        total = self.second[to_z, b, n].astype(F32) + self.first_b[to_z, y, :, n].astype(F32)
+        self.second[to_z, b, n] = total.astype(BF)
         if d:
             self._copy(4, d).start()
 
@@ -527,13 +543,14 @@
         z, y, c, x = place()
         for d in (1, 2, 3):
             self._copy(4, d).wait()
+        n = self.lanes
 
         def add(i):
             rows = block(i, 64)
-            total = self.second[z, rows].astype(F32)
+            total = self.second[z, rows, n].astype(F32)
             for d in range(3):
-                total = total + self.third[d, rows].astype(F32)
-            self.total[rows] = total
+                total = total + self.third[d, rows, n].astype(F32)
+            self.total[rows, n] = total
 
         loop(2, add)
         for copy in self._core():
@@ -630,8 +647,8 @@
 
 
 class SmallScatter:
-    def __init__(self, part, near_c, near_x, near_y, near_z, send, recv):
-        self.part, self.near_c, self.near_x, self.near_y, self.near_z = part, near_c, near_x, near_y, near_z
+    def __init__(self, part, near_c, near_z, near, send, recv):
+        self.part, self.near_c, self.near_z, self.near = part, near_c, near_z, near
         self.send, self.recv = send, recv
 
     def _copy(self, k):
@@ -639,35 +656,35 @@
         send, recv = self.send.at[k], self.recv.at[k]
         if k == 0:
             return remote(self.part.at[1 - c], self.near_c, send, recv, at(z, y, 1 - c, x))
-        if k == 1:
-            return remote(self.near_c.at[1 - x], self.near_x, send, recv, at(z, y, c, 1 - x))
-        if k == 2:
-            return remote(self.near_x.at[1 - y], self.near_y, send, recv, at(z, 1 - y, c, x))
-        to = lax.rem(z + k - 2, 4)
-        return remote(self.near_y.at[to], self.near_z.at[k - 3], send, recv, at(to, y, c, x))
+        if k <= 3:
+            to = lax.rem(z + k, 4)
+            return remote(self.near_c.at[to], self.near_z.at[k - 1], send, recv, at(to, y, c, x))
+        to_x, to_y = ((1 - x, y), (x, 1 - y), (1 - x, 1 - y))[k - 4]
+        return remote(self.near_z.at[3, to_x, to_y], self.near.at[k - 4], send, recv, at(z, to_y, c, to_x))
 
     def start(self):
         self._copy(0).start()
 
-    def step(self, k):
-        z, y, c, x = place()
-        self._copy(k).wait()
-        if k == 0:
-            self.near_c[...] = self.near_c[...] + self.part[c]
-            self._copy(1).start()
-        elif k == 1:
-            self.near_x[...] = self.near_x[...] + self.near_c[x]
-            self._copy(2).start()
-        else:
-            self.near_y[...] = self.near_y[...] + self.near_x[y]
-            for j in (3, 4, 5):
-                self._copy(j).start()
+    def along(self):
+        z, y, c, x = place()
+        self._copy(0).wait()
+        self.near_c[...] = self.near_c[...] + self.part[c]
+        for k in (1, 2, 3):
+            self._copy(k).start()
+
+    def across(self):
+        z, y, c, x = place()
+        for k in (1, 2, 3):
+            self._copy(k).wait()
+        self.near_z[3] = self.near_c[z] + self.near_z[0] + self.near_z[1] + self.near_z[2]
+        for k in (4, 5, 6):
+            self._copy(k).start()
 
     def finish(self):
         z, y, c, x = place()
-        for j in (3, 4, 5):
-            self._copy(j).wait()
-        return self.near_y[z] + self.near_z[0] + self.near_z[1] + self.near_z[2]
+        for k in (4, 5, 6):
+            self._copy(k).wait()
+        return self.near_z[3, x, y] + self.near[0] + self.near[1] + self.near[2]
 
 
 class Pair:
@@ -765,7 +782,7 @@
 
 
 INPUTS = """lat_own grad_own wq wp wu wd ada cond q_bias v_bias p_bias d_bias u_bias a_bias"""
-OUTPUTS = """block_mine input_mine q_out p_out u_out d_out held_a held_b held_d
+OUTPUTS = """block_mine input_mine q_out p_out u_out d_out held_a held_b
     ada_out cond_out ada_bias_out bias_out"""
 GROUP = (2, 4, 2, 128, 1024)
 TOKENS = (1024, 1024)
@@ -786,13 +803,12 @@
     out.update(small=f(16, 128), small_full=f(2, 4, 2, 2, 16, 128), wide=v(128, 3072), silu=f(16, 128))
     out.update(part=f(4, 2, 2, 8, 512), near_c=f(4, 2, 8, 512), near_y=f(4, 8, 512), near_z=f(4, 8, 512))
     out.update(mods=f(2, 8, 512), vectors=f(16, 1024), up_bias=f(1, 4096), stats=f(8, 1024), columns=f(8, 1024))
-    out.update(up_sums=f(2, 1, 1024), sums=f(2, 1, 768), all_mods=f(4, 2, 2, 8, 512), tall=f(128, 512))
-    out.update(bias_part=f(2, 2, 2, 4, 2, 128), bias_c=f(2, 2, 4, 2, 128), bias_x=f(2, 4, 2, 128))
-    out.update(bias_y=f(4, 2, 128), bias_z=f(3, 2, 128), found=f(16, 128), other=f(16, 128))
-    out.update(spread_x=f(2, 2, 4, 1, 128), spread_c=f(2, 4, 1, 128), spread_y=f(2, 4, 1, 128))
-    out.update(spread_z=f(4, 2, 1, 128), picked=f(8, 128), picked_other=f(8, 128))
-    out.update(gather_send=dma((4, 24)), gather_recv=dma((4, 24)), gather_local=dma((4, 4)))
-    out.update(scatter_send=dma((3, 28)), scatter_recv=dma((3, 28)), pair_send=dma((4, 4)), pair_recv=dma((4, 4)))
+    out.update(up_sums=f(2, 1, 1024), sums=f(2, 1, 768), half_mods=f(4, 2, 2, 8, 512), all_mods=f(4, 2, 2, 8, 512), tall=f(128, 512))
+    out.update(bias_part=f(2, 4, 2, 2, 2, 128), bias_c=f(4, 2, 2, 2, 128), bias_z=f(4, 2, 2, 2, 128))
+    out.update(bias_near=f(3, 2, 128), found=f(2, 4, 2, 1, 128), found_c=f(4, 2, 1, 128), found_z=f(4, 2, 1, 128))
+    out.update(found_near=f(3, 4, 1, 128), picked=f(8, 128), picked_other=f(8, 128))
+    out.update(gather_send=dma((4, 28)), gather_recv=dma((4, 28)), gather_local=dma((4, 6)))
+    out.update(scatter_send=dma((4, 28)), scatter_recv=dma((4, 28)), pair_send=dma((4, 4)), pair_recv=dma((4, 4)))
     out.update(swap_send=dma((4, 2)), swap_recv=dma((4, 2)), swap_local=dma((4,)))
     out.update(small_send=dma((4, 8)), small_recv=dma((4, 8)), load_sem=dma((12,)), free=regular)
     return out
@@ -822,25 +838,38 @@
             own, full, lanes, self.gather_send.at[i], self.gather_recv.at[i], self.gather_local.at[i]
         )
         self.q = gather(
-            0, lambda h: [(self.wq.at[j, :, block(h, 256)], 256 * j, 256) for j in range(3)], self.buf_a, (0, 768)
+            0,
+            lambda h: [
+                (self.wq.at[j, :, block(2 * h + k, 128)], 256 + 384 * k + 128 * j, 128)
+                for k in range(2)
+                for j in range(3)
+            ],
+            self.buf_a,
+            (256, 768),
         )
-        self.p = gather(1, lambda h: [(self.wp.at[:, block(h, 256)], 768, 256)], self.buf_a, (768, 256))
+        self.p = gather(1, lambda h: [(self.wp.at[:, block(h, 256)], 0, 256)], self.buf_a, (0, 256))
         self.u = gather(2, lambda h: [(self.wu.at[:, block(h, 1024)], 0, 1024)], self.gu, (0, 1024))
-        self.d = gather(3, lambda h: [(self.wd.at[:, block(h, 1024)], 0, 1024)], self.held_d, (0, 1024))
+        self.d = gather(3, lambda h: [(self.wd.at[:, block(h, 1024)], 0, 1024)], self.buf_b, (0, 1024))
+        heads = lambda k: lambda h: [
+            (self.q_out.at[j, :, block(2 * h + k, 128)], 256 + 384 * k + 128 * j, 128) for j in range(3)
+        ]
         outs = (
             lambda h: [(self.d_out.at[:, block(h, 1024)], 0, 1024)],
             lambda h: [(self.u_out.at[:, block(h, 1024)], 0, 1024)],
-            lambda h: [(self.q_out.at[j, :, block(h, 256)], 256 * j, 256) for j in range(3)]
-            + [(self.p_out.at[:, block(h, 256)], 768, 256)],
+            lambda h: heads(0)(h) + [(self.p_out.at[:, block(h, 256)], 0, 256)],
+            heads(1),
         )
-        parts = (self.buf_d, self.buf_c, self.buf_d)
-        firsts = ((self.first_a0, self.first_b0), (self.first_a1, self.first_b1), (self.first_a0, self.first_b0))
+        firsts = ((self.first_a0, self.first_b0), (self.first_a1, self.first_b1))
         rest = ((self.second0, self.third0), (self.second1, self.third1), (self.second2, self.third2))
-        self.down, self.up, self.attn = [
-            Scatter(
-                parts[i], *firsts[i], *rest[i], self.total, outs[i], self.scatter_send.at[i], self.scatter_recv.at[i]
-            )
-            for i in range(3)
+        plan = (
+            (self.buf_d, firsts[0], rest[0], (0, 1024)),
+            (self.buf_c, firsts[1], rest[1], (0, 1024)),
+            (self.buf_d, firsts[0], rest[2], (0, 640)),
+            (self.buf_d, firsts[0], rest[2], (640, 384)),
+        )
+        self.down, self.up, self.near_heads, self.far_heads = [
+            Scatter(part, *first, *more, self.total, lanes, outs[i], self.scatter_send.at[i], self.scatter_recv.at[i])
+            for i, (part, first, more, lanes) in enumerate(plan)
         ]
         swaps = [(self.lat_own, self.lat), (self.grad_own, self.grad)]
         self.swap_lat, self.swap_grad = [
@@ -877,8 +906,8 @@
         for j in range(6):
             self.small[10 + j // 4 : 11 + j // 4, j % 4 * 32 : j % 4 * 32 + 32] = a_bias[j : j + 1, :]
         greet(partners())
+        little.start()
         q.start_core()
-        little.start()
         for group in (p, u, d):
             group.start_core()
         self.swap_lat.start()
@@ -886,13 +915,15 @@
         ada = [self.load(j, self.ada.at[j], self.wide.at[block(c, 64), pl.ds(j * 512, 512)]) for j in range(6)]
         for copy in ada:
             copy.start()
+        little.step((0,), (1, 2, 3))
         q.enter()
-        little.step((0,), (1, 2, 3))
+        p.enter()
         self.part[...] = jnp.zeros_like(self.part)
         little.step((1, 2, 3), (4,))
         for copy in ada:
             copy.wait()
         little.step((4,), (5,))
+        q.first()
         row = z * 2 + y
         lhs = [self.small_full[x, b // 4, b // 2 % 2, b % 2, pl.ds(row, 1), :] for b in range(16)]
         lhs = jnp.concatenate(lhs, 0)
@@ -904,14 +935,12 @@
         near_c, near_y, near_z = self.near_c, self.near_y, self.near_z
         first = remote(self.part.at[:, :, 1 - c], near_c, send.at[1, 0], recv.at[1, 0], at(z, y, 1 - c, x))
         first.start()
-        q.arrived(2)
         first.wait()
         for zz in range(4):
             for yy in range(2):
                 near_c[zz, yy] = near_c[zz, yy] + self.part[zz, yy, c]
         second = remote(near_c.at[:, 1 - y], near_y, send.at[1, 1], recv.at[1, 1], at(z, 1 - y, c, x))
         second.start()
-        q.turn(0)
         second.wait()
         for zz in range(4):
             near_y[zz] = near_y[zz] + near_c[zz, y]
@@ -922,7 +951,12 @@
                 remote(near_y.at[to], near_z.at[s - 1], send.at[1, 1 + s], recv.at[1, 1 + s], at(to, y, c, x))
             )
             thirds[-1].start()
+        u.enter()
+        d.enter()
+        q.turn(0)
+        q.arrived(2)
         q.arrived(1)
+        q.arrived(3)
         for copy in thirds:
             copy.wait()
         near_z[3] = near_y[z] + near_z[0] + near_z[1] + near_z[2]
@@ -932,7 +966,6 @@
         def _():
             fourth.start()
 
-        q.arrived(3)
         self.swap_lat.share()
         q.turn(2)
 
@@ -960,8 +993,10 @@
         for k in range(4):
             self.vectors[6 + k : 7 + k, :] = bias[k]
         q.turn(3)
-        p.enter()
-        u.enter()
+        p.first()
+        for k in (2, 1, 3):
+            p.arrived(k)
+        u.first()
         self.swap_lat.finish()
 
     def attend(self):
@@ -979,29 +1014,30 @@
 
         def project(i):
             b, quarter = i // 4, lax.rem(i, 4)
-            columns = pl.ds(pl.multiple_of(b * 512 + c * 256, 256), 256)
-            values = nn(self.attn_in[block(quarter, 256), :], flat(self.buf_a[b, :, :, :, 0:768]))
-            query = values[:, 0:256] + vectors[6:7, columns]
-            value = values[:, 512:768] + vectors[7:8, columns]
-            self.buf_b[b, quarter, :, :, 0:256] = query.astype(BF).reshape(2, 128, 256)
-            self.buf_b[b, quarter, :, :, 256:512] = values[:, 256:512].astype(BF).reshape(2, 128, 256)
-            self.buf_b[b, quarter, :, :, 512:768] = value.astype(BF).reshape(2, 128, 256)
+            values = nn(self.attn_in[block(quarter, 256), :], flat(self.buf_a[b, :, :, :, 256:1024]))
+            for k in range(6):
+                value = values[:, k * 128 : (k + 1) * 128]
+                if k % 3 != 1:
+                    columns = pl.ds(pl.multiple_of(b * 512 + c * 256 + k // 3 * 128, 128), 128)
+                    row = 6 if k % 3 == 0 else 7
+                    value = value + vectors[row : row + 1, columns]
+                self.buf_d[b, quarter, :, :, 256 + k * 128 : 384 + k * 128] = value.astype(BF).reshape(2, 128, 128)
 
         loop(8, project)
-        for k in (2, 1, 3):
-            p.arrived(k)
         for k in (0, 2, 1, 3):
             p.turn(k)
+        for k in (2, 1, 3):
+            u.arrived(k)
         lane = lax.broadcasted_iota(jnp.int32, (1, 128), 1)
         self.lse[...] = jnp.zeros_like(self.lse)
 
         def attend(i):
             pair, half = i // 2, lax.rem(i, 2)
             rows, zz = block(half, 512), pl.ds(half * 2, 2)
-            b, q_at = pair // 2, pl.multiple_of(lax.rem(pair, 2) * 128, 128)
-            queries = flat(self.buf_b[b, zz, :, :, pl.ds(q_at, 128)]) * BF(0.125)
-            keys = flat(self.buf_b[b, :, :, :, pl.ds(q_at + 256, 128)])
-            values = flat(self.buf_b[b, :, :, :, pl.ds(q_at + 512, 128)])
+            b, k, q_at = lax.rem(pair, 2), pair // 2, pl.multiple_of(256 + pair // 2 * 384, 128)
+            queries = flat(self.buf_d[b, zz, :, :, pl.ds(q_at, 128)]) * BF(0.125)
+            keys = flat(self.buf_d[b, :, :, :, pl.ds(q_at + 128, 128)])
+            values = flat(self.buf_d[b, :, :, :, pl.ds(q_at + 256, 128)])
             result = None
             logs = self.lse[rows, :]
             for h in range(2):
@@ -1012,39 +1048,31 @@
                 mixture = nn(exponent.astype(BF), values) * (1.0 / summed)
                 result = mixture if h == 0 else jnp.where(in_half(0), result, mixture)
                 logs = jnp.where(lane == pair * 2 + h, largest + jnp.log(summed), logs)
-            self.buf_b[b, zz, :, :, pl.ds(q_at + 768, 128)] = result.astype(BF).reshape(2, 2, 128, 128)
+            self.buf_d[b, zz, :, :, block(k, 128)] = result.astype(BF).reshape(2, 2, 128, 128)
             self.lse[rows, :] = logs
 
-            @pl.when(i == 1)
-            def _():
-                u.arrived(2)
-                u.arrived(1)
-                u.arrived(3)
-
-            @pl.when(i == 3)
-            def _():
-                u.turn(0)
-                d.enter()
-
-            @pl.when(i == 5)
-            def _():
-                u.turn(2)
-                u.turn(1)
-                u.turn(3)
-
-        loop(8, attend)
+        ticks = {
+            0: lambda: u.turn(0),
+            3: lambda: u.turn(2),
+            4: lambda: u.turn(1),
+            5: lambda: u.turn(3),
+        }
+        loop(8, attend, ticks)
+        d.first()
         p.finish()
         self.load(0, self.buf_a, self.held_a).start()
         pair = self.pairs[0]
 
         def out(i):
             zz = i
-            partial = nt(flat(self.buf_b[0, zz, :, :, 768:1024]), flat(self.buf_a[0, :, :, :, 768:1024]))
-            partial += nt(flat(self.buf_b[1, zz, :, :, 768:1024]), flat(self.buf_a[1, :, :, :, 768:1024]))
+            partial = nt(flat(self.buf_d[0, zz, :, :, 0:256]), flat(self.buf_a[0, :, :, :, 0:256]))
+            partial += nt(flat(self.buf_d[1, zz, :, :, 0:256]), flat(self.buf_a[1, :, :, :, 0:256]))
             pair.give(i, partial)
 
         loop(4, out)
-        self.load(1, self.buf_b, self.held_b).start()
+        self.load(1, self.buf_d, self.held_b).start()
+        for k in (2, 1, 3):
+            d.arrived(k)
         self.swap_grad.share()
 
         def residual(i):
@@ -1074,8 +1102,6 @@
             stats[1:2, :] += column_sum(g.astype(F32)) * mine_too
 
         loop(4, enter)
-        for k in (2, 1, 3):
-            d.arrived(k)
         u.finish()
         self.load(0, self.buf_a, self.held_a).wait()
         d.turn(0)
@@ -1088,32 +1114,23 @@
             active[b, quarter] = value.astype(BF).reshape(2, 128, 1024)
             slope[b, quarter] = gradient.astype(BF).reshape(2, 128, 1024)
 
-            @pl.when(i == 5)
-            def _():
-                d.turn(2)
-                d.turn(1)
-
-        loop(8, ascend)
-        d.turn(3)
+        loop(8, ascend, {3: lambda: d.turn(2), 6: lambda: d.turn(1)})
+        self.load(1, self.buf_d, self.held_b).wait()
 
         def down_gradient(i):
             b, half = i // 2, lax.rem(i, 2)
             value = tn(g_two[:, block(half, 512)], flat(active[b]))
             self.buf_d[b, pl.ds(half * 2, 2)] = value.astype(BF).reshape(2, 2, 128, 1024)
 
-        loop(4, down_gradient)
+        loop(4, down_gradient, {0: lambda: d.turn(3)})
         down.start()
         d.finish()
-        self.load(1, self.buf_b, self.held_b).wait()
-        load = self.load(2, self.held_d, wd)
-        load.start()
-        load.wait()
         pair, back = self.pairs[1], self.pairs[2]
 
         def descend(i):
             pair.give(i, nt(flat(active[0, i]), flat(wd[0])) + nt(flat(active[1, i]), flat(wd[1])))
 
-        loop(4, descend)
+        loop(4, descend, {1: lambda: down.turn(2)})
 
         def hidden_gradient(i):
             b, quarter = i // 4, lax.rem(i, 4)
@@ -1122,7 +1139,7 @@
             hidden_grad[b, quarter] = value.reshape(2, 128, 1024)
             self.up_sums[b] += column_sum(value.astype(F32))
 
-        loop(8, hidden_gradient)
+        loop(8, hidden_gradient, {1: lambda: down.turn(1), 7: lambda: down.turn(3)})
         self.load(3, self.held_b, self.buf_b).start()
 
         def leave(i):
@@ -1136,20 +1153,16 @@
         def descend_back(i):
             back.give(i, nt(flat(hidden_grad[0, i]), flat(gu[0])) + nt(flat(hidden_grad[1, i]), flat(gu[1])))
 
-        loop(4, descend_back)
-        down.turn(2)
-        down.turn(1)
+        loop(4, descend_back, {0: lambda: down.turn(0), 2: lambda: down.leave(2)})
 
         def up_gradient(i):
             b, half = i // 2, lax.rem(i, 2)
             value = tn(mlp_in[:, block(half, 512)], flat(hidden_grad[b]))
             up_grad[b, pl.ds(half * 2, 2)] = value.astype(BF).reshape(2, 2, 128, 1024)
 
-        loop(4, up_gradient)
+        loop(4, up_gradient, {0: lambda: down.leave(1), 2: lambda: down.leave(3)})
         self.load(4, self.held_a, self.buf_a).start()
         up.start()
-        down.turn(3)
-        down.turn(0)
 
         def residual(i):
             rows = block(i, 256)
@@ -1168,42 +1181,42 @@
             stats[5:6, :] += column_sum(g.astype(F32)) * mine_too
 
         loop(4, residual)
-        down.leave(2)
+        down.leave(0)
+        for to in (at(z, 1 - y, c, x), at(z, y, c, 1 - x)):
+            pl.semaphore_signal(self.free, inc=1, device_id=to, device_id_type=MESH)
 
     def attend_back(self):
         z, y, c, x = place()
-        vectors, stats, down, up, attn = self.vectors, self.stats, self.down, self.up, self.attn
+        vectors, stats, down, up = self.vectors, self.stats, self.down, self.up
+        near, far = self.near_heads, self.far_heads
         acts, g_one, heads_grad, sums = self.buf_b, self.mlp_in, self.heads_grad, self.sums
         weights = self.buf_a
         sums[...] = jnp.zeros_like(sums)
         self.load(3, self.held_b, self.buf_b).wait()
         self.load(4, self.held_a, self.buf_a).wait()
-        down.leave(1)
 
         def enter(i):
             b, half = i // 2, lax.rem(i, 2)
-            value = nn(g_one[block(half, 512), :], flat(weights[b, :, :, :, 768:1024]))
+            value = nn(g_one[block(half, 512), :], flat(weights[b, :, :, :, 0:256]))
             heads_grad[b, block(half, 512), :] = value.astype(BF)
 
         loop(4, enter)
 
         def proj_gradient(i):
             b, half = i // 2, lax.rem(i, 2)
-            value = tn(g_one[:, block(half, 512)], flat(acts[b, :, :, :, 768:1024]))
-            self.buf_d[b, pl.ds(half * 2, 2), :, :, 768:1024] = value.astype(BF).reshape(2, 2, 128, 256)
+            value = tn(g_one[:, block(half, 512)], flat(acts[b, :, :, :, 0:256]))
+            self.buf_d[b, pl.ds(half * 2, 2), :, :, 0:256] = value.astype(BF).reshape(2, 2, 128, 256)
 
         loop(4, proj_gradient)
-        down.leave(3)
         lane = lax.broadcasted_iota(jnp.int32, (1, 128), 1)
 
-        def attend(i):
-            pair, quarter = i // 4, lax.rem(i, 4)
-            rows = block(quarter, 256)
-            b, at_lane = pair // 2, pl.multiple_of(lax.rem(pair, 2) * 128, 128)
-            queries = flat(acts[b, quarter, :, :, pl.ds(at_lane, 128)]) * BF(0.125)
-            keys = flat(acts[b, :, :, :, pl.ds(at_lane + 256, 128)])
-            values = flat(acts[b, :, :, :, pl.ds(at_lane + 512, 128)])
-            grads = heads_grad[b, rows, pl.ds(at_lane, 128)]
+        def attend(i, k):
+            b, quarter = i // 4, lax.rem(i, 4)
+            rows, at_lane = block(quarter, 256), 256 + 384 * k
+            queries = flat(acts[b, quarter, :, :, at_lane : at_lane + 128]) * BF(0.125)
+            keys = flat(acts[b, :, :, :, at_lane + 128 : at_lane + 256])
+            values = flat(acts[b, :, :, :, at_lane + 256 : at_lane + 384])
+            grads = heads_grad[b, rows, k * 128 : (k + 1) * 128]
 
             @pl.when(quarter == 0)
             def _():
@@ -1213,7 +1226,7 @@
             result = None
             logs = self.lse[rows, :]
             for h in range(2):
-                log = jnp.sum(jnp.where(lane == pair * 2 + h, logs, 0.0), -1, keepdims=True)
+                log = jnp.sum(jnp.where(lane == (k * 2 + b) * 2 + h, logs, 0.0), -1, keepdims=True)
                 query = jnp.where(in_half(h), queries, jnp.zeros_like(queries))
                 grad = jnp.where(in_half(h), grads, jnp.zeros_like(grads))
                 probs = jnp.exp(nt(query, keys) - log)
@@ -1225,61 +1238,53 @@
                 self.key_total[...] += tn(score_grad, query)
                 self.value_total[...] += tn(probs.astype(BF), grad)
             result = (result * 0.125).astype(BF)
-            acts[b, quarter, :, :, pl.ds(at_lane, 128)] = result.reshape(2, 128, 128)
-            sums[b, :, pl.ds(at_lane, 128)] += column_sum(result.astype(F32))
+            acts[b, quarter, :, :, at_lane : at_lane + 128] = result.reshape(2, 128, 128)
+            sums[b, :, k * 128 : (k + 1) * 128] += column_sum(result.astype(F32))
 
             @pl.when(quarter == 3)
             def _():
                 total = self.key_total[...].astype(BF)
-                acts[b, :, :, :, pl.ds(at_lane + 256, 128)] = total.reshape(4, 2, 128, 128)
+                acts[b, :, :, :, at_lane + 128 : at_lane + 256] = total.reshape(4, 2, 128, 128)
                 total = self.value_total[...].astype(BF)
-                acts[b, :, :, :, pl.ds(at_lane + 512, 128)] = total.reshape(4, 2, 128, 128)
-                sums[b, :, pl.ds(at_lane + 512, 128)] = column_sum(total.astype(F32))
-
-            @pl.when(i == 1)
-            def _():
-                down.leave(0)
-                for to in (at(z, 1 - y, c, x), at(z, y, c, 1 - x)):
-                    pl.semaphore_signal(self.free, inc=1, device_id=to, device_id_type=MESH)
-                self.swap_block.start()
-
-            @pl.when(i == 5)
-            def _():
-                up.turn(2)
-                up.turn(1)
-
-            @pl.when(i == 9)
-            def _():
-                up.turn(3)
-                up.turn(0)
-                down.last()
-
-            @pl.when(i == 13)
-            def _():
-                up.leave(2)
-                up.leave(1)
-
-        loop(16, attend)
-        up.leave(3)
-        up.leave(0)
-
-        def qkv_gradient(i):
+                acts[b, :, :, :, at_lane + 256 : at_lane + 384] = total.reshape(4, 2, 128, 128)
+                sums[b, :, 512 + k * 128 : 640 + k * 128] = column_sum(total.astype(F32))
+
+        def qkv_gradient(i, k):
             b, half = i // 2, lax.rem(i, 2)
-            value = tn(self.attn_in[:, block(half, 512)], flat(acts[b, :, :, :, 0:768]))
-            self.buf_d[b, pl.ds(half * 2, 2), :, :, 0:768] = value.astype(BF).reshape(2, 2, 128, 768)
-
-        loop(4, qkv_gradient)
+            lanes = slice(256 + 384 * k, 640 + 384 * k)
+            value = tn(self.attn_in[:, block(half, 512)], flat(acts[b, :, :, :, lanes]))
+            self.buf_d[b, pl.ds(half * 2, 2), :, :, lanes] = value.astype(BF).reshape(2, 2, 128, 384)
+
+        ticks = {
+            0: lambda: up.turn(2),
+            2: lambda: up.turn(1),
+            5: lambda: up.turn(3),
+        }
+        loop(8, lambda i: attend(i, 0), ticks)
+        up.turn(0)
+        loop(4, lambda i: qkv_gradient(i, 0))
+        pl.semaphore_wait(self.free, 2)
+        near.start()
+        up.leave(2)
+        ticks = {
+            0: lambda: down.last(),
+            1: lambda: up.leave(1),
+            2: lambda: near.turn(2),
+            3: lambda: up.leave(3),
+            4: lambda: near.turn(1),
+            5: lambda: up.leave(0),
+            6: lambda: self.swap_block.start(),
+            7: lambda: near.turn(3),
+        }
+        loop(8, lambda i: attend(i, 1), ticks)
+        pair = self.pairs[3]
+
+        def descend(i):
+            partial = nt(flat(acts[0, i, :, :, 256:1024]), flat(weights[0, :, :, :, 256:1024]))
+            pair.give(i, partial + nt(flat(acts[1, i, :, :, 256:1024]), flat(weights[1, :, :, :, 256:1024])))
+
+        loop(4, descend, {1: lambda: near.turn(0), 3: lambda: near.leave(2)})
         down.finish()
-        pl.semaphore_wait(self.free, 2)
-        attn.start()
-        pair = self.pairs[3]
-
-        def descend(i):
-            partial = nt(flat(acts[0, i, :, :, 0:768]), flat(weights[0, :, :, :, 0:768]))
-            pair.give(i, partial + nt(flat(acts[1, i, :, :, 0:768]), flat(weights[1, :, :, :, 0:768])))
-
-        loop(4, descend)
-        up.last()
 
         def leave(i):
             rows = block(i, 256)
@@ -1292,27 +1297,22 @@
             self.branch_one[rows, :] = (self.mid[rows, :] + scale * dn).astype(BF)
 
         loop(4, leave)
+        self.begin_end()
+        loop(4, lambda i: qkv_gradient(i, 1), {1: lambda: near.leave(1)})
+        far.start()
         self.swap_input.start()
-        self.swap_block.finish()
-
-    def end(self):
-        z, y, c, x = place()
-        stats, sums, up_sums, attn, up = self.stats, self.sums, self.up_sums, self.attn, self.up
-        send, recv, mods = self.small_send, self.small_recv, self.all_mods
+        up.last()
+
+    def begin_end(self):
+        z, y, c, x = place()
+        stats, sums, up_sums = self.stats, self.sums, self.up_sums
         rows = [stats[k : k + 1, :] for k in (6, 7, 4, 2, 3, 0)]
         for j in range(6):
             for h in range(2):
                 self.mods[h, j : j + 1, :] = rows[j][:, h * 512 : (h + 1) * 512]
-        far = remote(self.mods.at[1 - x], mods.at[z, y, 1 - c], send.at[2, 0], recv.at[2, 0], at(z, y, 1 - c, 1 - x))
-
-        @pl.when(c != x)
-        def _():
-            far.start()
-
-        @pl.when(c == x)
-        def _():
-            mods[z, y, c] = self.mods[x]
-
+        self.half_mods[z, y, x] = self.mods[c]
+        for d in (1, 2, 3):
+            self._mods(d).start()
         columns, bias_part = self.columns, self.bias_part
         columns[...] = jnp.zeros_like(columns)
         bias_part[...] = jnp.zeros_like(bias_part)
@@ -1325,42 +1325,66 @@
         pieces = narrow(columns[0:1, :], 0) + narrow(columns[1:2, :], 1)
         pieces = pieces + narrow(columns[2:3, :], 2) + narrow(columns[3:4, :], 3)
         for k, (zz, yy, cc, xx) in enumerate(devices()):
-            bias_part[cc, xx, yy, zz, 0:1, :] = pieces[k : k + 1, :]
+            bias_part[cc, zz, xx, yy, 0:1, :] = pieces[k : k + 1, :]
         for b in range(2):
             for i in range(8):
-                bias_part[i // 2 % 2, i % 2, i // 4, b * 2 + c, 1:2, :] = up_sums[b, :, i * 128 : (i + 1) * 128]
-        bias = SmallScatter(
-            bias_part, self.bias_c, self.bias_x, self.bias_y, self.bias_z, self.small_send.at[0], self.small_recv.at[3]
+                bias_part[i // 2 % 2, b * 2 + c, i % 2, i // 4, 1:2, :] = up_sums[b, :, i * 128 : (i + 1) * 128]
+        self.bias = SmallScatter(
+            bias_part, self.bias_c, self.bias_z, self.bias_near, self.small_send.at[0], self.small_recv.at[3]
         )
-        bias.start()
+        self.bias.start()
+        for d in (1, 2, 3):
+            self._mods(d).wait()
+        self._across(lambda copy: copy.start())
+        self.bias.along()
+
+    def _mods(self, d):
+        z, y, c, x = place()
+        spot = self.half_mods.at[z, y, x]
+        return remote(
+            spot, spot, self.small_send.at[2, d], self.small_recv.at[2, d], at(lax.rem(z + d, 4), y, c, x)
+        )
+
+    def _across(self, act):
+        z, y, c, x = place()
+        spot = self.half_mods.at[:, y, x]
+        copy = lambda k, to: remote(spot, spot, self.small_send.at[2, k], self.small_recv.at[2, k], to)
+
+        @pl.when(c == x)
+        def _():
+            act(copy(4, at(z, 1 - y, c, x)))
 
         @pl.when(c != x)
         def _():
-            far.wait()
-
-        spot = mods.at[z, y, c]
-        core = remote(spot, spot, send.at[2, 1], recv.at[2, 1], at(z, y, 1 - c, x))
-        core.start()
-        bias.step(0)
-        core.wait()
-        spot_y = mods.at[z, y]
-        across = remote(spot_y, spot_y, send.at[2, 2], recv.at[2, 2], at(z, 1 - y, c, x))
-        across.start()
-        bias.step(1)
-        attn.turn(2)
-        across.wait()
-        spot_z = mods.at[z]
-        along = [
-            remote(spot_z, spot_z, send.at[2, 2 + k], recv.at[2, 2 + k], at(lax.rem(z + k, 4), y, c, x))
-            for k in (1, 2, 3)
-        ]
-        for copy in along:
-            copy.start()
-        bias.step(2)
-        attn.turn(1)
+            act(copy(5, at(z, y, c, 1 - x)))
+            act(copy(6, at(z, 1 - y, c, 1 - x)))
+
+    def end(self):
+        z, y, c, x = place()
+        up, near, far, mods, bias = self.up, self.near_heads, self.far_heads, self.all_mods, self.bias
+        send, recv = self.small_send, self.small_recv
+        spot = self.half_mods.at[:, y, x]
+
+        @pl.when(c == x)
+        def _():
+            remote(spot, spot, send.at[2, 4], recv.at[2, 4], at(z, 1 - y, c, x)).wait()
+            remote(spot, spot, send.at[2, 5], recv.at[2, 5], at(z, y, c, 1 - x)).wait_recv()
+            remote(spot, spot, send.at[2, 6], recv.at[2, 6], at(z, 1 - y, c, 1 - x)).wait_recv()
+            share = remote(self.half_mods, mods, send.at[2, 7], recv.at[2, 7], at(z, y, 1 - c, x))
+            share.start()
+            keep = self.load(5, self.half_mods, mods)
+            keep.start()
+            keep.wait()
+            share.wait_send()
+
+        @pl.when(c != x)
+        def _():
+            remote(spot, spot, send.at[2, 5], recv.at[2, 5], at(z, y, c, 1 - x)).wait_send()
+            remote(spot, spot, send.at[2, 6], recv.at[2, 6], at(z, 1 - y, c, 1 - x)).wait_send()
+            remote(self.half_mods, mods, send.at[2, 7], recv.at[2, 7], at(z, y, 1 - c, x)).wait_recv()
+
+        bias.across()
         silu_rows = self.silu[...].astype(BF)
-        for copy in along:
-            copy.wait()
         total = jnp.zeros((16, 128), F32)
         bias_rows = []
         for j in range(6):
@@ -1371,59 +1395,62 @@
             self.ada_out[j] = self.tall[block(c, 64), :]
             total = total + nt(high, weights) + nt(low, weights)
             bias_rows.append(column_sum(values))
-        self.found[...] = total
+        found, found_c, found_z, found_near = self.found, self.found_c, self.found_z, self.found_near
+        for b in range(16):
+            found[b % 2, b // 4, b // 2 % 2] = total[b : b + 1, :]
+        core = remote(found.at[1 - c], found_c, send.at[3, 0], recv.at[1, 0], at(z, y, 1 - c, x))
+        core.start()
+        far.turn(2)
         group = (lax.rem(z, 2) * 2 + y) * 2 + c
         source = lax.broadcasted_iota(jnp.int32, (512, 128), 0)
         target = lax.broadcasted_iota(jnp.int32, (512, 128), 1)
         chosen = jnp.where((source == group * 64 + target) & (target < 64), 1.0, 0.0).astype(BF)
         self.picked[...] = exact_nn(jnp.concatenate(bias_rows + [jnp.zeros((2, 512), F32)], 0), chosen)
-        first = [
-            remote(self.found, self.other, send.at[3, 0], recv.at[1, 0], at(z, y, c, 1 - x)),
-            remote(self.picked, self.picked_other, send.at[3, 1], recv.at[1, 1], at(z, y, c, 1 - x)),
-        ]
-        for copy in first:
-            copy.start()
-        attn.turn(3)
-        for copy in first:
-            copy.wait()
-        self.ada_bias_out[...] = jnp.where(z // 2 == x, self.picked[...], self.picked_other[...])
-        total = self.found[...] + self.other[...]
-        spread_x, spread_c, spread_y, spread_z = self.spread_x, self.spread_c, self.spread_y, self.spread_z
-        for b in range(16):
-            spread_x[b % 2, b // 2 % 2, b // 4] = total[b : b + 1, :]
-        second = remote(spread_x.at[1 - c], spread_c, send.at[3, 2], recv.at[1, 2], at(z, y, 1 - c, x))
-        second.start()
-        self.bias_out[...] = bias.finish()
-        attn.turn(0)
-        second.wait()
-        spread_c[...] = spread_c[...] + spread_x[c]
-        third = remote(spread_c.at[1 - y], spread_y.at[y], send.at[3, 3], recv.at[1, 3], at(z, 1 - y, c, x))
-        third.start()
-        spread_y[y] = spread_c[y]
-        attn.leave(2)
-        third.wait()
-        fourth = []
+        swap = remote(self.picked, self.picked_other, send.at[3, 7], recv.at[1, 7], at(z, y, c, 1 - x))
+        swap.start()
+        core.wait()
+        found_c[...] = found_c[...] + found[c]
+        along = []
         for k in (1, 2, 3):
             to = lax.rem(z + k, 4)
-            fourth.append(
-                remote(spread_y.at[:, to], spread_z.at[z], send.at[3, 3 + k], recv.at[1, 3 + k], at(to, y, c, x))
+            along.append(remote(found_c.at[to], found_z.at[z], send.at[3, k], recv.at[1, k], at(to, y, c, x)))
+            along[-1].start()
+        found_z[z] = found_c[z]
+        near.leave(3)
+        far.turn(1)
+        near.leave(0)
+        for copy in along:
+            copy.wait()
+        across = []
+        for k, (to_y, to_x) in enumerate(((y, 1 - x), (1 - y, x), (1 - y, 1 - x))):
+            across.append(
+                remote(found_z.at[:, to_y], found_near.at[k], send.at[3, 4 + k], recv.at[1, 4 + k], at(z, to_y, c, to_x))
             )
-            fourth[-1].start()
-        spread_z[z] = spread_y[:, z]
-        attn.leave(1)
-        for copy in fourth:
+            across[-1].start()
+        far.turn(3)
+        far.turn(0)
+        up.finish()
+        near.last()
+        far.leave(2)
+        far.leave(1)
+        for copy in across:
             copy.wait()
+        swap.wait()
+        self.bias_out[...] = bias.finish()
+        self.ada_bias_out[...] = jnp.where(z // 2 == x, self.picked[...], self.picked_other[...])
+        same, other = found_z[:, y] + found_near[0], found_near[1] + found_near[2]
+        rows = [jnp.where(y == b % 2, same[b // 2], other[b // 2]) for b in range(8)]
         v = self.cond[...].astype(F32)
         v = jnp.concatenate([v[:, k * 128 : (k + 1) * 128] for k in range(8)], 0)
         gate = 1.0 / (1.0 + jnp.exp(-v))
-        row = jnp.concatenate([spread_z[b // 2, b % 2] for b in range(8)], 0)
-        self.cond_out[...] = row * gate * (1.0 + v * (1.0 - gate))
-        attn.leave(3)
-        attn.leave(0)
-        up.finish()
-        attn.last()
+        self.cond_out[...] = jnp.concatenate(rows, 0) * gate * (1.0 + v * (1.0 - gate))
+        far.leave(3)
+        far.leave(0)
+        near.finish()
+        far.last()
+        self.swap_block.finish()
         self.swap_input.finish()
-        attn.finish()
+        far.finish()
 
 
 def on_device_pairs(
@@ -1450,10 +1477,10 @@
     results = pl.pallas_call(
         pairs_kernel,
         out_shape=[rows, rows, out(3, 64, 512), out(64, 512), out(64, 2048), out(64, 2048)]
-        + [group] * 3
+        + [group] * 2
         + [out(6, 64, 512), out(8, 128), out(8, 128), out(2, 128)],
         in_specs=[IN_ANY] * 7 + [IN_VMEM] * 7,
-        out_specs=[IN_ANY] * 9 + [IN_VMEM] * 4,
+        out_specs=[IN_ANY] * 8 + [IN_VMEM] * 4,
         scratch_shapes=list(scratch().values()),
         compiler_params=pltpu.CompilerParams(
             collective_id=0, has_side_effects=True, vmem_limit_bytes=63 * MIB
@@ -1463,7 +1490,7 @@
         latents_in.reshape(512, 1024), grad_out.reshape(512, 1024), qkv_weight.transpose(1, 0, 2), proj_weight.T,
         up_weight, down_weight.T, ada_weight.transpose(1, 0, 2), condition, *small, ada_bias,
     )
-    block_mine, input_mine, q_out, p_out, u_out, d_out, _, _, _, ada_out, cond_out, ada_bias_out, bias_out = results
+    block_mine, input_mine, q_out, p_out, u_out, d_out, _, _, ada_out, cond_out, ada_bias_out, bias_out = results
     return (
         block_mine.reshape(512, 1, 1024),
         input_mine.astype(F32).reshape(512, 1, 1024),

time: 349 us -> 323 us (0.926)
  Pallas kernels: 333 us -> 307 us
    pallas_call x1, Pallas kernels: 333 us -> 307 us  [on_device_pairs(): pl.pallas_call(pairs_kernel, out_shape=[rows, rows, out(3, 64, 512), out(...]
where the time goes in v4:
time: 323 us
  Pallas kernels  307 us (95%)
  local copies, waits for them, and re-layouts  13.6 us (4%)
    pallas_call x1, Pallas kernels, on_device_pairs(): pl.pallas_call(pairs_kernel, out_shape=[rows, rows, out(3, 64, 512), out(...  307 us
    unnamed x19, local copies, waits for them, and re-layouts  8.53 us

profile of v4, /device:TPU:0, one launch (start us, length us, event | category | flops | bytes accessed | tf_op | source)
XLA Modules:
  0.0 323.0 jit_solution(16580265641759611605)
XLA Ops:
  0.7 307.3 %dit_block.1 = (bf16[512,1024]{1,0:T(8,128)(2,1)}, bf16[512,1024]{1,0:T(8,128)(2,1)}, f32[3,64,512]{2,1,0:T(8,128)}, f32[64,512]{1,0:T(8,128)}, f32[64,2048]{1,0...) custom-call(bf16[512,1024]{1,0:T(8,128)(2,1)} %bitcast.31, ...), custom_call_target="tpu_custom_call" | custom-call | tf_op jit(solution)/shard_map/dit_block/pallas_call | solution.py:1477
  307.9 1.3 constant_dynamic-slice_fusion
  309.3 1.3 constant_dynamic-slice_fusion.1
  310.5 1.4 slice_bitcast_fusion
  311.9 1.1 slice_bitcast_fusion.1
  313.0 1.5 bitcast_convert_fusion
  314.5 0.0 copy-start
  314.5 3.5 %copy.28 = f32[512,1,1024]{2,1,0:T(1,128)} copy(f32[512,1,1024]{2,0,1:T(8,128)S(1)} %bitcast_convert_fusion) | data formatting | bytes 4194304
  318.0 0.0 copy-start.4
  318.0 0.0 copy-start.5
  318.0 0.0 copy-start.3
  318.0 0.0 copy-done
  318.0 0.0 copy-start.2
  318.0 1.0 copy.35
  319.0 0.2 copy-done.4
  319.2 0.0 copy-start.1
  319.2 0.7 copy.36
  319.9 0.0 copy-done.5
  319.9 0.7 copy.37
  320.6 0.0 copy-done.3
  320.6 0.8 copy.38
  321.4 0.0 copy-done.2
  321.4 0.8 copy.39
  322.1 0.0 copy-done.1
  322.2 0.9 copy.40
Async XLA Ops:
  314.5 3.5 %copy-start = (bf16[512,1024]{1,0:T(8,128)(2,1)S(1)}, bf16[512,1024]{1,0:T(8,128)(2,1)}, u32[]{:S(2)}) copy-start(bf16[512,1024]{1,0:T(8,128)(2,1)} %get-tuple-element.24) | copy-start | bytes 3145732
  318.0 1.2 copy-start.4
  318.0 1.9 copy-start.5
  318.0 2.6 copy-start.3
  318.0 3.4 %copy-start.2 = (f32[64,2048]{1,0:T(8,128)S(1)}, f32[64,2048]{1,0:T(8,128)}, u32[]{:S(2)}) copy-start(f32[64,2048]{1,0:T(8,128)} %get-tuple-element.30) | copy-start | bytes 1572868
  319.2 3.0 copy-start.1

commit v5 on v4

--- a/solution.py
+++ b/solution.py
@@ -355,7 +355,9 @@
 MIB = 2**20
 IN_VMEM = pl.BlockSpec(memory_space=pltpu.VMEM)
 IN_ANY = pl.BlockSpec(memory_space=ANY)
-SPLIT = 80
+ROWS_A, ROWS_B, ROWS_W = (0, 64), (64, 48), (112, 16)
+ROWS_Z = 112
+FIRST = ((0, 80), (80, 48), None)
 
 
 def place():
@@ -407,8 +409,8 @@
 
 
 class Gather:
-    def __init__(self, own, full, lanes, send, recv, local):
-        self.own, self.full, self.lanes = own, full, pl.ds(*lanes)
+    def __init__(self, own, full, lanes, send, recv, local, rows=(ROWS_A, ROWS_B, ROWS_W)):
+        self.own, self.full, self.lanes, self.rows = own, full, pl.ds(*lanes), rows
         self.send, self.recv, self.local = send, recv, local
 
     def _core(self):
@@ -422,30 +424,43 @@
 
     def _copy(self, kind, d):
         z, y, c, x = place()
-        a, b, from_z = pl.ds(0, SPLIT), pl.ds(SPLIT, 128 - SPLIT), lax.rem(z - d + 4, 4)
+        a, b, w = [pl.ds(*rows) if rows else None for rows in self.rows]
+        from_z = lax.rem(z - d + 4, 4)
+        to_x, to_y, to_z = at(z, y, c, 1 - x), at(z, 1 - y, c, x), at(lax.rem(z + d, 4), y, c, x)
         if kind == 0:
-            spot, to = self.full.at[x, z, y, :, self.lanes], at(lax.rem(z + d, 4), y, c, x)
+            spot, to = self.full.at[x, z, y, pl.ds(0, sum(self.rows[1])), self.lanes], to_z
         elif kind == 1:
-            spot, to = self.full.at[x, from_z, y, a, self.lanes], at(z, y, c, 1 - x)
+            spot, to = self.full.at[x, from_z, y, a, self.lanes], to_x
         elif kind == 2:
-            spot, to = self.full.at[x, from_z, y, b, self.lanes], at(z, 1 - y, c, x)
+            spot, to = self.full.at[x, from_z, y, b, self.lanes], to_y
         elif kind == 3:
-            spot, to = self.full.at[:, from_z, y, a, self.lanes], at(z, 1 - y, c, x)
+            spot, to = self.full.at[:, from_z, y, a, self.lanes], to_y
+        elif kind == 4:
+            spot, to = self.full.at[x, from_z, :, b, self.lanes], to_x
+        elif kind == 5:
+            spot, to = self.full.at[:, z, :, w, self.lanes], to_z
+        elif d == 0:
+            spot, to = self.full.at[x, z, y, w, self.lanes], to_x
         else:
-            spot, to = self.full.at[x, from_z, :, b, self.lanes], at(z, y, c, 1 - x)
+            spot, to = self.full.at[:, z, y, w, self.lanes], to_y
         return remote(spot, spot, self.send.at[8 + 4 * kind + d], self.recv.at[8 + 4 * kind + d], to)
 
     def start_core(self):
         for copy in self._core():
             copy.start()
 
-    def enter(self):
+    def enter(self, along=(2, 1, 3)):
         for copy in self._core():
             copy.wait()
-        for d in (2, 1, 3):
+        self.pass_on(along)
+
+    def pass_on(self, along):
+        for d in along:
             self._copy(0, d).start()
 
     def first(self):
+        if self.rows[2]:
+            self._copy(6, 0).start()
         self._copy(1, 0).start()
         self._copy(2, 0).start()
 
@@ -455,26 +470,37 @@
         self._copy(2, d).start()
 
     def turn(self, d):
+        if self.rows[2] and d == 0:
+            self._copy(6, 0).wait()
+            self._copy(6, 1).start()
         self._copy(1, d).wait()
         self._copy(3, d).start()
         self._copy(2, d).wait()
         self._copy(4, d).start()
+        if self.rows[2] and d == 2:
+            self._copy(6, 1).wait()
+            for k in (2, 1, 3):
+                self._copy(5, k).start()
 
     def finish(self):
         for d in range(4):
             self._copy(3, d).wait()
             self._copy(4, d).wait()
+        if self.rows[2]:
+            for d in (2, 1, 3):
+                self._copy(5, d).wait()
 
 
 class Scatter:
-    def __init__(self, part, first_a, first_b, second, third, total, lanes, out, send, recv):
+    def __init__(self, part, first_a, first_b, second, third, wide_z, wide_y, wide_x, total, lanes, out, send, recv):
         self.part, self.first_a, self.first_b = part, first_a, first_b
+        self.wide_z, self.wide_y, self.wide_x = wide_z, wide_y, wide_x
         self.second, self.third, self.total, self.out = second, third, total, out
         self.lanes, self.send, self.recv = pl.ds(*lanes), send, recv
 
     def _copy(self, kind, d):
         z, y, c, x = place()
-        a, b, n, to_z = pl.ds(0, SPLIT), pl.ds(SPLIT, 128 - SPLIT), self.lanes, lax.rem(z + d, 4)
+        a, b, w, n, to_z = pl.ds(*ROWS_A), pl.ds(*ROWS_B), pl.ds(*ROWS_W), self.lanes, lax.rem(z + d, 4)
         send, recv = self.send.at[4 * kind + d], self.recv.at[4 * kind + d]
         to_x, to_y = at(z, y, c, 1 - x), at(z, 1 - y, c, x)
         if kind == 0:
@@ -485,7 +511,13 @@
             return remote(self.first_a.at[to_z, 1 - x, :, n], self.second.at[to_z, a, n], send, recv, to_x)
         if kind == 3:
             return remote(self.first_b.at[to_z, 1 - y, :, n], self.second.at[to_z, b, n], send, recv, to_y)
-        return remote(self.second.at[to_z, :, n], self.third.at[d - 1, :, n], send, recv, at(to_z, y, c, x))
+        if kind == 4:
+            return remote(self.second.at[to_z, :, n], self.third.at[d - 1, :, n], send, recv, at(to_z, y, c, x))
+        if kind == 5:
+            return remote(self.part.at[:, to_z, :, w, n], self.wide_z.at[d - 1, :, :, :, n], send, recv, at(to_z, y, c, x))
+        if d == 0:
+            return remote(self.wide_z.at[0, :, 1 - y, :, n], self.wide_y.at[:, :, n], send, recv, to_y)
+        return remote(self.wide_y.at[1 - x, :, n], self.wide_x.at[:, n], send, recv, to_x)
 
     def _core(self):
         z, y, c, x = place()
@@ -494,11 +526,11 @@
             lanes = pl.ds(first, width)
             copies.append(
                 remote(
-                    self.total.at[block(1 - c, 64), lanes], target, self.send.at[20 + i], self.recv.at[20 + i],
+                    self.total.at[block(1 - c, 64), lanes], target, self.send.at[28 + i], self.recv.at[28 + i],
                     at(z, y, 1 - c, x),
                 )
             )
-            copies.append(pltpu.make_async_copy(self.total.at[block(c, 64), lanes], target, self.send.at[24 + i]))
+            copies.append(pltpu.make_async_copy(self.total.at[block(c, 64), lanes], target, self.send.at[32 + i]))
         return copies
 
     def _start(self, d):
@@ -506,13 +538,15 @@
         self._copy(1, d).start()
 
     def start(self):
+        for d in (2, 1, 3):
+            self._copy(5, d).start()
         self._start(2)
         self._start(1)
 
     def turn(self, d):
         z, y, c, x = place()
         to_z, n = lax.rem(z + d, 4), self.lanes
-        a, b = pl.ds(0, SPLIT), pl.ds(SPLIT, 128 - SPLIT)
+        a, b, w = pl.ds(*ROWS_A), pl.ds(*ROWS_B), pl.ds(*ROWS_W)
         self._copy(0, d).wait()
         for k in range(2):
             total = self.first_a[to_z, k, :, n].astype(F32) + self.part[k, to_z, y, a, n].astype(F32)
@@ -525,11 +559,33 @@
         self._copy(3, d).start()
         if d in (1, 2):
             self._start({2: 3, 1: 0}[d])
+        elif d == 0:
+            self._fold_z()
+
+    def _fold_z(self):
+        z, y, c, x = place()
+        n, w = self.lanes, pl.ds(*ROWS_W)
+        for k in (2, 1, 3):
+            self._copy(5, k).wait()
+        for k in range(2):
+            total = self.part[k, z, :, w, n].astype(F32)
+            for s in range(3):
+                total = total + self.wide_z[s, k, :, :, n].astype(F32)
+            self.wide_z[0, k, :, :, n] = total.astype(BF)
+        self._copy(6, 0).start()
+
+    def _fold_y(self):
+        z, y, c, x = place()
+        n = self.lanes
+        self._copy(6, 0).wait()
+        total = self.wide_y[:, :, n].astype(F32) + self.wide_z[0, :, y, :, n].astype(F32)
+        self.wide_y[:, :, n] = total.astype(BF)
+        self._copy(6, 1).start()
 
     def leave(self, d):
         z, y, c, x = place()
         to_z, n = lax.rem(z + d, 4), self.lanes
-        a, b = pl.ds(0, SPLIT), pl.ds(SPLIT, 128 - SPLIT)
+        a, b = pl.ds(*ROWS_A), pl.ds(*ROWS_B)
         self._copy(2, d).wait()
         total = self.second[to_z, a, n].astype(F32) + self.first_a[to_z, x, :, n].astype(F32)
         self.second[to_z, a, n] = total.astype(BF)
@@ -538,21 +594,22 @@
         self.second[to_z, b, n] = total.astype(BF)
         if d:
             self._copy(4, d).start()
+        if d == 1:
+            self._fold_y()
 
     def last(self):
         z, y, c, x = place()
+        n, w = self.lanes, pl.ds(*ROWS_W)
+        self._copy(6, 1).wait()
+        self.total[w, n] = self.wide_x[:, n].astype(F32) + self.wide_y[x, :, n].astype(F32)
         for d in (1, 2, 3):
             self._copy(4, d).wait()
-        n = self.lanes
-
-        def add(i):
-            rows = block(i, 64)
+
+        for rows in (pl.ds(*ROWS_A), pl.ds(*ROWS_B)):
             total = self.second[z, rows, n].astype(F32)
             for d in range(3):
                 total = total + self.third[d, rows, n].astype(F32)
             self.total[rows, n] = total
-
-        loop(2, add)
         for copy in self._core():
             copy.start()
 
@@ -795,20 +852,22 @@
     out.update(mlp_in=v(*TOKENS), g_two=v(*TOKENS), mine=v(*TOKENS), theirs_a=v(*TOKENS), theirs_b=v(*TOKENS))
     out.update(buf_a=v(*GROUP), buf_b=v(*GROUP), gu=v(*GROUP), buf_c=v(*GROUP), buf_d=v(*GROUP))
     for i in range(2):
-        out[f"first_a{i}"], out[f"first_b{i}"] = v(4, 2, SPLIT, 1024), v(4, 2, 128 - SPLIT, 1024)
+        out[f"first_a{i}"], out[f"first_b{i}"] = v(4, 2, ROWS_A[1], 1024), v(4, 2, ROWS_B[1], 1024)
     for i in range(3):
-        out[f"second{i}"], out[f"third{i}"] = v(4, 128, 1024), v(3, 128, 1024)
+        out[f"second{i}"], out[f"third{i}"] = v(4, ROWS_Z, 1024), v(3, ROWS_Z, 1024)
+        out[f"wide_z{i}"], out[f"wide_y{i}"] = v(3, 2, 2, ROWS_W[1], 1024), v(2, ROWS_W[1], 1024)
+        out[f"wide_x{i}"] = v(ROWS_W[1], 1024)
     out.update(total=f(128, 1024), heads_grad=v(2, 1024, 256), lse=f(1024, 128))
     out.update(key_total=f(1024, 128), value_total=f(1024, 128))
     out.update(small=f(16, 128), small_full=f(2, 4, 2, 2, 16, 128), wide=v(128, 3072), silu=f(16, 128))
-    out.update(part=f(4, 2, 2, 8, 512), near_c=f(4, 2, 8, 512), near_y=f(4, 8, 512), near_z=f(4, 8, 512))
+    out.update(part=f(2, 4, 2, 8, 512), near_c=f(4, 2, 8, 512), near_z=f(4, 2, 8, 512), near_y=f(2, 8, 512))
     out.update(mods=f(2, 8, 512), vectors=f(16, 1024), up_bias=f(1, 4096), stats=f(8, 1024), columns=f(8, 1024))
     out.update(up_sums=f(2, 1, 1024), sums=f(2, 1, 768), half_mods=f(4, 2, 2, 8, 512), all_mods=f(4, 2, 2, 8, 512), tall=f(128, 512))
     out.update(bias_part=f(2, 4, 2, 2, 2, 128), bias_c=f(4, 2, 2, 2, 128), bias_z=f(4, 2, 2, 2, 128))
     out.update(bias_near=f(3, 2, 128), found=f(2, 4, 2, 1, 128), found_c=f(4, 2, 1, 128), found_z=f(4, 2, 1, 128))
     out.update(found_near=f(3, 4, 1, 128), picked=f(8, 128), picked_other=f(8, 128))
-    out.update(gather_send=dma((4, 28)), gather_recv=dma((4, 28)), gather_local=dma((4, 6)))
-    out.update(scatter_send=dma((4, 28)), scatter_recv=dma((4, 28)), pair_send=dma((4, 4)), pair_recv=dma((4, 4)))
+    out.update(gather_send=dma((4, 36)), gather_recv=dma((4, 36)), gather_local=dma((4, 6)))
+    out.update(scatter_send=dma((4, 36)), scatter_recv=dma((4, 36)), pair_send=dma((4, 4)), pair_recv=dma((4, 4)))
     out.update(swap_send=dma((4, 2)), swap_recv=dma((4, 2)), swap_local=dma((4,)))
     out.update(small_send=dma((4, 8)), small_recv=dma((4, 8)), load_sem=dma((12,)), free=regular)
     return out
@@ -834,8 +893,8 @@
         self.end()
 
     def set_up(self):
-        gather = lambda i, own, full, lanes: Gather(
-            own, full, lanes, self.gather_send.at[i], self.gather_recv.at[i], self.gather_local.at[i]
+        gather = lambda i, own, full, lanes, *rows: Gather(
+            own, full, lanes, self.gather_send.at[i], self.gather_recv.at[i], self.gather_local.at[i], *rows
         )
         self.q = gather(
             0,
@@ -846,6 +905,7 @@
             ],
             self.buf_a,
             (256, 768),
+            FIRST,
         )
         self.p = gather(1, lambda h: [(self.wp.at[:, block(h, 256)], 0, 256)], self.buf_a, (0, 256))
         self.u = gather(2, lambda h: [(self.wu.at[:, block(h, 1024)], 0, 1024)], self.gu, (0, 1024))
@@ -860,7 +920,11 @@
             heads(1),
         )
         firsts = ((self.first_a0, self.first_b0), (self.first_a1, self.first_b1))
-        rest = ((self.second0, self.third0), (self.second1, self.third1), (self.second2, self.third2))
+        rest = (
+            (self.second0, self.third0, self.wide_z0, self.wide_y0, self.wide_x0),
+            (self.second1, self.third1, self.wide_z1, self.wide_y1, self.wide_x1),
+            (self.second2, self.third2, self.wide_z2, self.wide_y2, self.wide_x2),
+        )
         plan = (
             (self.buf_d, firsts[0], rest[0], (0, 1024)),
             (self.buf_c, firsts[1], rest[1], (0, 1024)),
@@ -916,14 +980,13 @@
         for copy in ada:
             copy.start()
         little.step((0,), (1, 2, 3))
-        q.enter()
-        p.enter()
+        q.enter((2,))
         self.part[...] = jnp.zeros_like(self.part)
         little.step((1, 2, 3), (4,))
+        q.first()
         for copy in ada:
             copy.wait()
         little.step((4,), (5,))
-        q.first()
         row = z * 2 + y
         lhs = [self.small_full[x, b // 4, b // 2 % 2, b % 2, pl.ds(row, 1), :] for b in range(16)]
         lhs = jnp.concatenate(lhs, 0)
@@ -931,41 +994,38 @@
         for j in range(6):
             product = nn(lhs.astype(BF), self.wide[:, j * 512 : (j + 1) * 512])
             for b in range(16):
-                self.part[b // 4, b // 2 % 2, b % 2, j : j + 1, :] = product[b : b + 1, :]
+                self.part[b % 2, b // 4, b // 2 % 2, j : j + 1, :] = product[b : b + 1, :]
         near_c, near_y, near_z = self.near_c, self.near_y, self.near_z
-        first = remote(self.part.at[:, :, 1 - c], near_c, send.at[1, 0], recv.at[1, 0], at(z, y, 1 - c, x))
+        first = remote(self.part.at[1 - c], near_c, send.at[1, 0], recv.at[1, 0], at(z, y, 1 - c, x))
         first.start()
         first.wait()
-        for zz in range(4):
-            for yy in range(2):
-                near_c[zz, yy] = near_c[zz, yy] + self.part[zz, yy, c]
-        second = remote(near_c.at[:, 1 - y], near_y, send.at[1, 1], recv.at[1, 1], at(z, 1 - y, c, x))
-        second.start()
-        second.wait()
-        for zz in range(4):
-            near_y[zz] = near_y[zz] + near_c[zz, y]
-        thirds = []
+        near_c[...] = near_c[...] + self.part[c]
+        seconds = []
         for s in (1, 2, 3):
             to = lax.rem(z + s, 4)
-            thirds.append(
-                remote(near_y.at[to], near_z.at[s - 1], send.at[1, 1 + s], recv.at[1, 1 + s], at(to, y, c, x))
-            )
-            thirds[-1].start()
+            seconds.append(remote(near_c.at[to], near_z.at[s - 1], send.at[1, s], recv.at[1, s], at(to, y, c, x)))
+            seconds[-1].start()
+        q.pass_on((1, 3))
+        p.enter()
         u.enter()
-        d.enter()
+        for copy in seconds:
+            copy.wait()
+        near_z[3] = near_c[z] + near_z[0] + near_z[1] + near_z[2]
+        third = remote(near_z.at[3, 1 - y], near_y.at[0], send.at[1, 4], recv.at[1, 4], at(z, 1 - y, c, x))
+        third.start()
         q.turn(0)
+        third.wait()
+        near_y[1] = near_y[0] + near_z[3, y]
+        fourth = remote(near_y.at[1], self.mods.at[1 - c], send.at[1, 5], recv.at[1, 5], at(z, y, 1 - c, 1 - x))
+
+        @pl.when(c != x)
+        def _():
+            fourth.start()
+
         q.arrived(2)
         q.arrived(1)
         q.arrived(3)
-        for copy in thirds:
-            copy.wait()
-        near_z[3] = near_y[z] + near_z[0] + near_z[1] + near_z[2]
-        fourth = remote(near_z.at[3], self.mods.at[1 - c], send.at[1, 5], recv.at[1, 5], at(z, y, 1 - c, 1 - x))
-
-        @pl.when(c != x)
-        def _():
-            fourth.start()
-
+        d.enter()
         self.swap_lat.share()
         q.turn(2)
 
@@ -975,7 +1035,7 @@
 
         @pl.when(c == x)
         def _():
-            self.mods[c] = near_z[3]
+            self.mods[c] = near_y[1]
 
         fifth = remote(self.mods.at[c], self.mods.at[c], send.at[1, 6], recv.at[1, 6], at(z, y, 1 - c, x))
         fifth.start()

time: 323 us -> 286 us (0.89)
  Pallas kernels: 307 us -> 270 us
    pallas_call x1, Pallas kernels: 307 us -> 270 us  [on_device_pairs(): pl.pallas_call(pairs_kernel, out_shape=[rows, rows, out(3, 64, 512), out(...]
where the time goes in v5:
time: 286 us
  Pallas kernels  270 us (94%)
  local copies, waits for them, and re-layouts  13.6 us (5%)
    pallas_call x1, Pallas kernels, on_device_pairs(): pl.pallas_call(pairs_kernel, out_shape=[rows, rows, out(3, 64, 512), out(...  270 us
    unnamed x19, local copies, waits for them, and re-layouts  8.53 us

profile of v5, /device:TPU:0, one launch (start us, length us, event | category | flops | bytes accessed | tf_op | source)
XLA Modules:
  0.0 285.6 jit_solution(8542927903788842149)
XLA Ops:
  0.7 269.8 %dit_block.1 = (bf16[512,1024]{1,0:T(8,128)(2,1)}, bf16[512,1024]{1,0:T(8,128)(2,1)}, f32[3,64,512]{2,1,0:T(8,128)}, f32[64,512]{1,0:T(8,128)}, f32[64,2048]{1,0...) custom-call(bf16[512,1024]{1,0:T(8,128)(2,1)} %bitcast.31, ...), custom_call_target="tpu_custom_call" | custom-call | tf_op jit(solution)/shard_map/dit_block/pallas_call | solution.py:1537
  270.5 1.3 constant_dynamic-slice_fusion
  271.8 1.3 constant_dynamic-slice_fusion.1
  273.1 1.4 slice_bitcast_fusion
  274.4 1.1 slice_bitcast_fusion.1
  275.6 1.5 bitcast_convert_fusion
  277.0 0.0 copy-start
  277.0 3.5 %copy.28 = f32[512,1,1024]{2,1,0:T(1,128)} copy(f32[512,1,1024]{2,0,1:T(8,128)S(1)} %bitcast_convert_fusion) | data formatting | bytes 4194304
  280.5 0.0 copy-start.4
  280.5 0.0 copy-start.5
  280.5 0.0 copy-start.3
  280.5 0.0 copy-done
  280.5 0.0 copy-start.2
  280.5 1.0 copy.35
  281.5 0.2 copy-done.4
  281.7 0.0 copy-start.1
  281.7 0.7 copy.36
  282.5 0.0 copy-done.5
  282.5 0.7 copy.37
  283.1 0.0 copy-done.3
  283.1 0.8 copy.38
  283.9 0.0 copy-done.2
  283.9 0.8 copy.39
  284.7 0.0 copy-done.1
  284.7 0.9 copy.40
Async XLA Ops:
  277.0 3.5 %copy-start = (bf16[512,1024]{1,0:T(8,128)(2,1)S(1)}, bf16[512,1024]{1,0:T(8,128)(2,1)}, u32[]{:S(2)}) copy-start(bf16[512,1024]{1,0:T(8,128)(2,1)} %get-tuple-element.24) | copy-start | bytes 3145732
  280.5 1.2 copy-start.4
  280.5 1.9 copy-start.5
  280.5 2.6 copy-start.3
  280.5 3.4 %copy-start.2 = (f32[64,2048]{1,0:T(8,128)S(1)}, f32[64,2048]{1,0:T(8,128)}, u32[]{:S(2)}) copy-start(f32[64,2048]{1,0:T(8,128)} %get-tuple-element.30) | copy-start | bytes 1572868
  281.7 3.0 %copy-start.1 = (f32[6,64,512]{2,1,0:T(8,128)S(1)}, f32[6,64,512]{2,1,0:T(8,128)}, u32[]{:S(2)}) copy-start(f32[6,64,512]{2,1,0:T(8,128)} %get-tuple-element.31) | copy-start | bytes 2359300

commit v6 on v5

--- a/solution.py
+++ b/solution.py
@@ -355,9 +355,14 @@
 MIB = 2**20
 IN_VMEM = pl.BlockSpec(memory_space=pltpu.VMEM)
 IN_ANY = pl.BlockSpec(memory_space=ANY)
-ROWS_A, ROWS_B, ROWS_W = (0, 64), (64, 48), (112, 16)
-ROWS_Z = 112
-FIRST = ((0, 80), (80, 48), None)
+ROWS = dict(q=[80, 48, 0], p=[64, 48, 16], u=[64, 48, 16], d=[48, 48, 32])
+ROWS.update(down=[64, 48, 16], up=[64, 48, 16], near=[64, 48, 16], far=[64, 48, 16])
+MOST_A, MOST_B = 64, 48
+
+
+def cut(rows):
+    a, b, w = rows
+    return pl.ds(0, a), pl.ds(a, b), pl.ds(a + b, w), pl.ds(0, a + b)
 
 
 def place():
@@ -404,12 +409,12 @@
 def partners():
     z, y, c, x = place()
     out = [at(z, y, 1 - c, x), at(z, 1 - y, c, x), at(z, y, c, 1 - x), at(z, y, 1 - c, 1 - x)]
-    out.append(at(z, 1 - y, c, 1 - x))
+    out += [at(z, 1 - y, c, 1 - x), at(z, 1 - y, 1 - c, 1 - x)]
     return out + [at(lax.rem(z + d, 4), y, c, x) for d in (1, 2, 3)]
 
 
 class Gather:
-    def __init__(self, own, full, lanes, send, recv, local, rows=(ROWS_A, ROWS_B, ROWS_W)):
+    def __init__(self, own, full, lanes, rows, send, recv, local):
         self.own, self.full, self.lanes, self.rows = own, full, pl.ds(*lanes), rows
         self.send, self.recv, self.local = send, recv, local
 
@@ -424,11 +429,11 @@
 
     def _copy(self, kind, d):
         z, y, c, x = place()
-        a, b, w = [pl.ds(*rows) if rows else None for rows in self.rows]
+        a, b, w, first = cut(self.rows)
         from_z = lax.rem(z - d + 4, 4)
         to_x, to_y, to_z = at(z, y, c, 1 - x), at(z, 1 - y, c, x), at(lax.rem(z + d, 4), y, c, x)
         if kind == 0:
-            spot, to = self.full.at[x, z, y, pl.ds(0, sum(self.rows[1])), self.lanes], to_z
+            spot, to = self.full.at[x, z, y, first, self.lanes], to_z
         elif kind == 1:
             spot, to = self.full.at[x, from_z, y, a, self.lanes], to_x
         elif kind == 2:
@@ -477,10 +482,11 @@
         self._copy(3, d).start()
         self._copy(2, d).wait()
         self._copy(4, d).start()
-        if self.rows[2] and d == 2:
-            self._copy(6, 1).wait()
-            for k in (2, 1, 3):
-                self._copy(5, k).start()
+
+    def spread(self):
+        self._copy(6, 1).wait()
+        for k in (2, 1, 3):
+            self._copy(5, k).start()
 
     def finish(self):
         for d in range(4):
@@ -492,7 +498,10 @@
 
 
 class Scatter:
-    def __init__(self, part, first_a, first_b, second, third, wide_z, wide_y, wide_x, total, lanes, out, send, recv):
+    def __init__(
+        self, part, first_a, first_b, second, third, wide_z, wide_y, wide_x, total, lanes, rows, out, send, recv
+    ):
+        self.rows = rows
         self.part, self.first_a, self.first_b = part, first_a, first_b
         self.wide_z, self.wide_y, self.wide_x = wide_z, wide_y, wide_x
         self.second, self.third, self.total, self.out = second, third, total, out
@@ -500,24 +509,30 @@
 
     def _copy(self, kind, d):
         z, y, c, x = place()
-        a, b, w, n, to_z = pl.ds(*ROWS_A), pl.ds(*ROWS_B), pl.ds(*ROWS_W), self.lanes, lax.rem(z + d, 4)
+        n, to_z = self.lanes, lax.rem(z + d, 4)
+        a, b, w, first = cut(self.rows)
+        na, nb, nw = [pl.ds(0, count) for count in self.rows]
         send, recv = self.send.at[4 * kind + d], self.recv.at[4 * kind + d]
         to_x, to_y = at(z, y, c, 1 - x), at(z, 1 - y, c, x)
         if kind == 0:
-            return remote(self.part.at[:, to_z, 1 - y, a, n], self.first_a.at[to_z, :, :, n], send, recv, to_y)
+            return remote(self.part.at[:, to_z, 1 - y, a, n], self.first_a.at[to_z, :, na, n], send, recv, to_y)
         if kind == 1:
-            return remote(self.part.at[1 - x, to_z, :, b, n], self.first_b.at[to_z, :, :, n], send, recv, to_x)
+            return remote(self.part.at[1 - x, to_z, :, b, n], self.first_b.at[to_z, :, nb, n], send, recv, to_x)
         if kind == 2:
-            return remote(self.first_a.at[to_z, 1 - x, :, n], self.second.at[to_z, a, n], send, recv, to_x)
+            return remote(self.first_a.at[to_z, 1 - x, na, n], self.second.at[to_z, a, n], send, recv, to_x)
         if kind == 3:
-            return remote(self.first_b.at[to_z, 1 - y, :, n], self.second.at[to_z, b, n], send, recv, to_y)
+            return remote(self.first_b.at[to_z, 1 - y, nb, n], self.second.at[to_z, b, n], send, recv, to_y)
         if kind == 4:
-            return remote(self.second.at[to_z, :, n], self.third.at[d - 1, :, n], send, recv, at(to_z, y, c, x))
+            return remote(
+                self.second.at[to_z, first, n], self.third.at[d - 1, first, n], send, recv, at(to_z, y, c, x)
+            )
         if kind == 5:
-            return remote(self.part.at[:, to_z, :, w, n], self.wide_z.at[d - 1, :, :, :, n], send, recv, at(to_z, y, c, x))
+            return remote(
+                self.part.at[:, to_z, :, w, n], self.wide_z.at[d - 1, :, :, nw, n], send, recv, at(to_z, y, c, x)
+            )
         if d == 0:
-            return remote(self.wide_z.at[0, :, 1 - y, :, n], self.wide_y.at[:, :, n], send, recv, to_y)
-        return remote(self.wide_y.at[1 - x, :, n], self.wide_x.at[:, n], send, recv, to_x)
+            return remote(self.wide_z.at[0, :, 1 - y, nw, n], self.wide_y.at[:, nw, n], send, recv, to_y)
+        return remote(self.wide_y.at[1 - x, nw, n], self.wide_x.at[nw, n], send, recv, to_x)
 
     def _core(self):
         z, y, c, x = place()
@@ -540,72 +555,70 @@
     def start(self):
         for d in (2, 1, 3):
             self._copy(5, d).start()
-        self._start(2)
-        self._start(1)
+        for d in (2, 1, 3, 0):
+            self._start(d)
 
     def turn(self, d):
         z, y, c, x = place()
         to_z, n = lax.rem(z + d, 4), self.lanes
-        a, b, w = pl.ds(*ROWS_A), pl.ds(*ROWS_B), pl.ds(*ROWS_W)
+        a, b, _, _ = cut(self.rows)
+        na, nb, _ = [pl.ds(0, count) for count in self.rows]
         self._copy(0, d).wait()
         for k in range(2):
-            total = self.first_a[to_z, k, :, n].astype(F32) + self.part[k, to_z, y, a, n].astype(F32)
-            self.first_a[to_z, k, :, n] = total.astype(BF)
+            total = self.first_a[to_z, k, na, n].astype(F32) + self.part[k, to_z, y, a, n].astype(F32)
+            self.first_a[to_z, k, na, n] = total.astype(BF)
         self._copy(2, d).start()
         self._copy(1, d).wait()
         for k in range(2):
-            total = self.first_b[to_z, k, :, n].astype(F32) + self.part[x, to_z, k, b, n].astype(F32)
-            self.first_b[to_z, k, :, n] = total.astype(BF)
+            total = self.first_b[to_z, k, nb, n].astype(F32) + self.part[x, to_z, k, b, n].astype(F32)
+            self.first_b[to_z, k, nb, n] = total.astype(BF)
         self._copy(3, d).start()
-        if d in (1, 2):
-            self._start({2: 3, 1: 0}[d])
-        elif d == 0:
-            self._fold_z()
-
-    def _fold_z(self):
-        z, y, c, x = place()
-        n, w = self.lanes, pl.ds(*ROWS_W)
+
+    def fold_z(self):
+        z, y, c, x = place()
+        n, w, nw = self.lanes, cut(self.rows)[2], pl.ds(0, self.rows[2])
         for k in (2, 1, 3):
             self._copy(5, k).wait()
         for k in range(2):
-            total = self.part[k, z, :, w, n].astype(F32)
-            for s in range(3):
-                total = total + self.wide_z[s, k, :, :, n].astype(F32)
-            self.wide_z[0, k, :, :, n] = total.astype(BF)
+            for j in range(2):
+                total = self.part[k, z, j, w, n].astype(F32)
+                for s in range(3):
+                    total = total + self.wide_z[s, k, j, nw, n].astype(F32)
+                self.wide_z[0, k, j, nw, n] = total.astype(BF)
         self._copy(6, 0).start()
 
-    def _fold_y(self):
-        z, y, c, x = place()
-        n = self.lanes
+    def fold_y(self):
+        z, y, c, x = place()
+        n, nw = self.lanes, pl.ds(0, self.rows[2])
         self._copy(6, 0).wait()
-        total = self.wide_y[:, :, n].astype(F32) + self.wide_z[0, :, y, :, n].astype(F32)
-        self.wide_y[:, :, n] = total.astype(BF)
+        for k in range(2):
+            total = self.wide_y[k, nw, n].astype(F32) + self.wide_z[0, k, y, nw, n].astype(F32)
+            self.wide_y[k, nw, n] = total.astype(BF)
         self._copy(6, 1).start()
 
     def leave(self, d):
         z, y, c, x = place()
         to_z, n = lax.rem(z + d, 4), self.lanes
-        a, b = pl.ds(*ROWS_A), pl.ds(*ROWS_B)
+        a, b, _, _ = cut(self.rows)
+        na, nb, _ = [pl.ds(0, count) for count in self.rows]
         self._copy(2, d).wait()
-        total = self.second[to_z, a, n].astype(F32) + self.first_a[to_z, x, :, n].astype(F32)
+        total = self.second[to_z, a, n].astype(F32) + self.first_a[to_z, x, na, n].astype(F32)
         self.second[to_z, a, n] = total.astype(BF)
         self._copy(3, d).wait()
-        total = self.second[to_z, b, n].astype(F32) + self.first_b[to_z, y, :, n].astype(F32)
+        total = self.second[to_z, b, n].astype(F32) + self.first_b[to_z, y, nb, n].astype(F32)
         self.second[to_z, b, n] = total.astype(BF)
         if d:
             self._copy(4, d).start()
-        if d == 1:
-            self._fold_y()
 
     def last(self):
         z, y, c, x = place()
-        n, w = self.lanes, pl.ds(*ROWS_W)
+        n, nw = self.lanes, pl.ds(0, self.rows[2])
+        a, b, w, _ = cut(self.rows)
         self._copy(6, 1).wait()
-        self.total[w, n] = self.wide_x[:, n].astype(F32) + self.wide_y[x, :, n].astype(F32)
+        self.total[w, n] = self.wide_x[nw, n].astype(F32) + self.wide_y[x, nw, n].astype(F32)
         for d in (1, 2, 3):
             self._copy(4, d).wait()
-
-        for rows in (pl.ds(*ROWS_A), pl.ds(*ROWS_B)):
+        for rows in (a, b):
             total = self.second[z, rows, n].astype(F32)
             for d in range(3):
                 total = total + self.third[d, rows, n].astype(F32)
@@ -656,7 +669,7 @@
 
     def _both(self, act):
         z, y, c, x = place()
-        rows = self.full.at[block(c, 512)]
+        rows = self.full if self.full.shape == self.out.shape else self.full.at[block(c, 512)]
 
         @pl.when(c != x)
         def _():
@@ -840,7 +853,7 @@
 
 INPUTS = """lat_own grad_own wq wp wu wd ada cond q_bias v_bias p_bias d_bias u_bias a_bias"""
 OUTPUTS = """block_mine input_mine q_out p_out u_out d_out held_a held_b
-    ada_out cond_out ada_bias_out bias_out"""
+    ada_out small_out"""
 GROUP = (2, 4, 2, 128, 1024)
 TOKENS = (1024, 1024)
 
@@ -852,13 +865,13 @@
     out.update(mlp_in=v(*TOKENS), g_two=v(*TOKENS), mine=v(*TOKENS), theirs_a=v(*TOKENS), theirs_b=v(*TOKENS))
     out.update(buf_a=v(*GROUP), buf_b=v(*GROUP), gu=v(*GROUP), buf_c=v(*GROUP), buf_d=v(*GROUP))
     for i in range(2):
-        out[f"first_a{i}"], out[f"first_b{i}"] = v(4, 2, ROWS_A[1], 1024), v(4, 2, ROWS_B[1], 1024)
-    for i in range(3):
-        out[f"second{i}"], out[f"third{i}"] = v(4, ROWS_Z, 1024), v(3, ROWS_Z, 1024)
-        out[f"wide_z{i}"], out[f"wide_y{i}"] = v(3, 2, 2, ROWS_W[1], 1024), v(2, ROWS_W[1], 1024)
-        out[f"wide_x{i}"] = v(ROWS_W[1], 1024)
+        out[f"first_a{i}"], out[f"first_b{i}"] = v(4, 2, MOST_A, 1024), v(4, 2, MOST_B, 1024)
+    for i, name in enumerate(("down", "up", "near")):
+        a, b, w = ROWS[name]
+        out[f"second{i}"], out[f"third{i}"] = v(4, a + b, 1024), v(3, a + b, 1024)
+        out[f"wide_z{i}"], out[f"wide_y{i}"], out[f"wide_x{i}"] = v(3, 2, 2, w, 1024), v(2, w, 1024), v(w, 1024)
     out.update(total=f(128, 1024), heads_grad=v(2, 1024, 256), lse=f(1024, 128))
-    out.update(key_total=f(1024, 128), value_total=f(1024, 128))
+    out.update(key_total=f(1024, 128), value_total=f(1024, 128), input_grad=v(256, 16, 128))
     out.update(small=f(16, 128), small_full=f(2, 4, 2, 2, 16, 128), wide=v(128, 3072), silu=f(16, 128))
     out.update(part=f(2, 4, 2, 8, 512), near_c=f(4, 2, 8, 512), near_z=f(4, 2, 8, 512), near_y=f(2, 8, 512))
     out.update(mods=f(2, 8, 512), vectors=f(16, 1024), up_bias=f(1, 4096), stats=f(8, 1024), columns=f(8, 1024))
@@ -878,6 +891,62 @@
     r = dict(zip(names, refs))
     Block(r).run()
 
+PLAN = dict(
+    b0=(("q", "enter", ()), ("q", "pass_on", (2,)),),
+    b1=(("q", "first"), ("p", "enter", ()), ("u", "enter", ()), ("d", "enter", ()),),
+    b3=(("q", "pass_on", (1,)), ("q", "pass_on", (3,)), ("p", "pass_on", (2,)), ("p", "pass_on", (1,)), ("p", "pass_on", (3,)), ("u", "pass_on", (2,)), ("u", "pass_on", (1,)), ("u", "pass_on", (3,)), ("q", "turn", 0),),
+    b4=(("q", "arrived", 2), ("q", "arrived", 1), ("q", "arrived", 3), ("d", "pass_on", (2,)), ("d", "pass_on", (1,)), ("d", "pass_on", (3,)),),
+    b5=(("q", "turn", 2), ("swap_lat", "share"),),
+    b6=(("q", "turn", 1),),
+    b7=(("q", "turn", 3), ("p", "first"), ("p", "arrived", 2), ("p", "arrived", 1), ("p", "arrived", 3), ("u", "first"),),
+    project0=(("swap_grad", "start"),),
+    project7=(("p", "turn", 0), ("p", "turn", 2), ("p", "turn", 1), ("p", "turn", 3), ("p", "spread"), ("u", "arrived", 2), ("u", "arrived", 1), ("u", "arrived", 3),),
+    heads0=(("u", "turn", 0),),
+    heads3=(("u", "turn", 2), ("u", "spread"),),
+    heads4=(("u", "turn", 1),),
+    heads5=(("u", "turn", 3),),
+    heads7=(("d", "first"),),
+    out3=(("d", "arrived", 2), ("d", "arrived", 1), ("d", "arrived", 3), ("swap_grad", "share"),),
+    enter3=(("d", "turn", 0),),
+    ascend3=(("d", "turn", 2), ("d", "spread"),),
+    ascend6=(("d", "turn", 1),),
+    down0=(("d", "turn", 3),),
+    hidden1=(("down", "turn", 2),),
+    hidden7=(("down", "turn", 1),),
+    back1=(("down", "turn", 3),),
+    upper0=(("down", "turn", 0),),
+    upper1=(("down", "fold_z"),),
+    upper2=(("down", "leave", 2),),
+    rest0=(("down", "leave", 1),),
+    rest1=(("down", "fold_y"),),
+    rest3=(("down", "leave", 3),),
+    lift3=(("down", "leave", 0), ("", "signal_free"),),
+    proj3=(("swap_block", "start"),),
+    near0=(("up", "turn", 2),),
+    near2=(("up", "turn", 1),),
+    near5=(("up", "turn", 3),),
+    first0=(("up", "turn", 0), ("up", "fold_z"),),
+    first3=(("up", "leave", 2), ("down", "last"),),
+    far0=(("up", "leave", 1),),
+    far1=(("up", "fold_y"), ("up", "leave", 3),),
+    far2=(("near_heads", "turn", 2), ("up", "leave", 0),),
+    far4=(("near_heads", "turn", 1),),
+    far6=(("near_heads", "turn", 3),),
+    far7=(("near_heads", "turn", 0), ("near_heads", "fold_z"),),
+    second1=(("near_heads", "leave", 2),),
+    second3=(("near_heads", "leave", 1),),
+    drop1=(("near_heads", "fold_y"), ("near_heads", "leave", 3),),
+    drop3=(("near_heads", "leave", 0), ("down", "finish"),),
+    last0=(("far_heads", "turn", 2),),
+    last2=(("far_heads", "turn", 1),),
+    e0=(("swap_input", "start"), ("up", "last"),),
+    e2=(("far_heads", "turn", 3),),
+    e4=(("far_heads", "turn", 0), ("far_heads", "fold_z"),),
+    e6=(("far_heads", "leave", 2),),
+    e7=(("up", "finish"), ("far_heads", "leave", 1), ("far_heads", "fold_y"), ("near_heads", "last"),),
+    e8=(("far_heads", "leave", 3), ("far_heads", "leave", 0), ("far_heads", "last"),),
+)
+
 
 class Block:
     def __init__(self, r):
@@ -893,11 +962,12 @@
         self.end()
 
     def set_up(self):
-        gather = lambda i, own, full, lanes, *rows: Gather(
-            own, full, lanes, self.gather_send.at[i], self.gather_recv.at[i], self.gather_local.at[i], *rows
+        gather = lambda i, name, own, full, lanes: Gather(
+            own, full, lanes, ROWS[name], self.gather_send.at[i], self.gather_recv.at[i], self.gather_local.at[i]
         )
         self.q = gather(
             0,
+            "q",
             lambda h: [
                 (self.wq.at[j, :, block(2 * h + k, 128)], 256 + 384 * k + 128 * j, 128)
                 for k in range(2)
@@ -905,11 +975,10 @@
             ],
             self.buf_a,
             (256, 768),
-            FIRST,
         )
-        self.p = gather(1, lambda h: [(self.wp.at[:, block(h, 256)], 0, 256)], self.buf_a, (0, 256))
-        self.u = gather(2, lambda h: [(self.wu.at[:, block(h, 1024)], 0, 1024)], self.gu, (0, 1024))
-        self.d = gather(3, lambda h: [(self.wd.at[:, block(h, 1024)], 0, 1024)], self.buf_b, (0, 1024))
+        self.p = gather(1, "p", lambda h: [(self.wp.at[:, block(h, 256)], 0, 256)], self.buf_a, (0, 256))
+        self.u = gather(2, "u", lambda h: [(self.wu.at[:, block(h, 1024)], 0, 1024)], self.gu, (0, 1024))
+        self.d = gather(3, "d", lambda h: [(self.wd.at[:, block(h, 1024)], 0, 1024)], self.buf_b, (0, 1024))
         heads = lambda k: lambda h: [
             (self.q_out.at[j, :, block(2 * h + k, 128)], 256 + 384 * k + 128 * j, 128) for j in range(3)
         ]
@@ -926,21 +995,23 @@
             (self.second2, self.third2, self.wide_z2, self.wide_y2, self.wide_x2),
         )
         plan = (
-            (self.buf_d, firsts[0], rest[0], (0, 1024)),
-            (self.buf_c, firsts[1], rest[1], (0, 1024)),
-            (self.buf_d, firsts[0], rest[2], (0, 640)),
-            (self.buf_d, firsts[0], rest[2], (640, 384)),
+            (self.buf_d, firsts[0], rest[0], (0, 1024), ROWS["down"]),
+            (self.buf_c, firsts[1], rest[1], (0, 1024), ROWS["up"]),
+            (self.buf_d, firsts[0], rest[2], (0, 640), ROWS["near"]),
+            (self.buf_d, firsts[0], rest[2], (640, 384), ROWS["far"]),
         )
         self.down, self.up, self.near_heads, self.far_heads = [
-            Scatter(part, *first, *more, self.total, lanes, outs[i], self.scatter_send.at[i], self.scatter_recv.at[i])
-            for i, (part, first, more, lanes) in enumerate(plan)
+            Scatter(
+                part, *first, *more, self.total, lanes, rows, outs[i], self.scatter_send.at[i], self.scatter_recv.at[i]
+            )
+            for i, (part, first, more, lanes, rows) in enumerate(plan)
         ]
         swaps = [(self.lat_own, self.lat), (self.grad_own, self.grad)]
         self.swap_lat, self.swap_grad = [
             Swap(own, full, self.swap_send.at[i], self.swap_recv.at[i], self.swap_local.at[i])
             for i, (own, full) in enumerate(swaps)
         ]
-        backs = [(self.g_two, self.block_mine), (self.branch_one, self.input_mine)]
+        backs = [(self.g_two, self.block_mine), (self.input_grad, self.input_mine)]
         self.swap_block, self.swap_input = [
             SwapBack(full, out, self.swap_send.at[2 + i, 0], self.swap_recv.at[2 + i, 0], self.swap_local.at[2 + i])
             for i, (full, out) in enumerate(backs)
@@ -949,6 +1020,18 @@
             Pair(self.mine, theirs, self.pair_send.at[i], self.pair_recv.at[i])
             for i, theirs in enumerate((self.theirs_a, self.theirs_b, self.theirs_a, self.theirs_b))
         ]
+
+    def do(self, slot):
+        for owner, act, *given in PLAN.get(slot, ()):
+            getattr(getattr(self, owner) if owner else self, act)(*given)
+
+    def loop(self, count, body, name):
+        loop(count, body, {i: (lambda s=name + str(i): self.do(s)) for i in range(count) if name + str(i) in PLAN})
+
+    def signal_free(self):
+        z, y, c, x = place()
+        for to in (at(z, 1 - y, c, x), at(z, y, c, 1 - x)):
+            pl.semaphore_signal(self.free, inc=1, device_id=to, device_id_type=MESH)
 
     def load(self, i, source, target):
         return pltpu.make_async_copy(source, target, self.load_sem.at[i])
@@ -980,13 +1063,14 @@
         for copy in ada:
             copy.start()
         little.step((0,), (1, 2, 3))
-        q.enter((2,))
+        self.do("b0")
         self.part[...] = jnp.zeros_like(self.part)
         little.step((1, 2, 3), (4,))
-        q.first()
+        self.do("b1")
         for copy in ada:
             copy.wait()
         little.step((4,), (5,))
+        self.do("b2")
         row = z * 2 + y
         lhs = [self.small_full[x, b // 4, b // 2 % 2, b % 2, pl.ds(row, 1), :] for b in range(16)]
         lhs = jnp.concatenate(lhs, 0)
@@ -1005,46 +1089,23 @@
             to = lax.rem(z + s, 4)
             seconds.append(remote(near_c.at[to], near_z.at[s - 1], send.at[1, s], recv.at[1, s], at(to, y, c, x)))
             seconds[-1].start()
-        q.pass_on((1, 3))
-        p.enter()
-        u.enter()
+        self.do("b3")
         for copy in seconds:
             copy.wait()
         near_z[3] = near_c[z] + near_z[0] + near_z[1] + near_z[2]
-        third = remote(near_z.at[3, 1 - y], near_y.at[0], send.at[1, 4], recv.at[1, 4], at(z, 1 - y, c, x))
-        third.start()
-        q.turn(0)
-        third.wait()
-        near_y[1] = near_y[0] + near_z[3, y]
-        fourth = remote(near_y.at[1], self.mods.at[1 - c], send.at[1, 5], recv.at[1, 5], at(z, y, 1 - c, 1 - x))
-
-        @pl.when(c != x)
-        def _():
-            fourth.start()
-
-        q.arrived(2)
-        q.arrived(1)
-        q.arrived(3)
-        d.enter()
-        self.swap_lat.share()
-        q.turn(2)
-
-        @pl.when(c != x)
-        def _():
-            fourth.wait()
-
-        @pl.when(c == x)
-        def _():
-            self.mods[c] = near_y[1]
-
+        self._partials(lambda copy: copy.start())
+        self.do("b4")
+        self._partials(lambda copy: copy.wait())
+        self.mods[c] = near_y[0] + near_y[1]
         fifth = remote(self.mods.at[c], self.mods.at[c], send.at[1, 6], recv.at[1, 6], at(z, y, 1 - c, x))
         fifth.start()
+        self.do("b5")
         little.step((5,), ())
         bias = [widen(self.small_full, 8, k) for k in range(4)]
         ada_bias = [widen(self.small_full, 10 + j // 4, j % 4) for j in range(6)]
         for k, (zz, yy, cc, xx) in enumerate(devices()):
             self.up_bias[:, k * 128 : (k + 1) * 128] = self.small_full[xx, zz, yy, cc, 9:10, :]
-        q.turn(1)
+        self.do("b6")
         fifth.wait()
         for j in range(6):
             for h in range(2):
@@ -1052,12 +1113,25 @@
                 self.vectors[j : j + 1, lanes] = self.mods[h, j : j + 1, :] + ada_bias[j][:, lanes]
         for k in range(4):
             self.vectors[6 + k : 7 + k, :] = bias[k]
-        q.turn(3)
-        p.first()
-        for k in (2, 1, 3):
-            p.arrived(k)
-        u.first()
+        self.do("b7")
         self.swap_lat.finish()
+
+    def _partials(self, act):
+        z, y, c, x = place()
+        for k, to_y in enumerate((y, 1 - y)):
+            sems = self.small_send.at[1, 4 + k], self.small_recv.at[1, 4 + k]
+            source, target = self.near_z.at[3, to_y], self.near_y.at[y]
+
+            @pl.when(c != x)
+            def _():
+                act(remote(source, target, *sems, at(z, to_y, 1 - c, 1 - x)))
+
+            @pl.when(c == x)
+            def _():
+                if k:
+                    act(remote(source, target, *sems, at(z, to_y, c, x)))
+                else:
+                    act(pltpu.make_async_copy(source, target, self.load_sem.at[6]))
 
     def attend(self):
         z, y, c, x = place()
@@ -1068,9 +1142,8 @@
             normal, _ = normalise(self.lat[rows, :].astype(F32))
             self.attn_in[rows, :] = (normal * (1.0 + vectors[1:2, :]) + vectors[0:1, :]).astype(BF)
 
-        loop(4, modulated)
+        self.loop(4, modulated, "normal")
         q.finish()
-        self.swap_grad.start()
 
         def project(i):
             b, quarter = i // 4, lax.rem(i, 4)
@@ -1083,11 +1156,7 @@
                     value = value + vectors[row : row + 1, columns]
                 self.buf_d[b, quarter, :, :, 256 + k * 128 : 384 + k * 128] = value.astype(BF).reshape(2, 128, 128)
 
-        loop(8, project)
-        for k in (0, 2, 1, 3):
-            p.turn(k)
-        for k in (2, 1, 3):
-            u.arrived(k)
+        self.loop(8, project, "project")
         lane = lax.broadcasted_iota(jnp.int32, (1, 128), 1)
         self.lse[...] = jnp.zeros_like(self.lse)
 
@@ -1111,14 +1180,7 @@
             self.buf_d[b, zz, :, :, block(k, 128)] = result.astype(BF).reshape(2, 2, 128, 128)
             self.lse[rows, :] = logs
 
-        ticks = {
-            0: lambda: u.turn(0),
-            3: lambda: u.turn(2),
-            4: lambda: u.turn(1),
-            5: lambda: u.turn(3),
-        }
-        loop(8, attend, ticks)
-        d.first()
+        self.loop(8, attend, "heads")
         p.finish()
         self.load(0, self.buf_a, self.held_a).start()
         pair = self.pairs[0]
@@ -1129,11 +1191,8 @@
             partial += nt(flat(self.buf_d[1, zz, :, :, 0:256]), flat(self.buf_a[1, :, :, :, 0:256]))
             pair.give(i, partial)
 
-        loop(4, out)
+        self.loop(4, out, "out")
         self.load(1, self.buf_d, self.held_b).start()
-        for k in (2, 1, 3):
-            d.arrived(k)
-        self.swap_grad.share()
 
         def residual(i):
             rows = block(i, 256)
@@ -1141,7 +1200,7 @@
             self.branch_one[rows, :] = branch.astype(BF)
             self.mid[rows, :] = self.lat[rows, :].astype(F32) + vectors[2:3, :] * branch
 
-        loop(4, residual)
+        self.loop(4, residual, "middle")
 
     def mlp(self):
         z, y, c, x = place()
@@ -1161,10 +1220,9 @@
             mine_too = jnp.where(i // 2 == c, 1.0, 0.0)
             stats[1:2, :] += column_sum(g.astype(F32)) * mine_too
 
-        loop(4, enter)
+        self.loop(4, enter, "enter")
         u.finish()
         self.load(0, self.buf_a, self.held_a).wait()
-        d.turn(0)
 
         def ascend(i):
             b, quarter = i // 4, lax.rem(i, 4)
@@ -1174,7 +1232,7 @@
             active[b, quarter] = value.astype(BF).reshape(2, 128, 1024)
             slope[b, quarter] = gradient.astype(BF).reshape(2, 128, 1024)
 
-        loop(8, ascend, {3: lambda: d.turn(2), 6: lambda: d.turn(1)})
+        self.loop(8, ascend, "ascend")
         self.load(1, self.buf_d, self.held_b).wait()
 
         def down_gradient(i):
@@ -1182,7 +1240,7 @@
             value = tn(g_two[:, block(half, 512)], flat(active[b]))
             self.buf_d[b, pl.ds(half * 2, 2)] = value.astype(BF).reshape(2, 2, 128, 1024)
 
-        loop(4, down_gradient, {0: lambda: d.turn(3)})
+        self.loop(4, down_gradient, "down")
         down.start()
         d.finish()
         pair, back = self.pairs[1], self.pairs[2]
@@ -1190,7 +1248,7 @@
         def descend(i):
             pair.give(i, nt(flat(active[0, i]), flat(wd[0])) + nt(flat(active[1, i]), flat(wd[1])))
 
-        loop(4, descend, {1: lambda: down.turn(2)})
+        self.loop(4, descend, "descend")
 
         def hidden_gradient(i):
             b, quarter = i // 4, lax.rem(i, 4)
@@ -1199,7 +1257,7 @@
             hidden_grad[b, quarter] = value.reshape(2, 128, 1024)
             self.up_sums[b] += column_sum(value.astype(F32))
 
-        loop(8, hidden_gradient, {1: lambda: down.turn(1), 7: lambda: down.turn(3)})
+        self.loop(8, hidden_gradient, "hidden")
         self.load(3, self.held_b, self.buf_b).start()
 
         def leave(i):
@@ -1208,19 +1266,19 @@
             g_two[rows, :] = (mid[rows, :] + vectors[5:6, :] * branch_two).astype(BF)
             stats[0:1, :] += column_sum(grad[rows, :].astype(F32) * branch_two)
 
-        loop(4, leave)
+        self.loop(4, leave, "leave")
 
         def descend_back(i):
             back.give(i, nt(flat(hidden_grad[0, i]), flat(gu[0])) + nt(flat(hidden_grad[1, i]), flat(gu[1])))
 
-        loop(4, descend_back, {0: lambda: down.turn(0), 2: lambda: down.leave(2)})
+        self.loop(4, descend_back, "back")
 
         def up_gradient(i):
             b, half = i // 2, lax.rem(i, 2)
             value = tn(mlp_in[:, block(half, 512)], flat(hidden_grad[b]))
             up_grad[b, pl.ds(half * 2, 2)] = value.astype(BF).reshape(2, 2, 128, 1024)
 
-        loop(4, up_gradient, {0: lambda: down.leave(1), 2: lambda: down.leave(3)})
+        self.loop(4, up_gradient, "upper")
         self.load(4, self.held_a, self.buf_a).start()
         up.start()
 
@@ -1240,10 +1298,7 @@
             mine_too = jnp.where(i // 2 == c, 1.0, 0.0)
             stats[5:6, :] += column_sum(g.astype(F32)) * mine_too
 
-        loop(4, residual)
-        down.leave(0)
-        for to in (at(z, 1 - y, c, x), at(z, y, c, 1 - x)):
-            pl.semaphore_signal(self.free, inc=1, device_id=to, device_id_type=MESH)
+        self.loop(4, residual, "rest")
 
     def attend_back(self):
         z, y, c, x = place()
@@ -1260,14 +1315,14 @@
             value = nn(g_one[block(half, 512), :], flat(weights[b, :, :, :, 0:256]))
             heads_grad[b, block(half, 512), :] = value.astype(BF)
 
-        loop(4, enter)
+        self.loop(4, enter, "lift")
 
         def proj_gradient(i):
             b, half = i // 2, lax.rem(i, 2)
             value = tn(g_one[:, block(half, 512)], flat(acts[b, :, :, :, 0:256]))
             self.buf_d[b, pl.ds(half * 2, 2), :, :, 0:256] = value.astype(BF).reshape(2, 2, 128, 256)
 
-        loop(4, proj_gradient)
+        self.loop(4, proj_gradient, "proj")
         lane = lax.broadcasted_iota(jnp.int32, (1, 128), 1)
 
         def attend(i, k):
@@ -1315,36 +1370,21 @@
             value = tn(self.attn_in[:, block(half, 512)], flat(acts[b, :, :, :, lanes]))
             self.buf_d[b, pl.ds(half * 2, 2), :, :, lanes] = value.astype(BF).reshape(2, 2, 128, 384)
 
-        ticks = {
-            0: lambda: up.turn(2),
-            2: lambda: up.turn(1),
-            5: lambda: up.turn(3),
-        }
-        loop(8, lambda i: attend(i, 0), ticks)
-        up.turn(0)
-        loop(4, lambda i: qkv_gradient(i, 0))
+        self.loop(8, lambda i: attend(i, 0), "near")
+        self.loop(4, lambda i: qkv_gradient(i, 0), "first")
         pl.semaphore_wait(self.free, 2)
         near.start()
-        up.leave(2)
-        ticks = {
-            0: lambda: down.last(),
-            1: lambda: up.leave(1),
-            2: lambda: near.turn(2),
-            3: lambda: up.leave(3),
-            4: lambda: near.turn(1),
-            5: lambda: up.leave(0),
-            6: lambda: self.swap_block.start(),
-            7: lambda: near.turn(3),
-        }
-        loop(8, lambda i: attend(i, 1), ticks)
+        self.loop(8, lambda i: attend(i, 1), "far")
+        self.loop(4, lambda i: qkv_gradient(i, 1), "second")
+        far.start()
+        self.do("s0")
         pair = self.pairs[3]
 
         def descend(i):
             partial = nt(flat(acts[0, i, :, :, 256:1024]), flat(weights[0, :, :, :, 256:1024]))
             pair.give(i, partial + nt(flat(acts[1, i, :, :, 256:1024]), flat(weights[1, :, :, :, 256:1024])))
 
-        loop(4, descend, {1: lambda: near.turn(0), 3: lambda: near.leave(2)})
-        down.finish()
+        self.loop(4, descend, "drop")
 
         def leave(i):
             rows = block(i, 256)
@@ -1354,14 +1394,19 @@
             stats[7:8, :] += column_sum(dy * normal)
             dn = dy * (1.0 + vectors[1:2, :])
             dn = dn - jnp.mean(dn, -1, keepdims=True) - normal * jnp.mean(dn * normal, -1, keepdims=True)
-            self.branch_one[rows, :] = (self.mid[rows, :] + scale * dn).astype(BF)
-
-        loop(4, leave)
+            total = self.mid[rows, :] + scale * dn
+
+            @pl.when(i // 2 == c)
+            def _():
+                for half in range(2):
+                    for k in range(8):
+                        part = total[half * 128 : (half + 1) * 128, k * 128 : (k + 1) * 128]
+                        self.key_total[pl.ds(k, 128, stride=8), :] = part
+                    values = self.key_total[...].astype(BF).reshape(64, 16, 128)
+                    self.input_grad[block(lax.rem(i, 2) * 2 + half, 64)] = values
+
+        self.loop(4, leave, "last")
         self.begin_end()
-        loop(4, lambda i: qkv_gradient(i, 1), {1: lambda: near.leave(1)})
-        far.start()
-        self.swap_input.start()
-        up.last()
 
     def begin_end(self):
         z, y, c, x = place()
@@ -1373,6 +1418,7 @@
         self.half_mods[z, y, x] = self.mods[c]
         for d in (1, 2, 3):
             self._mods(d).start()
+        self.do("e0")
         columns, bias_part = self.columns, self.bias_part
         columns[...] = jnp.zeros_like(columns)
         bias_part[...] = jnp.zeros_like(bias_part)
@@ -1393,10 +1439,12 @@
             bias_part, self.bias_c, self.bias_z, self.bias_near, self.small_send.at[0], self.small_recv.at[3]
         )
         self.bias.start()
+        self.do("e1")
         for d in (1, 2, 3):
             self._mods(d).wait()
         self._across(lambda copy: copy.start())
         self.bias.along()
+        self.do("e2")
 
     def _mods(self, d):
         z, y, c, x = place()
@@ -1444,6 +1492,7 @@
             remote(self.half_mods, mods, send.at[2, 7], recv.at[2, 7], at(z, y, 1 - c, x)).wait_recv()
 
         bias.across()
+        self.do("e3")
         silu_rows = self.silu[...].astype(BF)
         total = jnp.zeros((16, 128), F32)
         bias_rows = []
@@ -1460,7 +1509,7 @@
             found[b % 2, b // 4, b // 2 % 2] = total[b : b + 1, :]
         core = remote(found.at[1 - c], found_c, send.at[3, 0], recv.at[1, 0], at(z, y, 1 - c, x))
         core.start()
-        far.turn(2)
+        self.do("e4")
         group = (lax.rem(z, 2) * 2 + y) * 2 + c
         source = lax.broadcasted_iota(jnp.int32, (512, 128), 0)
         target = lax.broadcasted_iota(jnp.int32, (512, 128), 1)
@@ -1468,6 +1517,7 @@
         self.picked[...] = exact_nn(jnp.concatenate(bias_rows + [jnp.zeros((2, 512), F32)], 0), chosen)
         swap = remote(self.picked, self.picked_other, send.at[3, 7], recv.at[1, 7], at(z, y, c, 1 - x))
         swap.start()
+        self.do("e5")
         core.wait()
         found_c[...] = found_c[...] + found[c]
         along = []
@@ -1476,9 +1526,7 @@
             along.append(remote(found_c.at[to], found_z.at[z], send.at[3, k], recv.at[1, k], at(to, y, c, x)))
             along[-1].start()
         found_z[z] = found_c[z]
-        near.leave(3)
-        far.turn(1)
-        near.leave(0)
+        self.do("e6")
         for copy in along:
             copy.wait()
         across = []
@@ -1487,27 +1535,23 @@
                 remote(found_z.at[:, to_y], found_near.at[k], send.at[3, 4 + k], recv.at[1, 4 + k], at(z, to_y, c, to_x))
             )
             across[-1].start()
-        far.turn(3)
-        far.turn(0)
-        up.finish()
-        near.last()
-        far.leave(2)
-        far.leave(1)
+        self.do("e7")
         for copy in across:
             copy.wait()
         swap.wait()
-        self.bias_out[...] = bias.finish()
-        self.ada_bias_out[...] = jnp.where(z // 2 == x, self.picked[...], self.picked_other[...])
+        self.small_out[...] = jnp.zeros_like(self.small_out)
+        self.small_out[4:6, :] = bias.finish()
+        picked = jnp.where(z // 2 == x, self.picked[...], self.picked_other[...])
+        self.small_out[8:16, 0:32] = jnp.where(x == 0, picked[:, 0:32], picked[:, 32:64])
         same, other = found_z[:, y] + found_near[0], found_near[1] + found_near[2]
         rows = [jnp.where(y == b % 2, same[b // 2], other[b // 2]) for b in range(8)]
         v = self.cond[...].astype(F32)
         v = jnp.concatenate([v[:, k * 128 : (k + 1) * 128] for k in range(8)], 0)
         gate = 1.0 / (1.0 + jnp.exp(-v))
-        self.cond_out[...] = jnp.concatenate(rows, 0) * gate * (1.0 + v * (1.0 - gate))
-        far.leave(3)
-        far.leave(0)
+        row = jnp.concatenate(rows, 0) * gate * (1.0 + v * (1.0 - gate))
+        self.small_out[0:4, :] = jnp.where(x == 0, row[0:4], row[4:8])
+        self.do("e8")
         near.finish()
-        far.last()
         self.swap_block.finish()
         self.swap_input.finish()
         far.finish()
@@ -1529,43 +1573,42 @@
     down_bias,
     ada_bias,
 ):
-    x = lax.axis_index("tp")
     small = [b.reshape(1, -1) for b in (query_bias, value_bias, proj_bias, down_bias, up_bias)]
     out = lambda *shape: jax.ShapeDtypeStruct(shape, F32)
     group = jax.ShapeDtypeStruct(GROUP, BF)
     rows = jax.ShapeDtypeStruct((512, 1024), BF)
     results = pl.pallas_call(
         pairs_kernel,
-        out_shape=[rows, rows, out(3, 64, 512), out(64, 512), out(64, 2048), out(64, 2048)]
+        out_shape=[rows, jax.ShapeDtypeStruct((256, 16, 128), BF), out(3, 64, 512), out(64, 512), out(64, 2048), out(64, 2048)]
         + [group] * 2
-        + [out(6, 64, 512), out(8, 128), out(8, 128), out(2, 128)],
+        + [out(6, 64, 512), out(16, 128)],
         in_specs=[IN_ANY] * 7 + [IN_VMEM] * 7,
-        out_specs=[IN_ANY] * 8 + [IN_VMEM] * 4,
+        out_specs=[IN_ANY] * 8 + [IN_VMEM] * 2,
         scratch_shapes=list(scratch().values()),
         compiler_params=pltpu.CompilerParams(
-            collective_id=0, has_side_effects=True, vmem_limit_bytes=63 * MIB
+            collective_id=0, has_side_effects=True, vmem_limit_bytes=63 * MIB + MIB // 2
         ),
         name="dit_block",
     )(
         latents_in.reshape(512, 1024), grad_out.reshape(512, 1024), qkv_weight.transpose(1, 0, 2), proj_weight.T,
         up_weight, down_weight.T, ada_weight.transpose(1, 0, 2), condition, *small, ada_bias,
     )
-    block_mine, input_mine, q_out, p_out, u_out, d_out, _, _, ada_out, cond_out, ada_bias_out, bias_out = results
+    block_mine, input_mine, q_out, p_out, u_out, d_out, _, _, ada_out, small_out = results
     return (
         block_mine.reshape(512, 1, 1024),
         input_mine.astype(F32).reshape(512, 1, 1024),
-        lax.dynamic_slice_in_dim(cond_out, x * 4, 4, 0).reshape(1, 512),
+        small_out[0:4].reshape(1, 512),
         q_out.transpose(1, 0, 2),
         p_out.T,
         u_out,
         d_out.T,
         ada_out.transpose(1, 0, 2),
-        bias_out[0, 0:32],
-        bias_out[0, 32:64],
-        bias_out[0, 64:96],
-        bias_out[1],
-        bias_out[0, 96:128],
-        lax.dynamic_slice_in_dim(ada_bias_out, x * 32, 32, 1)[:6],
+        small_out[4, 0:32],
+        small_out[4, 32:64],
+        small_out[4, 64:96],
+        small_out[5],
+        small_out[4, 96:128],
+        small_out[8:14, 0:32],
     )
 
 

time: 286 us -> 281 us (0.983)
  Pallas kernels: 270 us -> 265 us
    pallas_call x1, Pallas kernels: 270 us -> 265 us  [on_device_pairs(): pl.pallas_call(pairs_kernel, out_shape=[rows, jax.ShapeDtypeStruct((256,...]
    unnamed x19 -> x16, local copies, waits for them, and re-layouts: 8.53 us -> 6.15 us
where the time goes in v6:
time: 281 us; the launch traced here: 280 us
  Pallas kernels  265 us (94%)
  local copies, waits for them, and re-layouts  11.4 us (4%)
    pallas_call x1, Pallas kernels, on_device_pairs(): pl.pallas_call(pairs_kernel, out_shape=[rows, jax.ShapeDtypeStruct((256,...  265 us
    unnamed x16, local copies, waits for them, and re-layouts  6.15 us

profile of v6, /device:TPU:0, one launch (start us, length us, event | category | flops | bytes accessed | tf_op | source)
XLA Modules:
  0.0 280.3 jit_solution(14376403687274284629)
XLA Ops:
  0.7 265.4 %dit_block.1 = (bf16[512,1024]{1,0:T(8,128)(2,1)}, bf16[256,16,128]{2,1,0:T(8,128)(2,1)}, f32[3,64,512]{2,1,0:T(8,128)}, f32[64,512]{1,0:T(8,128)}, f32[64,2048]...) custom-call(bf16[512,1024]{1,0:T(8,128)(2,1)} %bitcast.29, ...), custom_call_target="tpu_custom_call" | custom-call | tf_op jit(solution)/shard_map/dit_block/pallas_call | solution.py:1580
  266.1 0.0 copy-start.3
  266.1 0.0 copy-start.4
  266.1 0.0 copy-start.2
  266.1 0.0 copy-start.1
  266.1 1.3 slice_bitcast_fusion.1
  267.5 1.3 slice.21
  268.7 1.4 slice_bitcast_fusion
  270.1 1.3 slice.27
  271.4 0.0 copy-start
  271.4 2.8 reshape.72
  274.2 2.3 copy.35
  276.4 0.0 copy-done.3
  276.4 0.7 copy.36
  277.2 0.0 copy-done.4
  277.2 0.7 copy.37
  277.9 0.0 copy-done.2
  277.9 0.8 copy.38
  278.6 0.0 copy-done.1
  278.7 0.8 copy.39
  279.4 0.0 copy-done
  279.4 0.9 copy.40
Async XLA Ops:
  266.1 10.3 %copy-start.3 = (f32[3,64,512]{2,1,0:T(8,128)S(1)}, f32[3,64,512]{2,1,0:T(8,128)}, u32[]{:S(2)}) copy-start(f32[3,64,512]{2,1,0:T(8,128)} %get-tuple-element.25) | copy-start | bytes 1179652
  266.1 11.1 %copy-start.4 = (f32[64,512]{1,0:T(8,128)S(1)}, f32[64,512]{1,0:T(8,128)}, u32[]{:S(2)}) copy-start(f32[64,512]{1,0:T(8,128)} %get-tuple-element.26) | copy-start | bytes 393220
  266.1 11.7 %copy-start.2 = (f32[64,2048]{1,0:T(8,128)S(1)}, f32[64,2048]{1,0:T(8,128)}, u32[]{:S(2)}) copy-start(f32[64,2048]{1,0:T(8,128)} %get-tuple-element.67) | copy-start | bytes 1572868
  266.1 12.5 %copy-start.1 = (f32[64,2048]{1,0:T(8,128)S(1)}, f32[64,2048]{1,0:T(8,128)}, u32[]{:S(2)}) copy-start(f32[64,2048]{1,0:T(8,128)} %get-tuple-element.28) | copy-start | bytes 1572868
  271.4 8.0 %copy-start = (f32[6,64,512]{2,1,0:T(8,128)S(1)}, f32[6,64,512]{2,1,0:T(8,128)}, u32[]{:S(2)}) copy-start(f32[6,64,512]{2,1,0:T(8,128)} %get-tuple-element.29) | copy-start | bytes 2359300

commit v7 on v6

--- a/solution.py
+++ b/solution.py
@@ -355,7 +355,7 @@
 MIB = 2**20
 IN_VMEM = pl.BlockSpec(memory_space=pltpu.VMEM)
 IN_ANY = pl.BlockSpec(memory_space=ANY)
-ROWS = dict(q=[80, 48, 0], p=[64, 48, 16], u=[64, 48, 16], d=[48, 48, 32])
+ROWS = dict(q=[80, 48, 0], p=[64, 48, 16], u=[48, 48, 32], d=[48, 48, 32])
 ROWS.update(down=[64, 48, 16], up=[64, 48, 16], near=[64, 48, 16], far=[64, 48, 16])
 MOST_A, MOST_B = 64, 48
 

time: 281 us -> 279 us (level)
  no operation moved by 1% of the time
where the time goes in v7:
time: 279 us
  Pallas kernels  264 us (95%)
  local copies, waits for them, and re-layouts  11.4 us (4%)
    pallas_call x1, Pallas kernels, on_device_pairs(): pl.pallas_call(pairs_kernel, out_shape=[rows, jax.ShapeDtypeStruct((256,...  264 us
    unnamed x16, local copies, waits for them, and re-layouts  6.15 us

profile of v7, /device:TPU:0, one launch (start us, length us, event | category | flops | bytes accessed | tf_op | source)
XLA Modules:
  0.0 278.8 jit_solution(6519719830999168441)
XLA Ops:
  0.7 263.9 %dit_block.1 = (bf16[512,1024]{1,0:T(8,128)(2,1)}, bf16[256,16,128]{2,1,0:T(8,128)(2,1)}, f32[3,64,512]{2,1,0:T(8,128)}, f32[64,512]{1,0:T(8,128)}, f32[64,2048]...) custom-call(bf16[512,1024]{1,0:T(8,128)(2,1)} %bitcast.29, ...), custom_call_target="tpu_custom_call" | custom-call | tf_op jit(solution)/shard_map/dit_block/pallas_call | solution.py:1580
  264.6 0.0 copy-start.3
  264.6 0.0 copy-start.4
  264.6 0.0 copy-start.2
  264.6 0.0 copy-start.1
  264.6 1.3 slice_bitcast_fusion.1
  266.0 1.3 slice.21
  267.2 1.4 slice_bitcast_fusion
  268.6 1.3 slice.27
  269.9 0.0 copy-start
  269.9 2.8 reshape.72
  272.7 2.3 copy.35
  274.9 0.0 copy-done.3
  274.9 0.7 copy.36
  275.7 0.0 copy-done.4
  275.7 0.7 copy.37
  276.4 0.0 copy-done.2
  276.4 0.8 copy.38
  277.2 0.0 copy-done.1
  277.2 0.8 copy.39
  277.9 0.0 copy-done
  277.9 0.9 copy.40
Async XLA Ops:
  264.6 10.3 %copy-start.3 = (f32[3,64,512]{2,1,0:T(8,128)S(1)}, f32[3,64,512]{2,1,0:T(8,128)}, u32[]{:S(2)}) copy-start(f32[3,64,512]{2,1,0:T(8,128)} %get-tuple-element.25) | copy-start | bytes 1179652
  264.6 11.1 %copy-start.4 = (f32[64,512]{1,0:T(8,128)S(1)}, f32[64,512]{1,0:T(8,128)}, u32[]{:S(2)}) copy-start(f32[64,512]{1,0:T(8,128)} %get-tuple-element.26) | copy-start | bytes 393220
  264.6 11.7 %copy-start.2 = (f32[64,2048]{1,0:T(8,128)S(1)}, f32[64,2048]{1,0:T(8,128)}, u32[]{:S(2)}) copy-start(f32[64,2048]{1,0:T(8,128)} %get-tuple-element.67) | copy-start | bytes 1572868
  264.6 12.5 %copy-start.1 = (f32[64,2048]{1,0:T(8,128)S(1)}, f32[64,2048]{1,0:T(8,128)}, u32[]{:S(2)}) copy-start(f32[64,2048]{1,0:T(8,128)} %get-tuple-element.28) | copy-start | bytes 1572868
  269.9 8.0 %copy-start = (f32[6,64,512]{2,1,0:T(8,128)S(1)}, f32[6,64,512]{2,1,0:T(8,128)}, u32[]{:S(2)}) copy-start(f32[6,64,512]{2,1,0:T(8,128)} %get-tuple-element.29) | copy-start | bytes 2359300

commit v8 on v7

--- a/solution.py
+++ b/solution.py
@@ -355,7 +355,7 @@
 MIB = 2**20
 IN_VMEM = pl.BlockSpec(memory_space=pltpu.VMEM)
 IN_ANY = pl.BlockSpec(memory_space=ANY)
-ROWS = dict(q=[80, 48, 0], p=[64, 48, 16], u=[48, 48, 32], d=[48, 48, 32])
+ROWS = dict(q=[80, 48, 0], p=[48, 48, 32], u=[48, 48, 32], d=[48, 48, 32])
 ROWS.update(down=[64, 48, 16], up=[64, 48, 16], near=[64, 48, 16], far=[64, 48, 16])
 MOST_A, MOST_B = 64, 48
 

time: 279 us -> 278 us (level)
  no operation moved by 1% of the time
where the time goes in v8:
time: 278 us
  Pallas kernels  263 us (95%)
  local copies, waits for them, and re-layouts  11.4 us (4%)
    pallas_call x1, Pallas kernels, on_device_pairs(): pl.pallas_call(pairs_kernel, out_shape=[rows, jax.ShapeDtypeStruct((256,...  263 us
    unnamed x16, local copies, waits for them, and re-layouts  6.15 us

profile of v8, /device:TPU:0, one launch (start us, length us, event | category | flops | bytes accessed | tf_op | source)
XLA Modules:
  0.0 277.5 jit_solution(15925926952655639779)
XLA Ops:
  0.7 262.6 %dit_block.1 = (bf16[512,1024]{1,0:T(8,128)(2,1)}, bf16[256,16,128]{2,1,0:T(8,128)(2,1)}, f32[3,64,512]{2,1,0:T(8,128)}, f32[64,512]{1,0:T(8,128)}, f32[64,2048]...) custom-call(bf16[512,1024]{1,0:T(8,128)(2,1)} %bitcast.29, ...), custom_call_target="tpu_custom_call" | custom-call | tf_op jit(solution)/shard_map/dit_block/pallas_call | solution.py:1580
  263.3 0.0 copy-start.3
  263.3 0.0 copy-start.4
  263.3 0.0 copy-start.2
  263.3 0.0 copy-start.1
  263.3 1.3 slice_bitcast_fusion.1
  264.6 1.3 slice.21
  265.9 1.4 slice_bitcast_fusion
  267.3 1.3 slice.27
  268.6 0.0 copy-start
  268.6 2.8 %reshape.72 = f32[256,16,128]{2,1,0:T(8,128)} convert(bf16[256,16,128]{2,1,0:T(8,128)(2,1)} %get-tuple-element.23) | non-fusion elementwise | flops 524288 | bytes 3145728 | tf_op jit(solution)/shard_map/reshape | solution.py:1599
  271.4 2.3 copy.35
  273.6 0.0 copy-done.3
  273.6 0.7 copy.36
  274.4 0.0 copy-done.4
  274.4 0.7 copy.37
  275.0 0.0 copy-done.2
  275.0 0.8 copy.38
  275.8 0.0 copy-done.1
  275.8 0.8 copy.39
  276.6 0.0 copy-done
  276.6 0.9 copy.40
Async XLA Ops:
  263.3 10.3 %copy-start.3 = (f32[3,64,512]{2,1,0:T(8,128)S(1)}, f32[3,64,512]{2,1,0:T(8,128)}, u32[]{:S(2)}) copy-start(f32[3,64,512]{2,1,0:T(8,128)} %get-tuple-element.25) | copy-start | bytes 1179652
  263.3 11.1 %copy-start.4 = (f32[64,512]{1,0:T(8,128)S(1)}, f32[64,512]{1,0:T(8,128)}, u32[]{:S(2)}) copy-start(f32[64,512]{1,0:T(8,128)} %get-tuple-element.26) | copy-start | bytes 393220
  263.3 11.7 %copy-start.2 = (f32[64,2048]{1,0:T(8,128)S(1)}, f32[64,2048]{1,0:T(8,128)}, u32[]{:S(2)}) copy-start(f32[64,2048]{1,0:T(8,128)} %get-tuple-element.67) | copy-start | bytes 1572868
  263.3 12.5 %copy-start.1 = (f32[64,2048]{1,0:T(8,128)S(1)}, f32[64,2048]{1,0:T(8,128)}, u32[]{:S(2)}) copy-start(f32[64,2048]{1,0:T(8,128)} %get-tuple-element.28) | copy-start | bytes 1572868
  268.6 8.0 %copy-start = (f32[6,64,512]{2,1,0:T(8,128)S(1)}, f32[6,64,512]{2,1,0:T(8,128)}, u32[]{:S(2)}) copy-start(f32[6,64,512]{2,1,0:T(8,128)} %get-tuple-element.29) | copy-start | bytes 2359300
